TPU v7x, 32 devices: a whole 2x2x4 slice. The times are simulated.
32 devices in a mesh: pulse: 2 (over y), grid: 16 (over z, x, core).
Axes of the slice: x: 2, y: 2, z: 4, core: 2. Of those that a mesh axis runs over, the one named last changes fastest.
Arguments:
- orbitals: float32 [16, 32, 32, 256], P('grid'), may hold values from -6 to 6
- potential: float32 [16, 32, 32], P('grid'), may hold values from -2 to 2
- pulse: float32 [2], P('pulse'), parts along dimension 0, may hold values from -3 to 3
- projectors: bfloat16 [256, 8, 256], P('grid'), may hold values from -0.375 to 0.375
- couplings: float32 [256, 8], P('grid'), may hold values from 1 to 8
- sphere_points: int32 [256, 256], P('grid'), may hold values from 0 to 1023
- atom_count: int32 [16], P('grid'), may hold values from 1 to 16, as said below
Outputs:
- propagated: float32 [32, 32, 32, 256], P(('pulse', 'grid')), parts along dimension 0
- dipole: float32 [2], P('pulse'), parts along dimension 0
There are 2 independent parts, one for each index of `pulse`. A program takes and returns all parts, laid end to end along the dimension named above; an argument that names none is the same for every part. Nothing has to cross between parts.
Inputs may be any that keep to these rules, and one draw needn't show every extreme that they name: The first and last slab are full: atom_count of them is 16. Slabs within an eighth of the axis from either end hold three quarters or more of 16 atoms, the others at most a quarter.
All inputs are finite; a program needn't handle non-finite values.
Results may differ from a plain program's by a relative error of at most 0.0003.
Values sent between devices are 32-bit elements; how exact they have to be, the bound alone decides.
No kernel may reach another device: no remote copies, remote signals or barrier semaphores. Data moves between devices by JAX's collectives and lax.ppermute only.
A program may use at most 64 MiB of HBM per device.

v0:
```python
import math

import jax
import jax.numpy as jnp
from jax import lax
from jax.sharding import PartitionSpec as P

TERMS = 4


time_step = 0.1
widest_block = 16


def extended(cells, sides, width):
    for axis, dim in sides:
        count = lax.axis_size(axis)
        ends = count - 1
        head = lax.slice_in_dim(cells, 0, width, axis=dim)
        tail = lax.slice_in_dim(cells, cells.shape[dim] - width, cells.shape[dim], axis=dim)
        cells = jnp.concatenate(
            [
                lax.ppermute(tail, axis, [(i, (i + 1) % count) for i in range(ends)]),
                cells,
                lax.ppermute(head, axis, [((i + 1) % count, i) for i in range(ends)]),
            ],
            axis=dim,
        )
    return cells


def sphere_terms(proj_block, weight_block, samples):
    coeffs = jnp.einsum("akp,apc->akc", proj_block, samples, precision=lax.Precision.HIGHEST)
    scaled = coeffs * weight_block[:, :, None]
    return jnp.einsum("akp,akc->apc", proj_block, scaled, precision=lax.Precision.HIGHEST)


def slot_blocks(flat_in, flat_out, proj_wide, weights, sphere_points, used_atoms):
    block_atoms = math.gcd(widest_block, proj_wide.shape[0])
    block_total = (used_atoms + block_atoms - 1) // block_atoms
    channels = flat_in.shape[1]

    def advance(block, target):
        samples = flat_in[sphere_points]
        contribution = sphere_terms(proj_wide, weights, samples)
        return target.at[sphere_points.reshape(-1)].add(contribution.reshape(-1, channels))

    return lax.fori_loop(0, block_total, advance, flat_out)


def local(orbitals, potential, pulse, projectors, couplings, sphere_points, atom_count):
    planes, rows_x, rows_y, channels = orbitals.shape
    half_orbitals = channels // 2
    slab_total = lax.axis_size("grid")
    total_planes = planes * slab_total
    plane_index = lax.axis_index("grid") * planes + jnp.arange(planes)
    plane_weight = (plane_index.astype(jnp.float32) + 0.5) / total_planes
    applied = pulse[0] * 4.0 * (plane_weight - 0.5)
    field_potential = (potential + applied[:, None, None])[..., None]
    atom_slots = projectors.shape[0]
    own_atoms = atom_count[0]
    slot_index = jnp.arange(atom_slots)
    occupied = (slot_index < own_atoms).astype(jnp.float32)
    weights = couplings * occupied[:, None]
    proj_wide = projectors.astype(jnp.float32)
    series_term = orbitals
    summed = orbitals
    for order in range(1, TERMS + 1):
        padded = extended(series_term, (("grid", 0),), 1)
        laplace = padded[2:] + padded[:-2]
        laplace = laplace + jnp.roll(series_term, 1, 1) + jnp.roll(series_term, -1, 1)
        laplace = (
            laplace + jnp.roll(series_term, 1, 2) + jnp.roll(series_term, -1, 2) - 6.0 * series_term
        )
        local_part = -0.5 * laplace + field_potential * series_term
        flat_in = series_term.reshape(-1, channels)
        flat_out = slot_blocks(
            flat_in, local_part.reshape(-1, channels), proj_wide, weights, sphere_points, own_atoms
        )
        image = flat_out.reshape(series_term.shape)
        factor = time_step / order
        series_term = jnp.concatenate(
            [factor * image[..., half_orbitals:], -factor * image[..., :half_orbitals]], axis=3
        )
        summed = summed + series_term
    local_moment = jnp.sum(plane_weight[:, None, None, None] * summed * summed)
    moment = lax.psum(local_moment, "grid")
    dipole = moment / (total_planes * rows_x * rows_y * half_orbitals)
    return (summed, dipole.reshape(1))


def solution(mesh):
    placed = (
        P("grid", None, None, None),
        P("grid", None, None),
        P("pulse"),
        P("grid", None, None),
        P("grid", None),
        P("grid", None),
        P("grid"),
    )
    return jax.shard_map(
        local,
        mesh=mesh,
        in_specs=placed,
        out_specs=(P(("pulse", "grid"), None, None, None), P("pulse")),
        check_vma=False,
    )
```

profile of v0, /device:TPU:0, one launch (start us, length us, event | category | flops | bytes accessed | tf_op | source)
XLA Modules:
  0.0 278.7 jit_solution(17982675274086059678)
XLA Ops:
  0.6 1.3 collective-permute-start
  1.9 3.1 %collective-permute-start.1 = (f32[1,32,32,256]{3,2,1,0:T(8,128)}, f32[1,32,32,256]{3,2,1,0:T(8,128)S(1)}, u32[]{:S(2)}, u32[]{:S(2)}) collective-permute-start(f32[1,32,32,256]{3,2,1,0:T(8,128)} %param.15), channel_id=1, source_target_pairs={{0,1},{1,2},{2,3},{3,4},{4,5},{5,6},{6,7},{7,8},{8,9},{9,10},{10,1... | collective-permute-start | bytes 3145736 | tf_op jit(solution)/shard_map/ppermute | solution.py:23
  5.0 1.7 fusion.63
  6.7 1.4 fusion.65
  9.5 0.8 copy.9
  10.2 0.7 fusion.61
  11.0 0.7 add_bitcast_fusion
  11.8 0.9 convert_element_type.16
  12.6 17.4 %gather_fusion = f32[4096,256]{1,0:T(8,128)} fusion(f32[1024,256]{1,0:T(8,128)} %bitcast.119, s32[4096]{0:T(1024)S(1)} %broadcast_clamp_fusion), kind=kCustom, calls=%fused_computation | custom fusion | bytes 8404992 | tf_op jit(solution)/shard_map/while/body/gather | solution.py:44
  30.1 0.3 fusion.64
  30.4 0.2 fusion.62
  30.6 1.6 copy-done.13
  32.3 1.5 fusion.66
  33.8 0.9 copy-done.16
  34.8 0.4 copy-done.17
  35.1 2.1 fusion.24
  37.3 28.5 %while.48 = (s32[]{:T(128)}, f32[1024,256]{1,0:T(8,128)S(1)}, s32[]{:T(128)}, s32[16,256]{1,0:T(8,128)S(1)}, f32[16,8]{1,0:T(8,128)S(1)}, /*index=5*/f32[16,256,...) while((s32[]{:T(128)}, f32[1024,256]{1,0:T(8,128)S(1)}, s32[]{:T(128)}, s32[16,256]{1,0:T(8,128)S(1)}, ...), condition=%wide.region_2.3_spmd, body=%wide.region_0.2_spmd.sunk | while | flops 101756928 | bytes 17121876 | solution.py:48
  37.3 5.2 %fusion.96 = f32[16,256,256]{1,2,0:T(8,128)} fusion(f32[16,8,256]{2,1,0:T(8,128)S(1)} %get-tuple-element.654, f32[16,256,8]{1,2,0:T(8,128)S(1)} %get-tuple-element.653, f32[16,8]{1,0:T(8,128)S(1)} %get-tuple-element.652), kind=kOutput, calls=%fused_computation.8.clone.1 | convolution fusion | flops 100696064 | bytes 4456960 | tf_op jit(solution)/shard_map/while/body/akp,akc->apc/dot_general | solution.py:35
  42.5 23.3 %scatter_fusion = f32[1024,256]{1,0:T(8,128)S(1)} fusion(f32[1024,256]{1,0:T(8,128)S(1)} %get-tuple-element.641, s32[4096]{0:T(1024)S(1)} %bitcast.135, f32[4096,256]{1,0:T(8,128)} %bitcast.123), kind=kCustom, calls=%fused_computation.4.clone.1 | custom fusion | flops 1048576 | bytes 12599296 | tf_op jit(solution)/shard_map/while/body/scatter-add | solution.py:46
  66.0 1.3 collective-permute-start.2
  67.3 6.0 %collective-permute-start.3 = (f32[1,32,32,256]{3,2,1,0:T(8,128)S(1)}, f32[1,32,32,256]{3,2,1,0:T(8,128)}, u32[]{:S(2)}, u32[]{:S(2)}) collective-permute-start(f32[1,32,32,256]{3,2,1,0:T(8,128)S(1)} %pad_maximum_fusion), channel_id=1, source_target_pairs={{0,1},{1,2},{2,3},{3,4},{4,5},{5,6},{6,7},{7,8},{8,9},{9,10},{10,1... | collective-permute-start | bytes 3145736 | tf_op jit(solution)/shard_map/ppermute | solution.py:23
  73.4 16.1 %gather_fusion.1 = f32[4096,256]{1,0:T(8,128)} fusion(f32[1024,256]{1,0:T(8,128)S(1)} %bitcast.120, s32[4096]{0:T(1024)S(1)} %broadcast_clamp_fusion), kind=kCustom, calls=%fused_computation.1 | custom fusion | bytes 8404992 | tf_op jit(solution)/shard_map/while/body/gather | solution.py:44
  89.9 1.8 copy-done.11
  91.7 1.5 fusion.67
  93.2 2.1 fusion.30
  95.3 28.7 %while.49 = (s32[]{:T(128)}, f32[1024,256]{1,0:T(8,128)S(1)}, s32[]{:T(128)}, s32[16,256]{1,0:T(8,128)S(1)}, f32[16,8]{1,0:T(8,128)S(1)}, /*index=5*/f32[16,256,...) while((s32[]{:T(128)}, f32[1024,256]{1,0:T(8,128)S(1)}, s32[]{:T(128)}, s32[16,256]{1,0:T(8,128)S(1)}, ...), condition=%wide.region_5.6_spmd, body=%wide.region_3.5_spmd.sunk | while | flops 101756928 | bytes 17121876 | solution.py:48
  95.5 5.2 %fusion.99 = f32[16,256,256]{1,2,0:T(8,128)} fusion(f32[16,8,256]{2,1,0:T(8,128)S(1)} %get-tuple-element.678, f32[16,256,8]{1,2,0:T(8,128)S(1)} %get-tuple-element.677, f32[16,8]{1,0:T(8,128)S(1)} %get-tuple-element.676), kind=kOutput, calls=%fused_computation.12.clone.1 | convolution fusion | flops 100696064 | bytes 4456960 | tf_op jit(solution)/shard_map/while/body/akp,akc->apc/dot_general | solution.py:35
  100.7 23.3 %scatter_fusion.1 = f32[1024,256]{1,0:T(8,128)S(1)} fusion(f32[1024,256]{1,0:T(8,128)S(1)} %get-tuple-element.665, s32[4096]{0:T(1024)S(1)} %bitcast.136, f32[4096,256]{1,0:T(8,128)} %bitcast.124), kind=kCustom, calls=%fused_computation.5.clone.1 | custom fusion | flops 1048576 | bytes 12599296 | tf_op jit(solution)/shard_map/while/body/scatter-add | solution.py:46
  124.3 1.3 collective-permute-start.4
  125.6 7.3 %collective-permute-start.5 = (f32[1,32,32,256]{3,2,1,0:T(8,128)S(1)}, f32[1,32,32,256]{3,2,1,0:T(8,128)}, u32[]{:S(2)}, u32[]{:S(2)}) collective-permute-start(f32[1,32,32,256]{3,2,1,0:T(8,128)S(1)} %pad_maximum_fusion.1), channel_id=1, source_target_pairs={{0,1},{1,2},{2,3},{3,4},{4,5},{5,6},{6,7},{7,8},{8,9},{9,10},{10,1... | collective-permute-start | bytes 3145736 | tf_op jit(solution)/shard_map/ppermute | solution.py:23
  132.8 16.1 %gather_fusion.2 = f32[4096,256]{1,0:T(8,128)} fusion(f32[1024,256]{1,0:T(8,128)S(1)} %bitcast.121, s32[4096]{0:T(1024)S(1)} %broadcast_clamp_fusion), kind=kCustom, calls=%fused_computation.2 | custom fusion | bytes 8404992 | tf_op jit(solution)/shard_map/while/body/gather | solution.py:44
  149.3 1.8 copy-done.12
  151.1 1.5 fusion.68
  152.7 2.1 fusion.36
  154.8 28.5 %while.50 = (s32[]{:T(128)}, f32[1024,256]{1,0:T(8,128)S(1)}, s32[]{:T(128)}, s32[16,256]{1,0:T(8,128)S(1)}, f32[16,8]{1,0:T(8,128)S(1)}, /*index=5*/f32[16,256,...) while((s32[]{:T(128)}, f32[1024,256]{1,0:T(8,128)S(1)}, s32[]{:T(128)}, s32[16,256]{1,0:T(8,128)S(1)}, ...), condition=%wide.region_8.9_spmd, body=%wide.region_6.8_spmd.sunk | while | flops 101756928 | bytes 17121876 | solution.py:48
  154.8 5.2 %fusion.102 = f32[16,256,256]{1,2,0:T(8,128)} fusion(f32[16,8,256]{2,1,0:T(8,128)S(1)} %get-tuple-element.702, f32[16,256,8]{1,2,0:T(8,128)S(1)} %get-tuple-element.701, f32[16,8]{1,0:T(8,128)S(1)} %get-tuple-element.700), kind=kOutput, calls=%fused_computation.16.clone.1 | convolution fusion | flops 100696064 | bytes 4456960 | tf_op jit(solution)/shard_map/while/body/akp,akc->apc/dot_general | solution.py:35
  160.0 23.3 %scatter_fusion.2 = f32[1024,256]{1,0:T(8,128)S(1)} fusion(f32[1024,256]{1,0:T(8,128)S(1)} %get-tuple-element.689, s32[4096]{0:T(1024)S(1)} %bitcast.137, f32[4096,256]{1,0:T(8,128)} %bitcast.125), kind=kCustom, calls=%fused_computation.6.clone.1 | custom fusion | flops 1048576 | bytes 12599296 | tf_op jit(solution)/shard_map/while/body/scatter-add | solution.py:46
  183.5 1.3 collective-permute-start.6
  184.8 5.2 %collective-permute-start.7 = (f32[1,32,32,256]{3,2,1,0:T(8,128)S(1)}, f32[1,32,32,256]{3,2,1,0:T(8,128)}, u32[]{:S(2)}, u32[]{:S(2)}) collective-permute-start(f32[1,32,32,256]{3,2,1,0:T(8,128)S(1)} %pad_maximum_fusion.2), channel_id=1, source_target_pairs={{0,1},{1,2},{2,3},{3,4},{4,5},{5,6},{6,7},{7,8},{8,9},{9,10},{10,1... | collective-permute-start | bytes 3145736 | tf_op jit(solution)/shard_map/ppermute | solution.py:23
  190.0 16.1 %gather_fusion.3 = f32[4096,256]{1,0:T(8,128)} fusion(f32[1024,256]{1,0:T(8,128)S(1)} %bitcast.122, s32[4096]{0:T(1024)S(1)} %broadcast_clamp_fusion), kind=kCustom, calls=%fused_computation.3 | custom fusion | bytes 8404992 | tf_op jit(solution)/shard_map/while/body/gather | solution.py:44
  206.5 1.8 copy-done.10
  208.3 1.5 fusion.69
  209.9 2.1 fusion.42
  212.0 28.5 %while.51 = (s32[]{:T(128)}, f32[1024,256]{1,0:T(8,128)S(1)}, s32[]{:T(128)}, s32[16,256]{1,0:T(8,128)S(1)}, f32[16,8]{1,0:T(8,128)S(1)}, /*index=5*/f32[16,256,...) while((s32[]{:T(128)}, f32[1024,256]{1,0:T(8,128)S(1)}, s32[]{:T(128)}, s32[16,256]{1,0:T(8,128)S(1)}, ...), condition=%wide.region_11.12_spmd, body=%wide.region_9.11_spmd.sunk | while | flops 101756928 | bytes 17121876 | solution.py:48
  212.0 5.2 %fusion.105 = f32[16,256,256]{1,2,0:T(8,128)} fusion(f32[16,8,256]{2,1,0:T(8,128)S(1)} %get-tuple-element.726, f32[16,256,8]{1,2,0:T(8,128)S(1)} %get-tuple-element.725, f32[16,8]{1,0:T(8,128)S(1)} %get-tuple-element.724), kind=kOutput, calls=%fused_computation.20.clone.1 | convolution fusion | flops 100696064 | bytes 4456960 | tf_op jit(solution)/shard_map/while/body/akp,akc->apc/dot_general | solution.py:35
  217.2 23.3 %scatter_fusion.3 = f32[1024,256]{1,0:T(8,128)S(1)} fusion(f32[1024,256]{1,0:T(8,128)S(1)} %get-tuple-element.713, s32[4096]{0:T(1024)S(1)} %bitcast.138, f32[4096,256]{1,0:T(8,128)} %bitcast.126), kind=kCustom, calls=%fused_computation.7.clone.1 | custom fusion | flops 1048576 | bytes 12599296 | tf_op jit(solution)/shard_map/while/body/scatter-add | solution.py:46
  240.7 3.4 %fusion.12 = (f32[]{:T(128)}, f32[1,32,32,256]{3,2,1,0:T(8,128)}) fusion(f32[]{:T(128)S(6)} %div.17, f32[1,32,32,128]{3,2,1,0:T(8,128)S(1)} %get-tuple-element.417, f32[1,32,32,128]{3,2,1,0:T(8,128)S(1)} %get-tuple-element.416, f32[1,32,32,128]{3,2,1,0:T(8,128)} %copy-done.8, f32[1,32,32,128]{3,2,1,0:T(8,128)} %copy-done.9, f32[1,32,32,128]{3,2,1,0:T(8,128)} %copy-done.6, ...), kind=kLoop, calls=%fused_computation.76 | loop fusion | flops 2883583 | bytes 6291464 | tf_op jit(solution)/shard_map/reduce_sum | solution.py:86
  244.1 32.8 %psum.7 = f32[]{:T(128)} all-reduce(f32[]{:T(128)} %get-tuple-element.414), channel_id=1, replica_groups=mesh['pulse'=2,'grid'=16] {'grid'}, use_global_device_ids=true, to_apply=%region_13.14 | all-reduce | flops 1 | bytes 8 | tf_op jit(solution)/shard_map/psum | solution.py:87
  (75 shorter events, 2.3 us)
Async XLA Ops:
  0.6 33.2 %collective-permute-start = (f32[1,32,32,256]{3,2,1,0:T(8,128)}, f32[1,32,32,256]{3,2,1,0:T(8,128)S(1)}, u32[]{:S(2)}, u32[]{:S(2)}) collective-permute-start(f32[1,32,32,256]{3,2,1,0:T(8,128)} %param.15), channel_id=1, source_target_pairs={{1,0},{2,1},{3,2},{4,3},{5,4},{6,5},{7,6},{8,7},{9,8},{10,9},{11,1... | collective-permute-start | bytes 3145736 | tf_op jit(solution)/shard_map/ppermute | solution.py:25
  1.9 31.9 %collective-permute-start.1 = (f32[1,32,32,256]{3,2,1,0:T(8,128)}, f32[1,32,32,256]{3,2,1,0:T(8,128)S(1)}, u32[]{:S(2)}, u32[]{:S(2)}) collective-permute-start(f32[1,32,32,256]{3,2,1,0:T(8,128)} %param.15), channel_id=1, source_target_pairs={{0,1},{1,2},{2,3},{3,4},{4,5},{5,6},{6,7},{7,8},{8,9},{9,10},{10,1... | collective-permute-start | bytes 3145736 | tf_op jit(solution)/shard_map/ppermute | solution.py:23
  12.6 17.4 %copy-start = (f32[1,32,32,256]{3,2,1,0:T(8,128)S(1)}, f32[1,32,32,256]{3,2,1,0:T(8,128)}, u32[]{:S(2)}) copy-start(f32[1,32,32,256]{3,2,1,0:T(8,128)} %param.15) | copy-start | bytes 3145732
  30.1 2.2 copy-start.13
  30.1 2.2 copy-start.15
  30.4 4.8 %copy-start.18 = (f32[1,32,1,256]{3,2,1,0:T(1,128)S(1)}, f32[1,32,1,256]{3,2,1,0:T(1,128)}, u32[]{:S(2)}) copy-start(f32[1,32,1,256]{3,2,1,0:T(1,128)} %get-tuple-element.451) | copy-start | bytes 98308
  30.4 4.7 %copy-start.19 = (f32[1,1,32,256]{3,2,1,0:T(8,128)S(1)}, f32[1,1,32,256]{3,2,1,0:T(8,128)}, u32[]{:S(2)}) copy-start(f32[1,1,32,256]{3,2,1,0:T(8,128)} %get-tuple-element.454) | copy-start | bytes 98308
  30.4 4.7 %copy-start.20 = (f32[1,1,32,256]{3,2,1,0:T(8,128)S(1)}, f32[1,1,32,256]{3,2,1,0:T(8,128)}, u32[]{:S(2)}) copy-start(f32[1,1,32,256]{3,2,1,0:T(8,128)} %get-tuple-element.455) | copy-start | bytes 98308
  33.8 1.0 copy-start.16
  33.8 1.3 copy-start.17
  35.1 2.1 copy-start.14
  65.9 27.3 %copy-start.2 = (f32[1,32,32,128]{3,2,1,0:T(8,128)}, f32[1,32,32,128]{3,2,1,0:T(8,128)S(1)}, u32[]{:S(2)}) copy-start(f32[1,32,32,128]{3,2,1,0:T(8,128)S(1)} %get-tuple-element.446) | copy-start | bytes 1572868
  65.9 27.3 %copy-start.4 = (f32[1,32,32,128]{3,2,1,0:T(8,128)}, f32[1,32,32,128]{3,2,1,0:T(8,128)S(1)}, u32[]{:S(2)}) copy-start(f32[1,32,32,128]{3,2,1,0:T(8,128)S(1)} %get-tuple-element.447) | copy-start | bytes 1572868
  66.0 27.2 %collective-permute-start.2 = (f32[1,32,32,256]{3,2,1,0:T(8,128)S(1)}, f32[1,32,32,256]{3,2,1,0:T(8,128)}, u32[]{:S(2)}, u32[]{:S(2)}) collective-permute-start(f32[1,32,32,256]{3,2,1,0:T(8,128)S(1)} %pad_maximum_fusion), channel_id=1, source_target_pairs={{1,0},{2,1},{3,2},{4,3},{5,4},{6,5},{7,6},{8,7},{9,8},{10,9},{11,1... | collective-permute-start | bytes 3145736 | tf_op jit(solution)/shard_map/ppermute | solution.py:25
  67.3 25.9 %collective-permute-start.3 = (f32[1,32,32,256]{3,2,1,0:T(8,128)S(1)}, f32[1,32,32,256]{3,2,1,0:T(8,128)}, u32[]{:S(2)}, u32[]{:S(2)}) collective-permute-start(f32[1,32,32,256]{3,2,1,0:T(8,128)S(1)} %pad_maximum_fusion), channel_id=1, source_target_pairs={{0,1},{1,2},{2,3},{3,4},{4,5},{5,6},{6,7},{7,8},{8,9},{9,10},{10,1... | collective-permute-start | bytes 3145736 | tf_op jit(solution)/shard_map/ppermute | solution.py:23
  89.5 2.2 copy-start.11
  124.2 28.5 %copy-start.6 = (f32[1,32,32,128]{3,2,1,0:T(8,128)}, f32[1,32,32,128]{3,2,1,0:T(8,128)S(1)}, u32[]{:S(2)}) copy-start(f32[1,32,32,128]{3,2,1,0:T(8,128)S(1)} %get-tuple-element.436) | copy-start | bytes 1572868
  124.2 28.5 %copy-start.7 = (f32[1,32,32,128]{3,2,1,0:T(8,128)}, f32[1,32,32,128]{3,2,1,0:T(8,128)S(1)}, u32[]{:S(2)}) copy-start(f32[1,32,32,128]{3,2,1,0:T(8,128)S(1)} %get-tuple-element.437) | copy-start | bytes 1572868
  124.3 28.4 %collective-permute-start.4 = (f32[1,32,32,256]{3,2,1,0:T(8,128)S(1)}, f32[1,32,32,256]{3,2,1,0:T(8,128)}, u32[]{:S(2)}, u32[]{:S(2)}) collective-permute-start(f32[1,32,32,256]{3,2,1,0:T(8,128)S(1)} %pad_maximum_fusion.1), channel_id=1, source_target_pairs={{1,0},{2,1},{3,2},{4,3},{5,4},{6,5},{7,6},{8,7},{9,8},{10,9},{11,1... | collective-permute-start | bytes 3145736 | tf_op jit(solution)/shard_map/ppermute | solution.py:25
  125.6 27.1 %collective-permute-start.5 = (f32[1,32,32,256]{3,2,1,0:T(8,128)S(1)}, f32[1,32,32,256]{3,2,1,0:T(8,128)}, u32[]{:S(2)}, u32[]{:S(2)}) collective-permute-start(f32[1,32,32,256]{3,2,1,0:T(8,128)S(1)} %pad_maximum_fusion.1), channel_id=1, source_target_pairs={{0,1},{1,2},{2,3},{3,4},{4,5},{5,6},{6,7},{7,8},{8,9},{9,10},{10,1... | collective-permute-start | bytes 3145736 | tf_op jit(solution)/shard_map/ppermute | solution.py:23
  148.9 2.2 copy-start.12
  183.4 26.4 %copy-start.8 = (f32[1,32,32,128]{3,2,1,0:T(8,128)}, f32[1,32,32,128]{3,2,1,0:T(8,128)S(1)}, u32[]{:S(2)}) copy-start(f32[1,32,32,128]{3,2,1,0:T(8,128)S(1)} %get-tuple-element.426) | copy-start | bytes 1572868
  183.4 26.4 %copy-start.9 = (f32[1,32,32,128]{3,2,1,0:T(8,128)}, f32[1,32,32,128]{3,2,1,0:T(8,128)S(1)}, u32[]{:S(2)}) copy-start(f32[1,32,32,128]{3,2,1,0:T(8,128)S(1)} %get-tuple-element.427) | copy-start | bytes 1572868
  183.5 26.3 %collective-permute-start.6 = (f32[1,32,32,256]{3,2,1,0:T(8,128)S(1)}, f32[1,32,32,256]{3,2,1,0:T(8,128)}, u32[]{:S(2)}, u32[]{:S(2)}) collective-permute-start(f32[1,32,32,256]{3,2,1,0:T(8,128)S(1)} %pad_maximum_fusion.2), channel_id=1, source_target_pairs={{1,0},{2,1},{3,2},{4,3},{5,4},{6,5},{7,6},{8,7},{9,8},{10,9},{11,1... | collective-permute-start | bytes 3145736 | tf_op jit(solution)/shard_map/ppermute | solution.py:25
  184.8 25.0 %collective-permute-start.7 = (f32[1,32,32,256]{3,2,1,0:T(8,128)S(1)}, f32[1,32,32,256]{3,2,1,0:T(8,128)}, u32[]{:S(2)}, u32[]{:S(2)}) collective-permute-start(f32[1,32,32,256]{3,2,1,0:T(8,128)S(1)} %pad_maximum_fusion.2), channel_id=1, source_target_pairs={{0,1},{1,2},{2,3},{3,4},{4,5},{5,6},{6,7},{7,8},{8,9},{9,10},{10,1... | collective-permute-start | bytes 3145736 | tf_op jit(solution)/shard_map/ppermute | solution.py:23
  206.1 2.2 copy-start.10
  212.0 28.7 %copy-start.1 = (f32[1,32,32,256]{3,2,1,0:T(8,128)S(1)}, f32[1,32,32,256]{3,2,1,0:T(8,128)}, u32[]{:S(2)}) copy-start(f32[1,32,32,256]{3,2,1,0:T(8,128)} %param.15) | copy-start | bytes 3145732
  212.0 28.7 %copy-start.3 = (f32[1,32,32,128]{3,2,1,0:T(8,128)S(1)}, f32[1,32,32,128]{3,2,1,0:T(8,128)}, u32[]{:S(2)}) copy-start(f32[1,32,32,128]{3,2,1,0:T(8,128)} %copy-done.2) | copy-start | bytes 1572868
  212.0 28.7 %copy-start.5 = (f32[1,32,32,128]{3,2,1,0:T(8,128)S(1)}, f32[1,32,32,128]{3,2,1,0:T(8,128)}, u32[]{:S(2)}) copy-start(f32[1,32,32,128]{3,2,1,0:T(8,128)} %copy-done.4) | copy-start | bytes 1572868
where the time goes:
time: 280 us; the launch traced here: 279 us
  other arithmetic  109 us (39%)
  local copies, waits for them, and re-layouts  78.6 us (28%)
  blocking collectives  32.8 us (12%)
  starting transfers between devices  26.8 us (10%)
  matrix products  26.8 us (10%)
  between operations  4.23 us (2%)
    scatter-add x4, other arithmetic, advance(): target.at[sphere_points.reshape(-1)].add(contribution.reshape(-1, channels))  93 us
    gather x4, local copies, waits for them, and re-layouts, advance(): samples = flat_in[sphere_points]  65.8 us
    psum x1, blocking collectives, local(): moment = lax.psum(local_moment, 'grid')  32.8 us
    ppermute x4, starting transfers between devices, extended(): lax.ppermute(tail, axis, [(i, (i + 1) % count) for i in range(ends)])  21.6 us
    dot_general x4, matrix products, sphere_terms(): jnp.einsum('akp,akc->apc', proj_block, scaled, precision=lax.Precision.HI...  20.7 us
    unnamed x44, local copies, waits for them, and re-layouts  9.13 us
    add x4, other arithmetic, local(): local_part = -0.5 * laplace + field_potential * series_term  8.38 us
    dot_general x4, matrix products, sphere_terms(): jnp.einsum('akp,apc->akc', proj_block, samples, precision=lax.Precision.H...  6.09 us
  transfers between devices with their start and end apart: 8, of which 0 were waited for; matrix products, arithmetic and copies ran while one was open for 29% of the time, Pallas kernels for 0%

commit v1 on v0

v1 whole, which is shorter than its diff:
```python
import functools

import jax
import jax.numpy as jnp
from jax import lax
from jax.experimental import pallas as pl
from jax.experimental.pallas import tpu as pltpu
from jax.sharding import PartitionSpec as P


TERMS = 4
TIME_STEP = 0.1
GROUP = 4
HALO = TERMS
SLOTS = GROUP + 2 * HALO
LIGHT = 4
F32 = jnp.float32
BF16 = jnp.bfloat16
NT = (((1,), (1,)), ((), ()))
NN = (((1,), (0,)), ((), ()))


def iota(shape, dim):
    return lax.broadcasted_iota(jnp.int32, shape, dim)


def split(value):
    high = value.astype(BF16)
    return high, (value - high.astype(F32)).astype(BF16)


def place():
    y, g = lax.axis_index("pulse"), lax.axis_index("grid")
    return y, g // GROUP, (g // 2) % 2, g % 2


def pack_kernel(orb, pot, proj, coup, points, count, near, far, heavy, packed, rows):
    y, _, x, _ = place()
    cells, channels = orb.shape
    lanes = cells // 8
    half = channels // 2
    first = iota((lanes, half), 1) < half // 2
    for j in range(8):
        chunk = slice(j * lanes, (j + 1) * lanes)
        re, im = orb[chunk, :half], orb[chunk, half:]
        low = jnp.where(first, re, pltpu.roll(im, half // 2, 1))
        high = jnp.where(first, pltpu.roll(re, half // 2, 1), im)
        packed[chunk, :] = jnp.where(y == 0, low, high)
    for j in range(8):
        rows[:, j * lanes : (j + 1) * lanes] = packed[pl.ds(j, lanes, stride=8), :].T
    part = half // 8
    for out, xx in ((near, x), (far, 1 - x)):
        for c in range(2):
            start = pl.multiple_of((2 * xx + c) * part, part)
            out[c * 2 * part : c * 2 * part + part, :] = rows[pl.ds(start, part), :]
            out[c * 2 * part + part : (c + 1) * 2 * part, :] = rows[pl.ds(start + half // 2, part), :]
    nx, ny = pot.shape
    yh = ny // 8
    col = iota((ny, cells), 1)
    pick = (iota((ny, cells), 0) == (col % lanes) % yh * 8 + col // lanes).astype(F32)
    spread = lax.dot_general(pot[...], pick, NN, precision=lax.Precision.HIGHEST, preferred_element_type=F32)
    keep = iota((nx, cells), 0) == (iota((nx, cells), 1) % lanes) // yh
    pot_row = jnp.sum(jnp.where(keep, spread, 0.0), axis=0, keepdims=True)
    atoms, k = coup.shape
    pick = (iota((k, atoms * k), 0) == iota((k, atoms * k), 1) % k).astype(F32)
    spread = lax.dot_general(coup[...], pick, NN, precision=lax.Precision.HIGHEST, preferred_element_type=F32)
    atom = iota((atoms, atoms * k), 0)
    keep = (atom == iota((atoms, atoms * k), 1) // k) & (atom < count[0])
    weight_row = jnp.sum(jnp.where(keep, spread, 0.0), axis=0, keepdims=True)
    size = points.shape[1]
    base = 4 * part
    for out in (near, far):
        for a in range(LIGHT):
            out[base : base + k, a * size : (a + 1) * size] = proj[a].astype(F32)
            out[base + k : base + k + 1, a * size : (a + 1) * size] = points[a : a + 1, :].astype(F32)
        out[base + k + 1 : base + k + 2, :] = pot_row
        out[base + k + 2 : base + k + 3, :] = jnp.zeros((1, cells), F32)
        out[base + k + 2 : base + k + 3, : atoms * k] = weight_row
        out[base + k + 3 : base + k + 8, :] = jnp.zeros((5, cells), F32)
    groups = atoms // LIGHT - 1
    for group in range(groups):
        for a in range(LIGHT):
            source = (group + 1) * LIGHT + a
            heavy[group * k : (group + 1) * k, a * size : (a + 1) * size] = proj[source].astype(F32)
            heavy[groups * k + group : groups * k + group + 1, a * size : (a + 1) * size] = (
                points[source : source + 1, :].astype(F32)
            )
    heavy[groups * (k + 1) :, :] = jnp.zeros((heavy.shape[0] - groups * (k + 1), cells), F32)


def matrix_of(proj, points, size):
    k = proj.shape[0]
    parts = []
    for a in range(LIGHT):
        values = proj[:, a * size : (a + 1) * size]
        cell = points[:, a * size : (a + 1) * size].astype(jnp.int32)
        low, lane = cell & 7, cell >> 3
        tall = jnp.concatenate([jnp.where(low == j, values, 0.0) for j in range(8)], axis=0).astype(BF16)
        hot = jnp.where(iota((128, size), 0) == lane, 1.0, 0.0).astype(BF16)
        sums = lax.dot_general(tall, hot, NT, preferred_element_type=F32)
        parts.append(jnp.concatenate([sums[j * k : (j + 1) * k, :] for j in range(8)], axis=1))
    return jnp.concatenate(parts, axis=0)


def roll_lanes(value, shift):
    return pltpu.roll(value, shift % value.shape[1], 1)


def evolve_kernel(slabs, shared_heavy, *refs):
    own_pulse, other_pulse = refs[:2]
    bundles = refs[2:14]
    heavies = refs[14:16] if not shared_heavy else refs[14:15]
    refs = refs[14 + len(heavies) :]
    outs, moment = refs[:4], refs[4]
    start, ping, pong, start_split, term_split, total, light, full, pots, weights, nonlocal_part = refs[5:]
    y, quad, x, c = place()
    quads = slabs // GROUP
    part = start.shape[1] // 2
    cells = start.shape[2]
    k = 8
    size = cells // LIGHT
    base = 4 * part
    span = LIGHT * k
    edge = max(slabs // 8, 1)
    has_low, has_high = quad > 0, quad < quads - 1

    for number, bundle in enumerate(bundles):
        direction, xf, cf = number // 4, number // 2 % 2, number % 2
        slot = direction * GROUP + 2 * (x if xf == 0 else 1 - x) + (c if cf == 0 else 1 - c)
        rows = bundle[pl.ds(pl.multiple_of(c * 2 * part, 2 * part), 2 * part), :]
        start[slot] = rows
        high, low = split(rows)
        start_split[slot, : 2 * part] = high
        start_split[slot, 2 * part :] = low
        pots[slot] = bundle[base + k + 1 : base + k + 2, :]
        weights[slot] = bundle[base + k + 2 : base + k + 3, : 4 * span]

        def build(bundle=bundle, slot=slot):
            matrix = matrix_of(bundle[base : base + k, :], bundle[base + k : base + k + 1, :], size)
            high, low = split(matrix)
            light[slot, :span] = high
            light[slot, span : 2 * span] = low
            light[slot, 2 * span :] = high

        if direction == 1:
            build()
        else:
            pl.when((has_low if direction == 0 else has_high) & (slot > 0) & (slot < SLOTS - 1))(build)

    def plane_of(slot):
        return quad * GROUP + slot - HALO

    def is_heavy(slot):
        plane = plane_of(slot)
        return (plane < edge) | (plane >= slabs - edge)

    def build_full(store, source, slot):
        wide = 4 * span
        full[store, 0:span] = light[slot, :span]
        full[store, wide : wide + span] = light[slot, span : 2 * span]
        full[store, 2 * wide : 2 * wide + span] = light[slot, :span]
        for group in range(3):
            high, low = split(
                matrix_of(source(group * k, k), source(3 * k + group, 1), size)
            )
            at = (group + 1) * span
            full[store, at : at + span] = high
            full[store, wide + at : wide + at + span] = low
            full[store, 2 * wide + at : 2 * wide + at + span] = high

    if shared_heavy:

        def store_of(slot):
            return slot - 1

        for slot in range(1, SLOTS - 1):
            exists = (plane_of(slot) >= 0) & (plane_of(slot) < slabs)

            @pl.when(exists & is_heavy(slot))
            def _(slot=slot):
                build_full(slot - 1, lambda at, n: heavies[0][slot - 1, at : at + n, :], slot)
    else:
        ends = (quad == 0) | (quad == quads - 1)
        beside = (quad == 1) | (quad == quads - 2)
        low_end = quad <= 1
        first_slot = jnp.where(ends, jnp.where(low_end, HALO, HALO + 2), jnp.where(low_end, 1, SLOTS - 2))

        def store_of(slot):
            return jnp.where(ends, slot - first_slot, 0)

        @pl.when(ends)
        def _():
            for cf in range(2):
                core = c if cf == 0 else 1 - c
                build_full(core, lambda at, n, cf=cf: heavies[cf][at : at + n, :], first_slot + core)

        @pl.when(beside)
        def _():
            mine = (c == 1) == low_end

            def source(at, n):
                return jnp.where(mine, heavies[0][at : at + n, :], heavies[1][at : at + n, :])

            build_full(0, source, first_slot)

    @pl.when(jnp.logical_not(has_low))
    def _():
        ping[HALO - 1] = jnp.zeros(ping.shape[1:], F32)
        pong[HALO - 1] = jnp.zeros(pong.shape[1:], F32)

    @pl.when(jnp.logical_not(has_high))
    def _():
        ping[HALO + GROUP] = jnp.zeros(ping.shape[1:], F32)
        pong[HALO + GROUP] = jnp.zeros(pong.shape[1:], F32)

    def project(halves, slot, count):
        def run(matrix, width):
            r = lax.dot_general(halves, matrix(0, 2 * width), NT, preferred_element_type=F32)
            coeffs = r[:count, :width] + r[count:, :width] + r[:count, width:]
            scaled = coeffs * weights[slot][:, :width]
            high, low = split(scaled)
            wide = jnp.concatenate([high, high, low], axis=1)
            nonlocal_part[:count] = lax.dot_general(wide, matrix(0, 3 * width), NN, preferred_element_type=F32)

        heavy = is_heavy(slot)

        @pl.when(heavy)
        def _():
            store = store_of(slot)
            run(lambda a, n: full[store, a : a + n, :], 4 * span)

        @pl.when(jnp.logical_not(heavy))
        def _():
            run(lambda a, n: light[slot, a : a + n, :], span)

    lane = iota((1, 128), 1)
    groups_y = 4
    wrap_up, wrap_down = lane % groups_y == groups_y - 1, lane % groups_y == 0

    def hamiltonian(field, slot, j, shift):
        cols = slice(j * 128, (j + 1) * 128)
        v = field[slot, :, cols]
        around = field[slot - 1, :, cols] + field[slot + 1, :, cols]
        around += roll_lanes(v, groups_y) + roll_lanes(v, -groups_y)
        if j < 7:
            around += field[slot, :, (j + 1) * 128 : (j + 2) * 128]
        else:
            w = field[slot, :, :128]
            around += jnp.where(wrap_up, roll_lanes(w, groups_y - 1), roll_lanes(w, -1))
        if j > 0:
            around += field[slot, :, (j - 1) * 128 : j * 128]
        else:
            w = field[slot, :, 7 * 128 :]
            around += jnp.where(wrap_down, roll_lanes(w, 1 - groups_y), roll_lanes(w, 1))
        return (pots[slot][:, cols] + shift) * v - 0.5 * around + nonlocal_part[: v.shape[0], cols], v

    def pulse_field(slot, p):
        strength = jnp.where(y == p, own_pulse[0], other_pulse[0])
        position = (plane_of(slot).astype(F32) + 0.5) / slabs
        return strength * 4.0 * (position - 0.5)

    def put(target, slot, rows, cols, value):
        target[slot, rows, cols] = value
        high, low = split(value)
        term_split[slot, rows, cols] = high
        term_split[slot, slice(4 * part + rows.start, 4 * part + rows.stop), cols] = low

    def bounds(order):
        reach = TERMS - order
        low = jnp.where(has_low, HALO - reach, HALO)
        high = jnp.where(has_high, HALO + GROUP + reach, HALO + GROUP)
        return low, high

    def first(slot, carry):
        project(start_split[slot], slot, 2 * part)
        fields = [pulse_field(slot, p) for p in range(2)]
        own = (slot >= HALO) & (slot < HALO + GROUP)
        for j in range(8):
            cols = slice(j * 128, (j + 1) * 128)
            h, v = hamiltonian(start, slot, j, 3.0)
            for p in range(2):
                image = h + fields[p] * v
                put(ping, slot, slice(p * part, (p + 1) * part), cols, TIME_STEP * image[part:])
                put(ping, slot, slice((2 + p) * part, (3 + p) * part), cols, -TIME_STEP * image[:part])

        @pl.when(own)
        def _():
            for p in range(2):
                for ri in range(2):
                    rows = slice((2 * ri + p) * part, (2 * ri + p + 1) * part)
                    total[slot - HALO, rows] = start[slot, ri * part : (ri + 1) * part] + ping[slot, rows]

        return carry

    lax.fori_loop(*bounds(1), first, 0)

    def later(order, source, target):
        factor = TIME_STEP / order

        def run(slot, carry):
            project(term_split[slot], slot, 4 * part)
            fields = [pulse_field(slot, p) for p in range(2)]
            pulse_of_row = iota((4 * part, 1), 0) // part % 2
            shift = jnp.where(pulse_of_row == 0, 3.0 + fields[0], 3.0 + fields[1])
            own = (slot >= HALO) & (slot < HALO + GROUP)
            index = jnp.clip(slot - HALO, 0, GROUP - 1)
            for j in range(8):
                cols = slice(j * 128, (j + 1) * 128)
                image, _ = hamiltonian(source, slot, j, shift)
                re, im = factor * image[2 * part :], -factor * image[: 2 * part]
                if order < TERMS:
                    put(target, slot, slice(0, 2 * part), cols, re)
                    put(target, slot, slice(2 * part, 4 * part), cols, im)

                    @pl.when(own)
                    def _(re=re, im=im, cols=cols):
                        total[index, : 2 * part, cols] += re
                        total[index, 2 * part :, cols] += im
                else:
                    total[index, : 2 * part, cols] += re
                    total[index, 2 * part :, cols] += im
            return carry

        lax.fori_loop(*bounds(order), run, 0)

    later(2, ping, pong)
    later(3, pong, ping)
    later(4, ping, pong)

    for p in range(2):
        value = jnp.zeros((part, 128), F32)
        for slot in range(GROUP):
            position = (plane_of(slot + HALO).astype(F32) + 0.5) / slabs
            squares = jnp.zeros((part, 128), F32)
            for ri in range(2):
                for j in range(8):
                    v = total[slot, (2 * ri + p) * part : (2 * ri + p + 1) * part, j * 128 : (j + 1) * 128]
                    squares += v * v
            value += position * squares
        moment[p : p + 1, :] = jnp.full((1, 128), jnp.sum(value), F32)
    for number, out in enumerate(outs):
        yy = y if number // 2 == 0 else 1 - y
        xx = x if number % 2 == 0 else 1 - x
        for core in range(2):
            for ri in range(2):
                start_row = pl.multiple_of((2 * ri + yy) * part, part)
                at = (2 * core + ri) * part
                out[at : at + part, :] = total[2 * xx + core, pl.ds(start_row, part), :]


def unpack_kernel(*refs):
    pieces, out, rows, halves = refs[:8], refs[8], refs[9], refs[10:]
    y, _, x, c = place()
    cells, channels = out.shape
    half = channels // 2
    part = half // 8
    for number, piece in enumerate(pieces):
        yy = y if number // 4 == 0 else 1 - y
        xx = x if number // 2 % 2 == 0 else 1 - x
        cc = c if number % 2 == 0 else 1 - c
        at = pl.multiple_of((4 * yy + 2 * xx + cc) * part, part)
        for ri in range(2):
            start = pl.multiple_of((2 * c + ri) * part, part)
            rows[pl.ds(at + ri * half, part), :] = piece[pl.ds(start, part), :]
    lanes = cells // 8
    for j in range(8):
        for ri in range(2):
            block = rows[ri * half : (ri + 1) * half, j * lanes : (j + 1) * lanes].T
            halves[ri][pl.ds(j, lanes, stride=8), :] = block
    for ri in range(2):
        out[:, ri * half : (ri + 1) * half] = halves[ri][...]


VMEM = pl.BlockSpec(memory_space=pltpu.VMEM)
SMEM = pl.BlockSpec(memory_space=pltpu.SMEM)
BOTH = ("pulse", "grid")


def local(slabs, orbitals, potential, pulse, projectors, couplings, sphere_points, atom_count):
    _, nx, ny, channels = orbitals.shape
    cells = nx * ny
    atoms, k, size = projectors.shape
    part = channels // 16
    y, g = lax.axis_index("pulse"), lax.axis_index("grid")
    quads = slabs // GROUP
    quad = g // GROUP

    def permute(value, target):
        pairs = []
        for p in range(2):
            for s in range(slabs):
                to = target(p, s)
                if to is not None:
                    pairs.append((p * slabs + s, to[0] * slabs + to[1]))
        return lax.ppermute(value, BOTH, pairs)

    def swap_core(value):
        return permute(value, lambda p, s: (p, s ^ 1))

    def shift(value, by):
        return permute(value, lambda p, s: (p, s + by) if 0 <= s + by < slabs else None)

    bundle = jax.ShapeDtypeStruct((5 * channels // 16, cells), F32)
    near, far, heavy = pl.pallas_call(
        pack_kernel,
        out_shape=(bundle, bundle, jax.ShapeDtypeStruct((32, cells), F32)),
        in_specs=[VMEM] * 5 + [SMEM],
        out_specs=[VMEM] * 3,
        scratch_shapes=[pltpu.VMEM((cells, channels // 2), F32), pltpu.VMEM((channels // 2, cells), F32)],
        name="pack",
    )(orbitals.reshape(cells, channels), potential.reshape(nx, ny), projectors, couplings, sphere_points, atom_count)

    beside = permute(far, lambda p, s: (p, s ^ 2))
    below1, above1 = shift(near, GROUP), shift(near, -GROUP)
    below2, above2 = shift(beside, GROUP), shift(beside, -GROUP)
    other_pulse = permute(pulse, lambda p, s: (1 - p, s))
    order = []
    for piece in (below1, below2, near, beside, above1, above2):
        order += [piece, swap_core(piece)]

    edge = max(slabs // 8, 1)
    shared_heavy = not (edge == 2 and quads >= 4)
    if shared_heavy:
        everywhere = lax.all_gather(heavy, "grid")
        blank = jnp.zeros((HALO - 1,) + heavy.shape, F32)
        padded = jnp.concatenate([blank, everywhere, blank])
        heavies = [lax.dynamic_slice_in_dim(padded, quad * GROUP, SLOTS - 2)]
        stores = SLOTS - 2
    else:
        crowded = (0, 1, slabs - 2, slabs - 1)
        across = permute(heavy, lambda p, s: (p, s ^ 2) if s in crowded else None)
        x = (g // 2) % 2
        own = ((quad == 0) & (x == 0)) | ((quad == quads - 1) & (x == 1))
        held = jnp.where(own, heavy, across)

        def outward(p, s):
            if s // GROUP == 0 and s % 2 == 1:
                return p, s + GROUP
            if s // GROUP == quads - 1 and s % 2 == 0:
                return p, s - GROUP
            return None

        moved = permute(held, outward)
        held = jnp.where((quad == 0) | (quad == quads - 1), held, moved)
        heavies = [held, swap_core(held)]
        stores = 2

    wide = 3 * atoms * k
    outs = pl.pallas_call(
        functools.partial(evolve_kernel, slabs, shared_heavy),
        out_shape=[jax.ShapeDtypeStruct((4 * part, cells), F32)] * 4 + [jax.ShapeDtypeStruct((2, 128), F32)],
        in_specs=[SMEM] * 2 + [VMEM] * (12 + len(heavies)),
        out_specs=[VMEM] * 5,
        scratch_shapes=[
            pltpu.VMEM((SLOTS, 2 * part, cells), F32),
            pltpu.VMEM((SLOTS, 4 * part, cells), F32),
            pltpu.VMEM((SLOTS, 4 * part, cells), F32),
            pltpu.VMEM((SLOTS, 4 * part, cells), BF16),
            pltpu.VMEM((SLOTS, 8 * part, cells), BF16),
            pltpu.VMEM((GROUP, 4 * part, cells), F32),
            pltpu.VMEM((SLOTS, 3 * LIGHT * k, cells), BF16),
            pltpu.VMEM((stores, wide, cells), BF16),
            pltpu.VMEM((SLOTS, 1, cells), F32),
            pltpu.VMEM((SLOTS, 1, 128), F32),
            pltpu.VMEM((4 * part, cells), F32),
        ],
        compiler_params=pltpu.CompilerParams(vmem_limit_bytes=50 * 2**20),
        name="evolve",
    )(pulse, other_pulse, *order, *heavies)
    moment = outs[4]
    finals = [
        outs[0],
        permute(outs[1], lambda p, s: (p, s ^ 2)),
        permute(outs[2], lambda p, s: (1 - p, s)),
        permute(outs[3], lambda p, s: (1 - p, s ^ 2)),
    ]
    pieces = []
    for piece in finals:
        pieces += [piece, swap_core(piece)]
    plane = pl.pallas_call(
        unpack_kernel,
        out_shape=jax.ShapeDtypeStruct((cells, channels), F32),
        in_specs=[VMEM] * 8,
        out_specs=VMEM,
        scratch_shapes=[pltpu.VMEM((channels, cells), F32)] + [pltpu.VMEM((cells, channels // 2), F32)] * 2,
        name="unpack",
    )(*pieces)

    shares = moment[:, :1]
    step = 1
    while step < quads:
        if quads & (quads - 1) == 0:
            shares = shares + permute(shares, lambda p, s, step=step: (p, s ^ (step * GROUP)))
            step *= 2
        else:
            shares = lax.psum(shares, BOTH) if step == 1 else shares
            step = quads
    if quads & (quads - 1) == 0:
        for target in (lambda p, s: (p, s ^ 1), lambda p, s: (p, s ^ 2), lambda p, s: (1 - p, s)):
            shares = shares + permute(shares, target)
    total = jnp.where(y == 0, shares[0], shares[1])
    dipole = total / (slabs * cells * (channels // 2))
    return plane.reshape(orbitals.shape), dipole.reshape(1)


def solution(mesh):
    placed = (
        P("grid", None, None, None),
        P("grid", None, None),
        P("pulse"),
        P("grid", None, None),
        P("grid", None),
        P("grid", None),
        P("grid"),
    )
    return jax.shard_map(
        functools.partial(local, mesh.shape["grid"]),
        mesh=mesh,
        in_specs=placed,
        out_specs=(P(("pulse", "grid"), None, None, None), P("pulse")),
        check_vma=False,
    )
```

time: 280 us -> 111 us (0.40)
  other arithmetic: 109 us -> 0.95 us
  local copies, waits for them, and re-layouts: 78.6 us -> 3.39 us
  Pallas kernels: 0 us -> 34.3 us
  blocking collectives: 32.8 us -> 0 us
  matrix products: 26.8 us -> 0 us
  waiting for transfers between devices: 0.02 us -> 24.3 us
  starting transfers between devices: 26.8 us -> 43.3 us
    scatter-add x4 -> x0, other arithmetic: 93 us -> none  [advance(): target.at[sphere_points.reshape(-1)].add(contribution.reshape(-1, channels))]
    gather x4 -> x0, local copies, waits for them, and re-layouts: 65.8 us -> none  [advance(): samples = flat_in[sphere_points]]
    pallas_call x0 -> x3, Pallas kernels: none -> 34.3 us  [the longest x1 28.6 us: local(): pl.pallas_call(functools.partial(evolve_kernel, slabs, shared_heavy), out...]
    psum x1 -> x0, blocking collectives: 32.8 us -> none  [local(): moment = lax.psum(local_moment, 'grid')]
    dot_general x8 -> x0, matrix products: 26.8 us -> none  [the longest x4 20.7 us: sphere_terms(): jnp.einsum('akp,akc->apc', proj_block, scaled, precision=lax.Precision.HI...]
    ppermute x8 -> x27, waiting for transfers between devices: 0.02 us -> 24.3 us  [permute(): return lax.ppermute(value, BOTH, pairs)]
    ppermute x8 -> x27, starting transfers between devices: 26.8 us -> 43.3 us  [permute(): return lax.ppermute(value, BOTH, pairs)]
    add x4 -> x5, other arithmetic: 8.38 us -> 0.02 us  [the longest x3 0.01 us: local(): shares = shares + permute(shares, target)]
  transfers between devices with their start and end apart: 8 -> 27, of which waited for: 0 -> 11; matrix products, arithmetic and copies ran while one was open for 29% -> 1% of each run, Pallas kernels for 0% -> 0%
where the time goes in v1:
time: 111 us
  starting transfers between devices  43.3 us (39%)
  Pallas kernels  34.3 us (31%)
  waiting for transfers between devices  24.3 us (22%)
  between operations  4.64 us (4%)
  local copies, waits for them, and re-layouts  3.39 us (3%)
    ppermute x27, starting transfers between devices, permute(): return lax.ppermute(value, BOTH, pairs)  43.3 us
    pallas_call x1, Pallas kernels, local(): pl.pallas_call(functools.partial(evolve_kernel, slabs, shared_heavy), out...  28.6 us
    ppermute x27, waiting for transfers between devices, permute(): return lax.ppermute(value, BOTH, pairs)  24.3 us
    pallas_call x1, Pallas kernels, local(): pl.pallas_call(unpack_kernel, out_shape=jax.ShapeDtypeStruct((cells, chan...  2.99 us
    unnamed x27, local copies, waits for them, and re-layouts  2.87 us
    pallas_call x1, Pallas kernels, local(): pl.pallas_call(pack_kernel, out_shape=(bundle, bundle, jax.ShapeDtypeStru...  2.72 us
  transfers between devices with their start and end apart: 27, of which 11 were waited for; matrix products, arithmetic and copies ran while one was open for 1% of the time, Pallas kernels for 0%

profile of v1, /device:TPU:0, one launch (start us, length us, event | category | flops | bytes accessed | tf_op | source)
XLA Modules:
  0.0 110.9 jit_solution(12365155502193187244)
XLA Ops:
  1.3 1.4 %copy.9.coup = f32[16,8]{1,0:T(8,128)} copy(f32[16,8]{0,1:T(8,128)} %param.11) | data formatting | bytes 1024 | tf_op args[4]
  2.6 2.7 %pack.1 = (f32[80,1024]{1,0:T(8,128)}, f32[80,1024]{1,0:T(8,128)}, f32[32,1024]{1,0:T(8,128)}) custom-call(f32[1024,256]{1,0:T(8,128)} %bitcast.9, f32[32,32]{1,0:T(8,128)} %bitcast.10, bf16[16,8,256]{2,1,0:T(8,128)(2,1)} %proj.1, f32[16,8]{1,0:T(8,128)} %copy.9.coup, s32[16,256]{1,0:T(8,128)} %points.1, s32[1]{0:T(128)S(6)} %copy.11.count), custom_call_target="tpu_custom_call" | custom-call | tf_op jit(solution)/shard_map/pack/pallas_call | solution.py:404
  5.3 5.0 %collective-permute-start.12 = (f32[32,1024]{1,0:T(8,128)}, f32[32,1024]{1,0:T(8,128)S(1)}, u32[]{:S(2)}, u32[]{:S(2)}) collective-permute-start(f32[32,1024]{1,0:T(8,128)} %get-tuple-element.12), channel_id=1, source_target_pairs={{0,2},{1,3},{14,12},{15,13},{16,18},{17,19},{30,28},{31,29}} | collective-permute-start | bytes 393224 | tf_op jit(solution)/shard_map/ppermute | solution.py:395
  10.3 0.1 collective-permute-start.3
  10.4 4.1 %collective-permute-done.12 = f32[32,1024]{1,0:T(8,128)S(1)} collective-permute-done((f32[32,1024]{1,0:T(8,128)}, f32[32,1024]{1,0:T(8,128)S(1)}, u32[]{:S(2)}, u32[]{:S(2)}) %collective-permute-start.12) | collective-permute-done | bytes 131104 | tf_op jit(solution)/shard_map/ppermute | solution.py:395
  14.5 0.9 broadcast_select_fusion
  15.4 0.7 collective-permute-start.13
  16.1 1.3 %collective-permute-start.8 = (f32[80,1024]{1,0:T(8,128)S(1)}, f32[80,1024]{1,0:T(8,128)S(1)}, u32[]{:S(2)}, u32[]{:S(2)}) collective-permute-start(f32[80,1024]{1,0:T(8,128)S(1)} %copy-done), channel_id=1, source_target_pairs={{4,0},{5,1},{6,2},{7,3},{8,4},{9,5},{10,6},{11,7},{12,8},{13,9},{1... | collective-permute-start | bytes 983048 | tf_op jit(solution)/shard_map/ppermute | solution.py:395
  17.4 0.1 collective-permute-start.6
  17.5 1.6 %collective-permute-start = (f32[1]{0:T(128)}, f32[1]{0:T(128)}, u32[]{:S(2)}, u32[]{:S(2)}) collective-permute-start(f32[1]{0:T(128)} %param.9), channel_id=1, source_target_pairs={{0,16},{1,17},{2,18},{3,19},{4,20},{5,21},{6,22},{7,23},{8,24},{9,... | collective-permute-start | bytes 20 | tf_op jit(solution)/shard_map/ppermute | solution.py:395
  19.1 2.1 %collective-permute-done.refs_1_ = f32[1]{0:T(128)} collective-permute-done((f32[1]{0:T(128)}, f32[1]{0:T(128)}, u32[]{:S(2)}, u32[]{:S(2)}) %collective-permute-start) | collective-permute-done | bytes 36 | tf_op jit(solution)/shard_map/ppermute | solution.py:395
  21.2 4.6 %collective-permute-start.1 = (f32[80,1024]{1,0:T(8,128)S(1)}, f32[80,1024]{1,0:T(8,128)S(1)}, u32[]{:S(2)}, u32[]{:S(2)}) collective-permute-start(f32[80,1024]{1,0:T(8,128)S(1)} %copy-done), channel_id=1, source_target_pairs={{0,4},{1,5},{2,6},{3,7},{4,8},{5,9},{6,10},{7,11},{8,12},{9,13},{1... | collective-permute-start | bytes 983048 | tf_op jit(solution)/shard_map/ppermute | solution.py:395
  25.8 1.3 %collective-permute-start.10 = (f32[80,1024]{1,0:T(8,128)S(1)}, f32[80,1024]{1,0:T(8,128)S(1)}, u32[]{:S(2)}, u32[]{:S(2)}) collective-permute-start(f32[80,1024]{1,0:T(8,128)S(1)} %collective-permute-done.3.refs_8_), channel_id=1, source_target_pairs={{4,0},{5,1},{6,2},{7,3},{8,4},{9,5},{10,6},{11,7},{12,8},{13,9},{1... | collective-permute-start | bytes 983048 | tf_op jit(solution)/shard_map/ppermute | solution.py:395
  27.1 0.0 collective-permute-done.13
  27.1 4.6 %collective-permute-start.4 = (f32[80,1024]{1,0:T(8,128)S(1)}, f32[80,1024]{1,0:T(8,128)S(1)}, u32[]{:S(2)}, u32[]{:S(2)}) collective-permute-start(f32[80,1024]{1,0:T(8,128)S(1)} %collective-permute-done.3.refs_8_), channel_id=1, source_target_pairs={{0,4},{1,5},{2,6},{3,7},{4,8},{5,9},{6,10},{7,11},{8,12},{9,13},{1... | collective-permute-start | bytes 983048 | tf_op jit(solution)/shard_map/ppermute | solution.py:395
  31.7 0.0 collective-permute-done.8.refs_10_
  31.7 0.0 copy-start.2
  31.7 0.1 collective-permute-start.14
  31.8 0.0 collective-permute-done.6.refs_7_
  31.8 0.5 collective-permute-start.7
  32.3 1.6 %collective-permute-done.1.refs_2_ = f32[80,1024]{1,0:T(8,128)S(1)} collective-permute-done((f32[80,1024]{1,0:T(8,128)S(1)}, f32[80,1024]{1,0:T(8,128)S(1)}, u32[]{:S(2)}, u32[]{:S(2)}) %collective-permute-start.1) | collective-permute-done | bytes 327712 | tf_op jit(solution)/shard_map/ppermute | solution.py:395
  33.9 0.0 collective-permute-start.9
  33.9 0.0 collective-permute-done.14.refs_15_
  33.9 0.5 collective-permute-start.2
  34.4 2.0 %collective-permute-done.10.refs_12_ = f32[80,1024]{1,0:T(8,128)S(1)} collective-permute-done((f32[80,1024]{1,0:T(8,128)S(1)}, f32[80,1024]{1,0:T(8,128)S(1)}, u32[]{:S(2)}, u32[]{:S(2)}) %collective-permute-start.10) | collective-permute-done | bytes 327712 | tf_op jit(solution)/shard_map/ppermute | solution.py:395
  36.5 2.9 %collective-permute-done.4.refs_4_ = f32[80,1024]{1,0:T(8,128)S(1)} collective-permute-done((f32[80,1024]{1,0:T(8,128)S(1)}, f32[80,1024]{1,0:T(8,128)S(1)}, u32[]{:S(2)}, u32[]{:S(2)}) %collective-permute-start.4) | collective-permute-done | bytes 327712 | tf_op jit(solution)/shard_map/ppermute | solution.py:395
  40.0 0.9 collective-permute-done.5.refs_5_
  41.0 28.6 %evolve.1 = (f32[64,1024]{1,0:T(8,128)S(1)}, f32[64,1024]{1,0:T(8,128)S(1)}, f32[64,1024]{1,0:T(8,128)S(1)}, f32[64,1024]{1,0:T(8,128)S(1)}, f32[2,128]{1,0:T(2,128)S(1)}) custom-call(f32[1]{0:T(128)S(6)} %copy.10.refs_0_, f32[1]{0:T(128)} %collective-permute-done.refs_1_, f32[80,1024]{1,0:T(8,128)S(1)} %collective-permute-done.1.refs_2_, ...), custom_call_target="tpu_custom_call" | custom-call | tf_op jit(solution)/shard_map/evolve/pallas_call | solution.py:449
  69.6 1.6 %collective-permute-start.16 = (f32[64,1024]{1,0:T(8,128)S(1)}, f32[64,1024]{1,0:T(8,128)S(1)}, u32[]{:S(2)}, u32[]{:S(2)}) collective-permute-start(f32[64,1024]{1,0:T(8,128)S(1)} %get-tuple-element.14), channel_id=1, source_target_pairs={{0,2},{1,3},{2,0},{3,1},{4,6},{5,7},{6,4},{7,5},{8,10},{9,11},{10,... | collective-permute-start | bytes 786440 | tf_op jit(solution)/shard_map/ppermute | solution.py:395
  71.1 1.5 %collective-permute-start.18 = (f32[64,1024]{1,0:T(8,128)S(1)}, f32[64,1024]{1,0:T(8,128)S(1)}, u32[]{:S(2)}, u32[]{:S(2)}) collective-permute-start(f32[64,1024]{1,0:T(8,128)S(1)} %get-tuple-element.15), channel_id=1, source_target_pairs={{0,16},{1,17},{2,18},{3,19},{4,20},{5,21},{6,22},{7,23},{8,24},{9,... | collective-permute-start | bytes 786440 | tf_op jit(solution)/shard_map/ppermute | solution.py:395
  72.6 0.5 collective-permute-start.20
  73.1 8.3 %collective-permute-start.22 = (f32[2,1]{1,0:T(2,128)S(1)}, f32[2,1]{1,0:T(2,128)S(1)}, u32[]{:S(2)}, u32[]{:S(2)}) collective-permute-start(f32[2,1]{1,0:T(2,128)S(1)} %bitcast.7), channel_id=1, source_target_pairs={{0,4},{1,5},{2,6},{3,7},{4,0},{5,1},{6,2},{7,3},{8,12},{9,13},{10,... | collective-permute-start | bytes 32 | tf_op jit(solution)/shard_map/ppermute | solution.py:395
  81.4 0.5 collective-permute-start.17
  81.9 3.2 %collective-permute-done.18.refs_4_ = f32[64,1024]{1,0:T(8,128)S(1)} collective-permute-done((f32[64,1024]{1,0:T(8,128)S(1)}, f32[64,1024]{1,0:T(8,128)S(1)}, u32[]{:S(2)}, u32[]{:S(2)}) %collective-permute-start.18) | collective-permute-done | bytes 262176 | tf_op jit(solution)/shard_map/ppermute | solution.py:395
  85.1 0.5 collective-permute-start.21
  85.6 8.0 %collective-permute-start.23 = (f32[2,1]{1,0:T(2,128)S(1)}, f32[2,1]{1,0:T(2,128)S(1)}, u32[]{:S(2)}, u32[]{:S(2)}) collective-permute-start(f32[2,1]{1,0:T(2,128)S(1)} %slice_add_fusion), channel_id=1, source_target_pairs={{0,8},{1,9},{2,10},{3,11},{4,12},{5,13},{6,14},{7,15},{8,0},{9,1},... | collective-permute-start | bytes 32 | tf_op jit(solution)/shard_map/ppermute | solution.py:395
  93.6 1.5 %collective-permute-done.23 = f32[2,1]{1,0:T(2,128)S(1)} collective-permute-done((f32[2,1]{1,0:T(2,128)S(1)}, f32[2,1]{1,0:T(2,128)S(1)}, u32[]{:S(2)}, u32[]{:S(2)}) %collective-permute-start.23) | collective-permute-done | bytes 40 | tf_op jit(solution)/shard_map/ppermute | solution.py:395
  95.2 1.1 %collective-permute-done.24 = f32[2,1]{1,0:T(2,128)S(1)} collective-permute-done((f32[2,1]{1,0:T(2,128)S(1)}, f32[2,1]{1,0:T(2,128)S(1)}, u32[]{:S(2)}, u32[]{:S(2)}) %collective-permute-start.24) | collective-permute-done | bytes 40 | tf_op jit(solution)/shard_map/ppermute | solution.py:395
  96.3 0.8 collective-permute-start.25
  97.1 2.8 %collective-permute-done.25 = f32[2,1]{1,0:T(2,128)S(1)} collective-permute-done((f32[2,1]{1,0:T(2,128)S(1)}, f32[2,1]{1,0:T(2,128)S(1)}, u32[]{:S(2)}, u32[]{:S(2)}) %collective-permute-start.25) | collective-permute-done | bytes 40 | tf_op jit(solution)/shard_map/ppermute | solution.py:395
  99.9 1.5 %collective-permute-start.26 = (f32[2,1]{1,0:T(2,128)S(1)}, f32[2,1]{1,0:T(2,128)S(1)}, u32[]{:S(2)}, u32[]{:S(2)}) collective-permute-start(f32[2,1]{1,0:T(2,128)S(1)} %add.25), channel_id=1, source_target_pairs={{0,16},{1,17},{2,18},{3,19},{4,20},{5,21},{6,22},{7,23},{8,24},{9,... | collective-permute-start | bytes 32 | tf_op jit(solution)/shard_map/ppermute | solution.py:395
  101.4 2.0 %collective-permute-done.26 = f32[2,1]{1,0:T(2,128)S(1)} collective-permute-done((f32[2,1]{1,0:T(2,128)S(1)}, f32[2,1]{1,0:T(2,128)S(1)}, u32[]{:S(2)}, u32[]{:S(2)}) %collective-permute-start.26) | collective-permute-done | bytes 40 | tf_op jit(solution)/shard_map/ppermute | solution.py:395
  103.5 0.5 fusion
  105.3 0.6 copy-done.9
  105.9 0.1 copy-done.10
  106.0 0.1 copy-done.11
  106.1 0.7 copy-done.12
  106.8 3.0 %unpack.1 = f32[1024,256]{1,0:T(8,128)} custom-call(f32[64,1024]{1,0:T(8,128)} %copy-done.1, f32[64,1024]{1,0:T(8,128)} %copy-done.9, f32[64,1024]{1,0:T(8,128)} %copy-done.6, f32[64,1024]{1,0:T(8,128)} %copy-done.10, f32[64,1024]{1,0:T(8,128)} %copy-done.7, f32[64,1024]{1,0:T(8,128)} %copy-done.11, f32[64,1024]{1,0:T(8,128)} %copy-done.8, f32[64,1024]{1,0:T(8,128)} %copy-done.12), custom_call_target="tpu_custom_call" | custom-call | tf_op jit(solution)/shard_map/unpack/pallas_call | solution.py:480
  (44 shorter events, 0.1 us)
Async XLA Ops:
  5.3 10.8 %copy-start = (f32[80,1024]{1,0:T(8,128)S(1)}, f32[80,1024]{1,0:T(8,128)}, u32[]{:S(2)}) copy-start(f32[80,1024]{1,0:T(8,128)} %get-tuple-element.10.refs_6_) | copy-start | bytes 983044
  5.3 9.2 %collective-permute-start.12 = (f32[32,1024]{1,0:T(8,128)}, f32[32,1024]{1,0:T(8,128)S(1)}, u32[]{:S(2)}, u32[]{:S(2)}) collective-permute-start(f32[32,1024]{1,0:T(8,128)} %get-tuple-element.12), channel_id=1, source_target_pairs={{0,2},{1,3},{14,12},{15,13},{16,18},{17,19},{30,28},{31,29}} | collective-permute-start | bytes 393224 | tf_op jit(solution)/shard_map/ppermute | solution.py:395
  10.3 15.4 %collective-permute-start.3 = (f32[80,1024]{1,0:T(8,128)}, f32[80,1024]{1,0:T(8,128)S(1)}, u32[]{:S(2)}, u32[]{:S(2)}) collective-permute-start(f32[80,1024]{1,0:T(8,128)} %get-tuple-element.11), channel_id=1, source_target_pairs={{0,2},{1,3},{2,0},{3,1},{4,6},{5,7},{6,4},{7,5},{8,10},{9,11},{10,... | collective-permute-start | bytes 983048 | tf_op jit(solution)/shard_map/ppermute | solution.py:395
  15.4 11.6 %collective-permute-start.13 = (f32[32,1024]{1,0:T(8,128)S(1)}, f32[32,1024]{1,0:T(8,128)S(1)}, u32[]{:S(2)}, u32[]{:S(2)}) collective-permute-start(f32[32,1024]{1,0:T(8,128)S(1)} %broadcast_select_fusion), channel_id=1, source_target_pairs={{1,5},{3,7},{12,8},{14,10},{17,21},{19,23},{28,24},{30,26}} | collective-permute-start | bytes 393224 | tf_op jit(solution)/shard_map/ppermute | solution.py:395
  16.1 15.6 %collective-permute-start.8 = (f32[80,1024]{1,0:T(8,128)S(1)}, f32[80,1024]{1,0:T(8,128)S(1)}, u32[]{:S(2)}, u32[]{:S(2)}) collective-permute-start(f32[80,1024]{1,0:T(8,128)S(1)} %copy-done), channel_id=1, source_target_pairs={{4,0},{5,1},{6,2},{7,3},{8,4},{9,5},{10,6},{11,7},{12,8},{13,9},{1... | collective-permute-start | bytes 983048 | tf_op jit(solution)/shard_map/ppermute | solution.py:395
  17.4 14.4 %collective-permute-start.6 = (f32[80,1024]{1,0:T(8,128)S(1)}, f32[80,1024]{1,0:T(8,128)S(1)}, u32[]{:S(2)}, u32[]{:S(2)}) collective-permute-start(f32[80,1024]{1,0:T(8,128)S(1)} %copy-done), channel_id=1, source_target_pairs={{0,1},{1,0},{2,3},{3,2},{4,5},{5,4},{6,7},{7,6},{8,9},{9,8},{10,11... | collective-permute-start | bytes 983048 | tf_op jit(solution)/shard_map/ppermute | solution.py:395
  17.5 3.7 %collective-permute-start = (f32[1]{0:T(128)}, f32[1]{0:T(128)}, u32[]{:S(2)}, u32[]{:S(2)}) collective-permute-start(f32[1]{0:T(128)} %param.9), channel_id=1, source_target_pairs={{0,16},{1,17},{2,18},{3,19},{4,20},{5,21},{6,22},{7,23},{8,24},{9,... | collective-permute-start | bytes 20 | tf_op jit(solution)/shard_map/ppermute | solution.py:395
  21.2 12.7 %collective-permute-start.1 = (f32[80,1024]{1,0:T(8,128)S(1)}, f32[80,1024]{1,0:T(8,128)S(1)}, u32[]{:S(2)}, u32[]{:S(2)}) collective-permute-start(f32[80,1024]{1,0:T(8,128)S(1)} %copy-done), channel_id=1, source_target_pairs={{0,4},{1,5},{2,6},{3,7},{4,8},{5,9},{6,10},{7,11},{8,12},{9,13},{1... | collective-permute-start | bytes 983048 | tf_op jit(solution)/shard_map/ppermute | solution.py:395
  25.8 10.7 %collective-permute-start.10 = (f32[80,1024]{1,0:T(8,128)S(1)}, f32[80,1024]{1,0:T(8,128)S(1)}, u32[]{:S(2)}, u32[]{:S(2)}) collective-permute-start(f32[80,1024]{1,0:T(8,128)S(1)} %collective-permute-done.3.refs_8_), channel_id=1, source_target_pairs={{4,0},{5,1},{6,2},{7,3},{8,4},{9,5},{10,6},{11,7},{12,8},{13,9},{1... | collective-permute-start | bytes 983048 | tf_op jit(solution)/shard_map/ppermute | solution.py:395
  27.1 12.2 %collective-permute-start.4 = (f32[80,1024]{1,0:T(8,128)S(1)}, f32[80,1024]{1,0:T(8,128)S(1)}, u32[]{:S(2)}, u32[]{:S(2)}) collective-permute-start(f32[80,1024]{1,0:T(8,128)S(1)} %collective-permute-done.3.refs_8_), channel_id=1, source_target_pairs={{0,4},{1,5},{2,6},{3,7},{4,8},{5,9},{6,10},{7,11},{8,12},{9,13},{1... | collective-permute-start | bytes 983048 | tf_op jit(solution)/shard_map/ppermute | solution.py:395
  31.7 9.3 %copy-start.2 = (f32[80,1024]{1,0:T(8,128)}, f32[80,1024]{1,0:T(8,128)S(1)}, u32[]{:S(2)}) copy-start(f32[80,1024]{1,0:T(8,128)S(1)} %collective-permute-done.8.refs_10_) | copy-start | bytes 983044
  31.7 2.2 %collective-permute-start.14 = (f32[32,1024]{1,0:T(8,128)S(1)}, f32[32,1024]{1,0:T(8,128)S(1)}, u32[]{:S(2)}, u32[]{:S(2)}) collective-permute-start(f32[32,1024]{1,0:T(8,128)S(1)} %broadcast_select_fusion.1.refs_14_), channel_id=1, source_target_pairs={{0,1},{1,0},{2,3},{3,2},{4,5},{5,4},{6,7},{7,6},{8,9},{9,8},{10,11... | collective-permute-start | bytes 393224 | tf_op jit(solution)/shard_map/ppermute | solution.py:395
  31.8 8.2 %collective-permute-start.7 = (f32[80,1024]{1,0:T(8,128)S(1)}, f32[80,1024]{1,0:T(8,128)S(1)}, u32[]{:S(2)}, u32[]{:S(2)}) collective-permute-start(f32[80,1024]{1,0:T(8,128)S(1)} %collective-permute-done.3.refs_8_), channel_id=1, source_target_pairs={{0,1},{1,0},{2,3},{3,2},{4,5},{5,4},{6,7},{7,6},{8,9},{9,8},{10,11... | collective-permute-start | bytes 983048 | tf_op jit(solution)/shard_map/ppermute | solution.py:395
  33.9 6.1 %collective-permute-start.9 = (f32[80,1024]{1,0:T(8,128)S(1)}, f32[80,1024]{1,0:T(8,128)S(1)}, u32[]{:S(2)}, u32[]{:S(2)}) collective-permute-start(f32[80,1024]{1,0:T(8,128)S(1)} %collective-permute-done.8.refs_10_), channel_id=1, source_target_pairs={{0,1},{1,0},{2,3},{3,2},{4,5},{5,4},{6,7},{7,6},{8,9},{9,8},{10,11... | collective-permute-start | bytes 983048 | tf_op jit(solution)/shard_map/ppermute | solution.py:395
  33.9 6.1 %collective-permute-start.2 = (f32[80,1024]{1,0:T(8,128)S(1)}, f32[80,1024]{1,0:T(8,128)S(1)}, u32[]{:S(2)}, u32[]{:S(2)}) collective-permute-start(f32[80,1024]{1,0:T(8,128)S(1)} %collective-permute-done.1.refs_2_), channel_id=1, source_target_pairs={{0,1},{1,0},{2,3},{3,2},{4,5},{5,4},{6,7},{7,6},{8,9},{9,8},{10,11... | collective-permute-start | bytes 983048 | tf_op jit(solution)/shard_map/ppermute | solution.py:395
  36.4 4.5 %copy-start.3 = (f32[80,1024]{1,0:T(8,128)}, f32[80,1024]{1,0:T(8,128)S(1)}, u32[]{:S(2)}) copy-start(f32[80,1024]{1,0:T(8,128)S(1)} %collective-permute-done.10.refs_12_) | copy-start | bytes 983044
  36.5 3.6 %collective-permute-start.11 = (f32[80,1024]{1,0:T(8,128)S(1)}, f32[80,1024]{1,0:T(8,128)S(1)}, u32[]{:S(2)}, u32[]{:S(2)}) collective-permute-start(f32[80,1024]{1,0:T(8,128)S(1)} %collective-permute-done.10.refs_12_), channel_id=1, source_target_pairs={{0,1},{1,0},{2,3},{3,2},{4,5},{5,4},{6,7},{7,6},{8,9},{9,8},{10,11... | collective-permute-start | bytes 983048 | tf_op jit(solution)/shard_map/ppermute | solution.py:395
  39.3 1.6 %collective-permute-start.5 = (f32[80,1024]{1,0:T(8,128)S(1)}, f32[80,1024]{1,0:T(8,128)S(1)}, u32[]{:S(2)}, u32[]{:S(2)}) collective-permute-start(f32[80,1024]{1,0:T(8,128)S(1)} %collective-permute-done.4.refs_4_), channel_id=1, source_target_pairs={{0,1},{1,0},{2,3},{3,2},{4,5},{5,4},{6,7},{7,6},{8,9},{9,8},{10,11... | collective-permute-start | bytes 983048 | tf_op jit(solution)/shard_map/ppermute | solution.py:395
  40.0 1.0 copy-start.4
  40.0 0.9 copy-start.5
  69.6 35.7 %copy-start.1 = (f32[64,1024]{1,0:T(8,128)}, f32[64,1024]{1,0:T(8,128)S(1)}, u32[]{:S(2)}) copy-start(f32[64,1024]{1,0:T(8,128)S(1)} %get-tuple-element.13.refs_0_) | copy-start | bytes 786436
  69.6 11.8 %collective-permute-start.16 = (f32[64,1024]{1,0:T(8,128)S(1)}, f32[64,1024]{1,0:T(8,128)S(1)}, u32[]{:S(2)}, u32[]{:S(2)}) collective-permute-start(f32[64,1024]{1,0:T(8,128)S(1)} %get-tuple-element.14), channel_id=1, source_target_pairs={{0,2},{1,3},{2,0},{3,1},{4,6},{5,7},{6,4},{7,5},{8,10},{9,11},{10,... | collective-permute-start | bytes 786440 | tf_op jit(solution)/shard_map/ppermute | solution.py:395
  71.1 14.0 %collective-permute-start.18 = (f32[64,1024]{1,0:T(8,128)S(1)}, f32[64,1024]{1,0:T(8,128)S(1)}, u32[]{:S(2)}, u32[]{:S(2)}) collective-permute-start(f32[64,1024]{1,0:T(8,128)S(1)} %get-tuple-element.15), channel_id=1, source_target_pairs={{0,16},{1,17},{2,18},{3,19},{4,20},{5,21},{6,22},{7,23},{8,24},{9,... | collective-permute-start | bytes 786440 | tf_op jit(solution)/shard_map/ppermute | solution.py:395
  72.6 12.5 %collective-permute-start.20 = (f32[64,1024]{1,0:T(8,128)S(1)}, f32[64,1024]{1,0:T(8,128)S(1)}, u32[]{:S(2)}, u32[]{:S(2)}) collective-permute-start(f32[64,1024]{1,0:T(8,128)S(1)} %get-tuple-element.16), channel_id=1, source_target_pairs={{0,18},{1,19},{2,16},{3,17},{4,22},{5,23},{6,20},{7,21},{8,26},{9,... | collective-permute-start | bytes 786440 | tf_op jit(solution)/shard_map/ppermute | solution.py:395
  73.1 12.5 %collective-permute-start.22 = (f32[2,1]{1,0:T(2,128)S(1)}, f32[2,1]{1,0:T(2,128)S(1)}, u32[]{:S(2)}, u32[]{:S(2)}) collective-permute-start(f32[2,1]{1,0:T(2,128)S(1)} %bitcast.7), channel_id=1, source_target_pairs={{0,4},{1,5},{2,6},{3,7},{4,0},{5,1},{6,2},{7,3},{8,12},{9,13},{10,... | collective-permute-start | bytes 32 | tf_op jit(solution)/shard_map/ppermute | solution.py:395
  81.4 23.8 %collective-permute-start.15 = (f32[64,1024]{1,0:T(8,128)S(1)}, f32[64,1024]{1,0:T(8,128)S(1)}, u32[]{:S(2)}, u32[]{:S(2)}) collective-permute-start(f32[64,1024]{1,0:T(8,128)S(1)} %get-tuple-element.13.refs_0_), channel_id=1, source_target_pairs={{0,1},{1,0},{2,3},{3,2},{4,5},{5,4},{6,7},{7,6},{8,9},{9,8},{10,11... | collective-permute-start | bytes 786440 | tf_op jit(solution)/shard_map/ppermute | solution.py:395
  81.4 23.9 %copy-start.6 = (f32[64,1024]{1,0:T(8,128)}, f32[64,1024]{1,0:T(8,128)S(1)}, u32[]{:S(2)}) copy-start(f32[64,1024]{1,0:T(8,128)S(1)} %collective-permute-done.16.refs_2_) | copy-start | bytes 786436
  81.4 23.8 %collective-permute-start.17 = (f32[64,1024]{1,0:T(8,128)S(1)}, f32[64,1024]{1,0:T(8,128)S(1)}, u32[]{:S(2)}, u32[]{:S(2)}) collective-permute-start(f32[64,1024]{1,0:T(8,128)S(1)} %collective-permute-done.16.refs_2_), channel_id=1, source_target_pairs={{0,1},{1,0},{2,3},{3,2},{4,5},{5,4},{6,7},{7,6},{8,9},{9,8},{10,11... | collective-permute-start | bytes 786440 | tf_op jit(solution)/shard_map/ppermute | solution.py:395
  85.1 20.2 %copy-start.7 = (f32[64,1024]{1,0:T(8,128)}, f32[64,1024]{1,0:T(8,128)S(1)}, u32[]{:S(2)}) copy-start(f32[64,1024]{1,0:T(8,128)S(1)} %collective-permute-done.18.refs_4_) | copy-start | bytes 786436
  85.1 20.1 %collective-permute-start.19 = (f32[64,1024]{1,0:T(8,128)S(1)}, f32[64,1024]{1,0:T(8,128)S(1)}, u32[]{:S(2)}, u32[]{:S(2)}) collective-permute-start(f32[64,1024]{1,0:T(8,128)S(1)} %collective-permute-done.18.refs_4_), channel_id=1, source_target_pairs={{0,1},{1,0},{2,3},{3,2},{4,5},{5,4},{6,7},{7,6},{8,9},{9,8},{10,11... | collective-permute-start | bytes 786440 | tf_op jit(solution)/shard_map/ppermute | solution.py:395
  85.1 20.2 %copy-start.8 = (f32[64,1024]{1,0:T(8,128)}, f32[64,1024]{1,0:T(8,128)S(1)}, u32[]{:S(2)}) copy-start(f32[64,1024]{1,0:T(8,128)S(1)} %collective-permute-done.20.refs_6_) | copy-start | bytes 786436
  85.1 20.1 %collective-permute-start.21 = (f32[64,1024]{1,0:T(8,128)S(1)}, f32[64,1024]{1,0:T(8,128)S(1)}, u32[]{:S(2)}, u32[]{:S(2)}) collective-permute-start(f32[64,1024]{1,0:T(8,128)S(1)} %collective-permute-done.20.refs_6_), channel_id=1, source_target_pairs={{0,1},{1,0},{2,3},{3,2},{4,5},{5,4},{6,7},{7,6},{8,9},{9,8},{10,11... | collective-permute-start | bytes 786440 | tf_op jit(solution)/shard_map/ppermute | solution.py:395
  85.6 9.5 %collective-permute-start.23 = (f32[2,1]{1,0:T(2,128)S(1)}, f32[2,1]{1,0:T(2,128)S(1)}, u32[]{:S(2)}, u32[]{:S(2)}) collective-permute-start(f32[2,1]{1,0:T(2,128)S(1)} %slice_add_fusion), channel_id=1, source_target_pairs={{0,8},{1,9},{2,10},{3,11},{4,12},{5,13},{6,14},{7,15},{8,0},{9,1},... | collective-permute-start | bytes 32 | tf_op jit(solution)/shard_map/ppermute | solution.py:395
  95.2 1.1 %collective-permute-start.24 = (f32[2,1]{1,0:T(2,128)S(1)}, f32[2,1]{1,0:T(2,128)S(1)}, u32[]{:S(2)}, u32[]{:S(2)}) collective-permute-start(f32[2,1]{1,0:T(2,128)S(1)} %add.23), channel_id=1, source_target_pairs={{0,1},{1,0},{2,3},{3,2},{4,5},{5,4},{6,7},{7,6},{8,9},{9,8},{10,11... | collective-permute-start | bytes 32 | tf_op jit(solution)/shard_map/ppermute | solution.py:395
  96.3 3.6 %collective-permute-start.25 = (f32[2,1]{1,0:T(2,128)S(1)}, f32[2,1]{1,0:T(2,128)S(1)}, u32[]{:S(2)}, u32[]{:S(2)}) collective-permute-start(f32[2,1]{1,0:T(2,128)S(1)} %add.24), channel_id=1, source_target_pairs={{0,2},{1,3},{2,0},{3,1},{4,6},{5,7},{6,4},{7,5},{8,10},{9,11},{10,... | collective-permute-start | bytes 32 | tf_op jit(solution)/shard_map/ppermute | solution.py:395
  99.9 3.6 %collective-permute-start.26 = (f32[2,1]{1,0:T(2,128)S(1)}, f32[2,1]{1,0:T(2,128)S(1)}, u32[]{:S(2)}, u32[]{:S(2)}) collective-permute-start(f32[2,1]{1,0:T(2,128)S(1)} %add.25), channel_id=1, source_target_pairs={{0,16},{1,17},{2,18},{3,19},{4,20},{5,21},{6,22},{7,23},{8,24},{9,... | collective-permute-start | bytes 32 | tf_op jit(solution)/shard_map/ppermute | solution.py:395
  105.2 0.7 copy-start.9
  105.2 0.8 copy-start.10
  105.2 0.8 copy-start.11
  106.1 0.7 copy-start.12

commit v2 on v1

v2 whole, which is shorter than its diff:
```python
import functools

import jax
import jax.numpy as jnp
from jax import lax
from jax.experimental import pallas as pl
from jax.experimental.pallas import tpu as pltpu
from jax.sharding import PartitionSpec as P


TERMS = 4
TIME_STEP = 0.1
GROUP = 4
HALO = TERMS
SLOTS = GROUP + 2 * HALO
LIGHT = 4
F32 = jnp.float32
BF16 = jnp.bfloat16
NT = (((1,), (1,)), ((), ()))
NN = (((1,), (0,)), ((), ()))


def iota(shape, dim):
    return lax.broadcasted_iota(jnp.int32, shape, dim)


def split(value):
    high = value.astype(BF16)
    return high, (value - high.astype(F32)).astype(BF16)


def place():
    y, g = lax.axis_index("pulse"), lax.axis_index("grid")
    return y, g // GROUP, (g // 2) % 2, g % 2


def pack_kernel(orb, pot, proj, coup, points, count, near, far, packed, rows):
    y, _, x, _ = place()
    cells, channels = orb.shape
    lanes = cells // 8
    half = channels // 2
    first = iota((lanes, half), 1) < half // 2
    for j in range(8):
        chunk = slice(j * lanes, (j + 1) * lanes)
        re, im = orb[chunk, :half], orb[chunk, half:]
        low = jnp.where(first, re, pltpu.roll(im, half // 2, 1))
        high = jnp.where(first, pltpu.roll(re, half // 2, 1), im)
        packed[chunk, :] = jnp.where(y == 0, low, high)
    for j in range(8):
        rows[:, j * lanes : (j + 1) * lanes] = packed[pl.ds(j, lanes, stride=8), :].T
    part = half // 8
    for out, xx in ((near, x), (far, 1 - x)):
        for c in range(2):
            start = pl.multiple_of((2 * xx + c) * part, part)
            out[c * 2 * part : c * 2 * part + part, :] = rows[pl.ds(start, part), :]
            out[c * 2 * part + part : (c + 1) * 2 * part, :] = rows[pl.ds(start + half // 2, part), :]
    nx, ny = pot.shape
    yh = ny // 8
    col = iota((ny, cells), 1)
    pick = (iota((ny, cells), 0) == (col % lanes) % yh * 8 + col // lanes).astype(F32)
    spread = lax.dot_general(pot[...], pick, NN, precision=lax.Precision.HIGHEST, preferred_element_type=F32)
    keep = iota((nx, cells), 0) == (iota((nx, cells), 1) % lanes) // yh
    pot_row = jnp.sum(jnp.where(keep, spread, 0.0), axis=0, keepdims=True)
    k, atoms = coup.shape
    pick = (iota((atoms, atoms * k), 0) == iota((atoms, atoms * k), 1) // k).astype(F32)
    spread = lax.dot_general(coup[...], pick, NN, precision=lax.Precision.HIGHEST, preferred_element_type=F32)
    column = iota((k, atoms * k), 1)
    keep = (iota((k, atoms * k), 0) == column % k) & (column // k < count[0])
    weight_row = jnp.sum(jnp.where(keep, spread, 0.0), axis=0, keepdims=True)
    size = points.shape[1]
    base = 4 * part
    for out in (near, far):
        for a in range(LIGHT):
            out[base : base + k, a * size : (a + 1) * size] = proj[a].astype(F32)
            out[base + k : base + k + 1, a * size : (a + 1) * size] = points[a : a + 1, :].astype(F32)
        out[base + k + 1 : base + k + 2, :] = pot_row
        out[base + k + 2 : base + k + 3, :] = jnp.zeros((1, cells), F32)
        out[base + k + 2 : base + k + 3, : atoms * k] = weight_row
        out[base + k + 3 : base + k + 8, :] = jnp.zeros((5, cells), F32)


def rest_kernel(proj, points, near, rest):
    atoms, k, size = proj.shape
    groups = atoms // LIGHT - 1
    for group in range(groups):
        for a in range(LIGHT):
            source = (group + 1) * LIGHT + a
            rest[group * k : (group + 1) * k, a * size : (a + 1) * size] = proj[source].astype(F32)
            rest[groups * k + group : groups * k + group + 1, a * size : (a + 1) * size] = (
                points[source : source + 1, :].astype(F32)
            )
    used = groups * (k + 1)
    rest[used:, :] = near[near.shape[0] - rest.shape[0] + used :, :]


def matrix_of(proj, points, size):
    k = proj.shape[0]
    parts = []
    for a in range(LIGHT):
        values = proj[:, a * size : (a + 1) * size]
        cell = points[:, a * size : (a + 1) * size].astype(jnp.int32)
        low, lane = cell & 7, cell >> 3
        tall = jnp.concatenate([jnp.where(low == j, values, 0.0) for j in range(8)], axis=0).astype(BF16)
        hot = jnp.where(iota((128, size), 0) == lane, 1.0, 0.0).astype(BF16)
        sums = lax.dot_general(tall, hot, NT, preferred_element_type=F32)
        parts.append(jnp.concatenate([sums[j * k : (j + 1) * k, :] for j in range(8)], axis=1))
    return jnp.concatenate(parts, axis=0)


def matrices_kernel(*refs):
    bundles, out = refs[:-1], refs[-1]
    for number, bundle in enumerate(bundles):
        base = bundle.shape[0] - 16
        k, size = 8, bundle.shape[1] // LIGHT
        high, low = split(matrix_of(bundle[base : base + k, :], bundle[base + k : base + k + 1, :], size))
        span = LIGHT * k
        out[number, :span] = high
        out[number, span : 2 * span] = low
        out[number, 2 * span :] = high


def roll_lanes(value, shift):
    return pltpu.roll(value, shift % value.shape[1], 1)


def evolve_kernel(slabs, shared_heavy, *refs):
    own_pulse, other_pulse = refs[:2]
    bundles, ready = refs[2:14], refs[14:16]
    heavies = refs[16:17] if shared_heavy else refs[16:18]
    refs = refs[16 + len(heavies) :]
    outs, moment = refs[:4], refs[4]
    start, term1, term2, term3, start_split, split1, split2, total, light, full, pots, weights = refs[5:]
    y, quad, x, c = place()
    quads = slabs // GROUP
    part = start.shape[1] // 2
    cells = start.shape[2]
    k = 8
    size = cells // LIGHT
    base = 4 * part
    span = LIGHT * k
    edge = max(slabs // 8, 1)
    has_low, has_high = quad > 0, quad < quads - 1

    for number, bundle in enumerate(bundles):
        direction, xf, cf = number // 4, number // 2 % 2, number % 2
        slot = direction * GROUP + 2 * (x if xf == 0 else 1 - x) + (c if cf == 0 else 1 - c)
        rows = bundle[pl.ds(pl.multiple_of(c * 2 * part, 2 * part), 2 * part), :]
        start[slot] = rows
        high, low = split(rows)
        start_split[slot, : 2 * part] = high
        start_split[slot, 2 * part :] = low
        pots[slot] = bundle[base + k + 1 : base + k + 2, :]
        weights[slot] = bundle[base + k + 2 : base + k + 3, : 4 * span]

        if direction == 1:
            light[slot] = ready[0][2 * xf + cf]
        elif xf == 0:
            light[slot] = ready[1][direction + cf]
        else:

            @pl.when((has_low if direction == 0 else has_high) & (slot > 0) & (slot < SLOTS - 1))
            def _(bundle=bundle, slot=slot):
                high, low = split(matrix_of(bundle[base : base + k, :], bundle[base + k : base + k + 1, :], size))
                light[slot, :span] = high
                light[slot, span : 2 * span] = low
                light[slot, 2 * span :] = high

    def plane_of(slot):
        return quad * GROUP + slot - HALO

    def is_heavy(slot):
        plane = plane_of(slot)
        return (plane < edge) | (plane >= slabs - edge)

    extra = 3 * span

    def build_full(store, source):
        for group in range(3):
            high, low = split(matrix_of(source(group * k, k), source(3 * k + group, 1), size))
            for part_of, value in enumerate((high, low, high)):
                at = part_of * extra + group * span
                full[store, at : at + span] = value

    if shared_heavy:

        def store_of(slot):
            return slot - 1

        for slot in range(1, SLOTS - 1):
            exists = (plane_of(slot) >= 0) & (plane_of(slot) < slabs)

            @pl.when(exists & is_heavy(slot))
            def _(slot=slot):
                build_full(slot - 1, lambda at, n: heavies[0][slot - 1, at : at + n, :])
    else:
        ends = (quad == 0) | (quad == quads - 1)
        beside = (quad == 1) | (quad == quads - 2)
        low_end = quad <= 1
        first_slot = jnp.where(low_end, HALO, HALO + 2)

        def store_of(slot):
            return jnp.where(ends, slot - first_slot, 0)

        @pl.when(ends)
        def _():
            for cf in range(2):
                build_full(c if cf == 0 else 1 - c, lambda at, n, cf=cf: heavies[cf][at : at + n, :])

        @pl.when(beside)
        def _():
            mine = (c == 1) == low_end
            build_full(0, lambda at, n: jnp.where(mine, heavies[0][at : at + n, :], heavies[1][at : at + n, :]))

    for missing, slot in ((jnp.logical_not(has_low), HALO - 1), (jnp.logical_not(has_high), HALO + GROUP)):

        @pl.when(missing)
        def _(slot=slot):
            for term in (term1, term2, term3):
                term[slot] = jnp.zeros(term.shape[1:], F32)

    def coefficients(halves, matrix, weight, count, width, factor):
        r = lax.dot_general(halves, matrix, NT, preferred_element_type=F32)
        coeffs = r[:count, :width] + r[count:, :width] + r[:count, width:]
        sign = jnp.where(iota((count, width), 0) < count // 2, -factor, factor)
        high, low = split(coeffs * weight * sign)
        return jnp.concatenate([high, high, low], axis=1)

    lane = iota((1, 128), 1)
    groups_y = 4
    wrap_up, wrap_down = lane % groups_y == groups_y - 1, lane % groups_y == 0

    def columns(j):
        return slice(j * 128, (j + 1) * 128)

    def neighbours(field, slot, j, v):
        around = field[slot - 1, :, columns(j)] + field[slot + 1, :, columns(j)]
        around += roll_lanes(v, groups_y) + roll_lanes(v, -groups_y)
        w = field[slot, :, columns((j + 1) % 8)]
        around += w if j < 7 else jnp.where(wrap_up, roll_lanes(w, groups_y - 1), roll_lanes(w, -1))
        w = field[slot, :, columns((j - 1) % 8)]
        return around + (w if j > 0 else jnp.where(wrap_down, roll_lanes(w, 1 - groups_y), roll_lanes(w, 1)))

    def pulse_field(slot, p):
        strength = jnp.where(y == p, own_pulse[0], other_pulse[0])
        position = (plane_of(slot).astype(F32) + 0.5) / slabs
        return strength * 4.0 * (position - 0.5)

    def put(term, halves, slot, rows, cols, value):
        term[slot, rows, cols] = value
        high, low = split(value)
        halves[slot, rows, cols] = high
        halves[slot, slice(4 * part + rows.start, 4 * part + rows.stop), cols] = low

    def bounds(order):
        reach = TERMS - order
        low = jnp.where(has_low, HALO - reach, HALO)
        high = jnp.where(has_high, HALO + GROUP + reach, HALO + GROUP)
        return low, high

    def sweep(order, halves, count, apply, correct):
        factor = TIME_STEP / order
        low, high = bounds(order)

        def ahead(slot):
            return coefficients(
                halves[slot], light[slot, : 2 * span, :], weights[slot][:, :span], count, span, factor
            )

        def body(slot, wide):
            following = ahead(jnp.minimum(slot + 1, high - 1))
            apply(slot, lax.dot_general(wide, light[slot], NN, preferred_element_type=F32))

            @pl.when(is_heavy(slot))
            def _():
                store = store_of(slot)
                wide = coefficients(
                    halves[slot], full[store, : 2 * extra, :], weights[slot][:, span:], count, extra, factor
                )
                correct(slot, lax.dot_general(wide, full[store], NN, preferred_element_type=F32))

            return following

        lax.fori_loop(low, high, body, ahead(low))

    re, im = slice(0, 2 * part), slice(2 * part, 4 * part)

    def apply_first(slot, projected):
        fields = [pulse_field(slot, p) for p in range(2)]
        pot = pots[slot] + 3.0
        for j in range(8):
            cols = columns(j)
            v = start[slot, :, cols]
            around = neighbours(start, slot, j, v)
            sign = jnp.where(iota(v.shape, 0) < part, -TIME_STEP, TIME_STEP)
            image = sign * (pot[:, cols] * v - 0.5 * around) + projected[:, cols]
            turned = sign * v
            for p in range(2):
                value = image + fields[p] * turned
                put(term1, split1, slot, slice(p * part, (p + 1) * part), cols, value[part:])
                put(term1, split1, slot, slice((2 + p) * part, (3 + p) * part), cols, value[:part])

    def correct_first(slot, projected):
        for j in range(8):
            cols = columns(j)
            for p in range(2):
                for ri in range(2):
                    rows = slice((2 * ri + p) * part, (2 * ri + p + 1) * part)
                    more = projected[(1 - ri) * part : (2 - ri) * part, cols]
                    put(term1, split1, slot, rows, cols, term1[slot, rows, cols] + more)

    sweep(1, start_split, 2 * part, apply_first, correct_first)

    def image_of(order, source, slot, projected):
        factor = TIME_STEP / order
        fields = [pulse_field(slot, p) for p in range(2)]
        row = iota((4 * part, 128), 0)
        sign = jnp.where(row < 2 * part, -factor, factor)
        shift = sign * jnp.where(row // part % 2 == 0, 3.0 + fields[0], 3.0 + fields[1])
        half = -0.5 * sign
        for j in range(8):
            cols = columns(j)
            v = source[slot, :, cols]
            around = neighbours(source, slot, j, v)
            yield cols, (pots[slot][:, cols] * sign + shift) * v + half * around + projected[:, cols]

    def later(order, source, halves, target, target_split):
        def apply(slot, projected):
            for cols, image in image_of(order, source, slot, projected):
                put(target, target_split, slot, re, cols, image[im])
                put(target, target_split, slot, im, cols, image[re])

        def correct(slot, projected):
            for j in range(8):
                cols = columns(j)
                put(target, target_split, slot, re, cols, target[slot, re, cols] + projected[im, cols])
                put(target, target_split, slot, im, cols, target[slot, im, cols] + projected[re, cols])

        sweep(order, halves, 4 * part, apply, correct)

    later(2, term1, split1, term2, split2)
    later(3, term2, split2, term3, split1)

    def apply_last(slot, projected):
        at = slot - HALO
        for cols, image in image_of(TERMS, term3, slot, projected):
            terms = term1[slot, :, cols] + term2[slot, :, cols] + term3[slot, :, cols]
            for ri in range(2):
                begun = start[slot, ri * part : (ri + 1) * part, cols]
                for p in range(2):
                    rows = slice((2 * ri + p) * part, (2 * ri + p + 1) * part)
                    turned = slice((2 - 2 * ri + p) * part, (3 - 2 * ri + p) * part)
                    total[at, rows, cols] = begun + terms[rows] + image[turned]

    def correct_last(slot, projected):
        at = slot - HALO
        total[at, re] += projected[im]
        total[at, im] += projected[re]

    sweep(TERMS, split1, 4 * part, apply_last, correct_last)

    shares = jnp.zeros((4 * part, 128), F32)
    for slot in range(GROUP):
        position = (plane_of(slot + HALO).astype(F32) + 0.5) / slabs
        squares = jnp.zeros((4 * part, 128), F32)
        for j in range(8):
            v = total[slot, :, columns(j)]
            squares += v * v
        shares += position * squares
    for p in range(2):
        rows = slice(p * part, (p + 1) * part)
        value = jnp.sum(shares[rows] + shares[slice((2 + p) * part, (3 + p) * part)])
        moment[p : p + 1, :] = jnp.full((1, 128), value, F32)
    for number, out in enumerate(outs):
        yy = y if number // 2 == 0 else 1 - y
        xx = x if number % 2 == 0 else 1 - x
        for core in range(2):
            for ri in range(2):
                start_row = pl.multiple_of((2 * ri + yy) * part, part)
                at = (2 * core + ri) * part
                out[at : at + part, :] = total[2 * xx + core, pl.ds(start_row, part), :]


def unpack_kernel(*refs):
    pieces, out, rows, halves = refs[:8], refs[8], refs[9], refs[10:]
    y, _, x, c = place()
    cells, channels = out.shape
    half = channels // 2
    part = half // 8
    for number, piece in enumerate(pieces):
        yy = y if number // 4 == 0 else 1 - y
        xx = x if number // 2 % 2 == 0 else 1 - x
        cc = c if number % 2 == 0 else 1 - c
        at = pl.multiple_of((4 * yy + 2 * xx + cc) * part, part)
        for ri in range(2):
            start = pl.multiple_of((2 * c + ri) * part, part)
            rows[pl.ds(at + ri * half, part), :] = piece[pl.ds(start, part), :]
    lanes = cells // 8
    for j in range(8):
        for ri in range(2):
            block = rows[ri * half : (ri + 1) * half, j * lanes : (j + 1) * lanes].T
            halves[ri][pl.ds(j, lanes, stride=8), :] = block
    for ri in range(2):
        out[:, ri * half : (ri + 1) * half] = halves[ri][...]


VMEM = pl.BlockSpec(memory_space=pltpu.VMEM)
SMEM = pl.BlockSpec(memory_space=pltpu.SMEM)
BOTH = ("pulse", "grid")


def local(slabs, orbitals, potential, pulse, projectors, couplings, sphere_points, atom_count):
    _, nx, ny, channels = orbitals.shape
    cells = nx * ny
    atoms, k, size = projectors.shape
    part = channels // 16
    y, g = lax.axis_index("pulse"), lax.axis_index("grid")
    quads = slabs // GROUP
    quad = g // GROUP

    def permute(value, target):
        pairs = []
        for p in range(2):
            for s in range(slabs):
                to = target(p, s)
                if to is not None:
                    pairs.append((p * slabs + s, to[0] * slabs + to[1]))
        return lax.ppermute(value, BOTH, pairs)

    def swap_core(value):
        return permute(value, lambda p, s: (p, s ^ 1))

    def shift(value, by):
        return permute(value, lambda p, s: (p, s + by) if 0 <= s + by < slabs else None)

    bundle = jax.ShapeDtypeStruct((5 * channels // 16, cells), F32)
    near, far = pl.pallas_call(
        pack_kernel,
        out_shape=(bundle, bundle),
        in_specs=[VMEM] * 5 + [SMEM],
        out_specs=[VMEM] * 2,
        scratch_shapes=[pltpu.VMEM((cells, channels // 2), F32), pltpu.VMEM((channels // 2, cells), F32)],
        name="pack",
    )(orbitals.reshape(cells, channels), potential.reshape(nx, ny), projectors, couplings.T, sphere_points, atom_count)
    beside = permute(far, lambda p, s: (p, s ^ 2))
    below1, above1 = shift(near, GROUP), shift(near, -GROUP)
    heavy = pl.pallas_call(
        rest_kernel,
        out_shape=jax.ShapeDtypeStruct((32, cells), F32),
        in_specs=[VMEM] * 3,
        out_specs=VMEM,
        name="rest",
    )(projectors, sphere_points, near)
    pulse_sent, heavy = lax.optimization_barrier((pulse, heavy))
    below2, above2 = shift(beside, GROUP), shift(beside, -GROUP)
    other_pulse = permute(pulse_sent, lambda p, s: (1 - p, s))
    order = []
    for piece in (below1, below2, near, beside, above1, above2):
        order += [piece, swap_core(piece)]

    def matrices(bundles):
        return pl.pallas_call(
            matrices_kernel,
            out_shape=jax.ShapeDtypeStruct((len(bundles), 3 * LIGHT * k, cells), BF16),
            in_specs=[VMEM] * len(bundles),
            out_specs=VMEM,
            name="matrices",
        )(*bundles)

    ready = [matrices(order[4:8]), matrices(order[:2] + order[8:10])]

    edge = max(slabs // 8, 1)
    shared_heavy = not (edge == 2 and quads >= 4)
    if shared_heavy:
        everywhere = lax.all_gather(heavy, "grid")
        blank = jnp.zeros((HALO - 1,) + heavy.shape, F32)
        padded = jnp.concatenate([blank, everywhere, blank])
        heavies = [lax.dynamic_slice_in_dim(padded, quad * GROUP, SLOTS - 2)]
        stores = SLOTS - 2
    else:
        crowded = (0, 1, slabs - 2, slabs - 1)
        across = permute(heavy, lambda p, s: (p, s ^ 2) if s in crowded else None)
        x = (g // 2) % 2
        own = ((quad == 0) & (x == 0)) | ((quad == quads - 1) & (x == 1))
        held = jnp.where(own, heavy, across)

        def outward(p, s):
            if s // GROUP == 0 and s % 2 == 1:
                return p, s + GROUP
            if s // GROUP == quads - 1 and s % 2 == 0:
                return p, s - GROUP
            return None

        moved = permute(held, outward)
        held = jnp.where((quad == 0) | (quad == quads - 1), held, moved)
        heavies = [held, swap_core(held)]
        stores = 2

    wide = 3 * (atoms - LIGHT) * k
    outs = pl.pallas_call(
        functools.partial(evolve_kernel, slabs, shared_heavy),
        out_shape=[jax.ShapeDtypeStruct((4 * part, cells), F32)] * 4 + [jax.ShapeDtypeStruct((2, 128), F32)],
        in_specs=[SMEM] * 2 + [VMEM] * (14 + len(heavies)),
        out_specs=[VMEM] * 5,
        scratch_shapes=[pltpu.VMEM((SLOTS, 2 * part, cells), F32)]
        + [pltpu.VMEM((SLOTS, 4 * part, cells), F32)] * 3
        + [pltpu.VMEM((SLOTS, 4 * part, cells), BF16)]
        + [pltpu.VMEM((SLOTS, 8 * part, cells), BF16)] * 2
        + [
            pltpu.VMEM((GROUP, 4 * part, cells), F32),
            pltpu.VMEM((SLOTS, 3 * LIGHT * k, cells), BF16),
            pltpu.VMEM((stores, wide, cells), BF16),
            pltpu.VMEM((SLOTS, 1, cells), F32),
            pltpu.VMEM((SLOTS, 1, 128), F32),
        ],
        compiler_params=pltpu.CompilerParams(vmem_limit_bytes=(36 if not shared_heavy else 50) * 2**20),
        name="evolve",
    )(pulse, other_pulse, *order, *ready, *heavies)
    moment = outs[4]
    finals = [
        outs[0],
        permute(outs[1], lambda p, s: (p, s ^ 2)),
        permute(outs[2], lambda p, s: (1 - p, s)),
        permute(outs[3], lambda p, s: (1 - p, s ^ 2)),
    ]
    devices = 2 * slabs
    shares = jnp.broadcast_to(jnp.concatenate([moment[0], moment[1]])[None, None, :], (devices, 1, 256))
    shares = lax.all_to_all(shares, BOTH, 0, 0)
    *finals, shares = lax.optimization_barrier((*finals, shares))
    pieces = []
    for piece in finals:
        pieces += [piece, swap_core(piece)]
    plane = pl.pallas_call(
        unpack_kernel,
        out_shape=jax.ShapeDtypeStruct((cells, channels), F32),
        in_specs=[VMEM] * 8,
        out_specs=VMEM,
        scratch_shapes=[pltpu.VMEM((channels, cells), F32)] + [pltpu.VMEM((cells, channels // 2), F32)] * 2,
        compiler_params=pltpu.CompilerParams(vmem_limit_bytes=16 * 2**20),
        name="unpack",
    )(*pieces)

    total = jnp.where(y == 0, jnp.sum(shares[:, 0, 0]), jnp.sum(shares[:, 0, 128]))
    dipole = total / (slabs * cells * (channels // 2))
    return plane.reshape(orbitals.shape), dipole.reshape(1)


def solution(mesh):
    placed = (
        P("grid", None, None, None),
        P("grid", None, None),
        P("pulse"),
        P("grid", None, None),
        P("grid", None),
        P("grid", None),
        P("grid"),
    )
    return jax.shard_map(
        functools.partial(local, mesh.shape["grid"]),
        mesh=mesh,
        in_specs=placed,
        out_specs=(P(("pulse", "grid"), None, None, None), P("pulse")),
        check_vma=False,
    )
```

time: 111 us -> 85.2 us (0.77)
  waiting for transfers between devices: 24.3 us -> 0.78 us
  starting transfers between devices: 43.3 us -> 29.9 us
  blocking collectives: 0 us -> 12.7 us
  Pallas kernels: 34.3 us -> 31.1 us
    ppermute x27 -> x22, waiting for transfers between devices: 24.3 us -> 0.78 us  [permute(): return lax.ppermute(value, BOTH, pairs)]
    ppermute x27 -> x22, starting transfers between devices: 43.3 us -> 29.9 us  [permute(): return lax.ppermute(value, BOTH, pairs)]
    all_to_all x0 -> x1, blocking collectives: none -> 12.7 us  [local(): shares = lax.all_to_all(shares, BOTH, 0, 0)]
    pallas_call x1, Pallas kernels: 28.6 us -> 19.9 us  [local(): pl.pallas_call(functools.partial(evolve_kernel, slabs, shared_heavy), out...]
    pallas_call x1 -> x4, Pallas kernels: 2.72 us -> 9.71 us  [the longest x2 5.36 us: matrices(): pl.pallas_call(matrices_kernel, out_shape=jax.ShapeDtypeStruct((len(bundl...]
    pallas_call x1, Pallas kernels: 2.99 us -> 1.51 us  [local(): pl.pallas_call(unpack_kernel, out_shape=jax.ShapeDtypeStruct((cells, chan...]
    unnamed x27 -> x28, local copies, waits for them, and re-layouts: 2.87 us -> 3.83 us
  transfers between devices with their start and end apart: 27 -> 22, of which waited for: 11 -> 3; matrix products, arithmetic and copies ran while one was open for 1% -> 2% of each run, Pallas kernels for 0% -> 8%
where the time goes in v2:
time: 85.2 us; the launch traced here: 84.6 us
  Pallas kernels  31.1 us (37%)
  starting transfers between devices  29.9 us (35%)
  blocking collectives  12.7 us (15%)
  between operations  4.7 us (6%)
  local copies, waits for them, and re-layouts  3.85 us (5%)
  other arithmetic  1.61 us (2%)
    ppermute x22, starting transfers between devices, permute(): return lax.ppermute(value, BOTH, pairs)  29.9 us
    pallas_call x1, Pallas kernels, local(): pl.pallas_call(functools.partial(evolve_kernel, slabs, shared_heavy), out...  19.9 us
    all_to_all x1, blocking collectives, local(): shares = lax.all_to_all(shares, BOTH, 0, 0)  12.7 us
    pallas_call x2, Pallas kernels, matrices(): pl.pallas_call(matrices_kernel, out_shape=jax.ShapeDtypeStruct((len(bundl...  5.36 us
    unnamed x28, local copies, waits for them, and re-layouts  3.83 us
    pallas_call x1, Pallas kernels, local(): pl.pallas_call(pack_kernel, out_shape=(bundle, bundle), in_specs=[VMEM] *...  2.67 us
  transfers between devices with their start and end apart: 22, of which 3 were waited for; matrix products, arithmetic and copies ran while one was open for 2% of the time, Pallas kernels for 8%

profile of v2, /device:TPU:0, one launch (start us, length us, event | category | flops | bytes accessed | tf_op | source)
XLA Modules:
  0.0 84.6 jit_solution(10497776230530527579)
XLA Ops:
  1.3 2.7 %pack.1 = (f32[80,1024]{1,0:T(8,128)}, f32[80,1024]{1,0:T(8,128)}) custom-call(f32[1024,256]{1,0:T(8,128)} %bitcast.10, f32[32,32]{1,0:T(8,128)} %bitcast.11, bf16[16,8,256]{2,1,0:T(8,128)(2,1)} %proj.3, f32[8,16]{1,0:T(8,128)} %bitcast.12, s32[16,256]{1,0:T(8,128)} %points.3, s32[1]{0:T(128)S(6)} %copy.14.count), custom_call_target="tpu_custom_call" | custom-call | tf_op jit(solution)/shard_map/pack/pallas_call | solution.py:436
  3.9 2.9 %collective-permute-start.3 = (f32[80,1024]{1,0:T(8,128)}, f32[80,1024]{1,0:T(8,128)}, u32[]{:S(2)}, u32[]{:S(2)}) collective-permute-start(f32[80,1024]{1,0:T(8,128)} %get-tuple-element.18), channel_id=1, source_target_pairs={{0,2},{1,3},{2,0},{3,1},{4,6},{5,7},{6,4},{7,5},{8,10},{9,11},{10,... | collective-permute-start | bytes 983048 | tf_op jit(solution)/shard_map/ppermute | solution.py:427
  6.9 1.3 %collective-permute-start.8 = (f32[80,1024]{1,0:T(8,128)}, f32[80,1024]{1,0:T(8,128)S(1)}, u32[]{:S(2)}, u32[]{:S(2)}) collective-permute-start(f32[80,1024]{1,0:T(8,128)} %get-tuple-element.16.near.refs_0_.refs_6_), channel_id=1, source_target_pairs={{4,0},{5,1},{6,2},{7,3},{8,4},{9,5},{10,6},{11,7},{12,8},{13,9},{1... | collective-permute-start | bytes 983048 | tf_op jit(solution)/shard_map/ppermute | solution.py:427
  8.2 1.7 %rest.1 = f32[32,1024]{1,0:T(8,128)} custom-call(bf16[16,8,256]{2,1,0:T(8,128)(2,1)} %proj.3, s32[16,256]{1,0:T(8,128)} %points.3, f32[80,1024]{1,0:T(8,128)} %get-tuple-element.16.near.refs_0_.refs_6_), custom_call_target="tpu_custom_call" | custom-call | tf_op jit(solution)/shard_map/rest/pallas_call | solution.py:446
  9.9 1.9 %collective-permute-start.12 = (f32[32,1024]{1,0:T(8,128)}, f32[32,1024]{1,0:T(8,128)S(1)}, u32[]{:S(2)}, u32[]{:S(2)}) collective-permute-start(f32[32,1024]{1,0:T(8,128)} %rest.1), channel_id=1, source_target_pairs={{0,2},{1,3},{14,12},{15,13},{16,18},{17,19},{30,28},{31,29}} | collective-permute-start | bytes 393224 | tf_op jit(solution)/shard_map/ppermute | solution.py:427
  11.8 3.3 %collective-permute-start.1 = (f32[80,1024]{1,0:T(8,128)}, f32[80,1024]{1,0:T(8,128)S(1)}, u32[]{:S(2)}, u32[]{:S(2)}) collective-permute-start(f32[80,1024]{1,0:T(8,128)} %get-tuple-element.16.near.refs_0_.refs_6_), channel_id=1, source_target_pairs={{0,4},{1,5},{2,6},{3,7},{4,8},{5,9},{6,10},{7,11},{8,12},{9,13},{1... | collective-permute-start | bytes 983048 | tf_op jit(solution)/shard_map/ppermute | solution.py:427
  15.1 0.2 collective-permute-done.3.refs_2_.refs_8_
  15.3 1.3 %collective-permute-start.10 = (f32[80,1024]{1,0:T(8,128)}, f32[80,1024]{1,0:T(8,128)S(1)}, u32[]{:S(2)}, u32[]{:S(2)}) collective-permute-start(f32[80,1024]{1,0:T(8,128)} %collective-permute-done.3.refs_2_.refs_8_), channel_id=1, source_target_pairs={{4,0},{5,1},{6,2},{7,3},{8,4},{9,5},{10,6},{11,7},{12,8},{13,9},{1... | collective-permute-start | bytes 983048 | tf_op jit(solution)/shard_map/ppermute | solution.py:427
  16.6 4.6 %collective-permute-start.4 = (f32[80,1024]{1,0:T(8,128)}, f32[80,1024]{1,0:T(8,128)S(1)}, u32[]{:S(2)}, u32[]{:S(2)}) collective-permute-start(f32[80,1024]{1,0:T(8,128)} %collective-permute-done.3.refs_2_.refs_8_), channel_id=1, source_target_pairs={{0,4},{1,5},{2,6},{3,7},{4,8},{5,9},{6,10},{7,11},{8,12},{9,13},{1... | collective-permute-start | bytes 983048 | tf_op jit(solution)/shard_map/ppermute | solution.py:427
  21.2 0.0 collective-permute-done.8.refs_2_.refs_10_
  21.2 0.1 collective-permute-start.9
  21.3 0.0 collective-permute-done.12
  21.3 1.0 %broadcast_select_fusion = f32[32,1024]{1,0:T(8,128)S(1)} fusion(f32[32,1024]{1,0:T(8,128)} %rest.1, f32[32,1024]{1,0:T(8,128)S(1)} %collective-permute-done.12, pred[]{:T(512)S(6)} %or.7), kind=kLoop, calls=%fused_computation | loop fusion | flops 32768 | bytes 393217 | tf_op jit(solution)/shard_map/jit(_where)/select_n | solution.py:484
  22.2 0.7 collective-permute-start.13
  22.9 0.4 collective-permute-done.1.refs_0_.refs_2_
  23.3 1.8 %collective-permute-start.2 = (f32[80,1024]{1,0:T(8,128)S(1)}, f32[80,1024]{1,0:T(8,128)S(1)}, u32[]{:S(2)}, u32[]{:S(2)}) collective-permute-start(f32[80,1024]{1,0:T(8,128)S(1)} %collective-permute-done.1.refs_0_.refs_2_), channel_id=1, source_target_pairs={{0,1},{1,0},{2,3},{3,2},{4,5},{5,4},{6,7},{7,6},{8,9},{9,8},{10,11... | collective-permute-start | bytes 983048 | tf_op jit(solution)/shard_map/ppermute | solution.py:427
  25.1 0.0 collective-permute-done.13
  25.1 4.9 %collective-permute-start.6 = (f32[80,1024]{1,0:T(8,128)}, f32[80,1024]{1,0:T(8,128)S(1)}, u32[]{:S(2)}, u32[]{:S(2)}) collective-permute-start(f32[80,1024]{1,0:T(8,128)} %get-tuple-element.16.near.refs_0_.refs_6_), channel_id=1, source_target_pairs={{0,1},{1,0},{2,3},{3,2},{4,5},{5,4},{6,7},{7,6},{8,9},{9,8},{10,11... | collective-permute-start | bytes 983048 | tf_op jit(solution)/shard_map/ppermute | solution.py:427
  30.1 0.0 collective-permute-done.10.refs_12_
  30.1 0.0 collective-permute-start.7
  30.1 0.1 collective-permute-done.4.refs_4_
  30.2 0.4 collective-permute-start.11
  30.6 0.0 collective-permute-done.9.refs_3_.refs_11_
  30.6 0.1 collective-permute-start.5
  30.8 0.0 collective-permute-done.2.refs_1_.refs_3_
  30.8 0.4 collective-permute-start.14
  31.9 2.7 %matrices.3.refs_15_ = bf16[4,96,1024]{2,1,0:T(8,128)(2,1)} custom-call(f32[80,1024]{1,0:T(8,128)} %copy-done.4, f32[80,1024]{1,0:T(8,128)} %copy-done.8, f32[80,1024]{1,0:T(8,128)} %copy-done.2, f32[80,1024]{1,0:T(8,128)} %copy-done.6), custom_call_target="tpu_custom_call" | custom-call | tf_op jit(solution)/shard_map/matrices/pallas_call | solution.py:461
  34.6 1.6 %collective-permute-start = (f32[1]{0:T(128)}, f32[1]{0:T(128)}, u32[]{:S(2)}, u32[]{:S(2)}) collective-permute-start(f32[1]{0:T(128)} %param.9), channel_id=1, source_target_pairs={{0,16},{1,17},{2,18},{3,19},{4,20},{5,21},{6,22},{7,23},{8,24},{9,... | collective-permute-start | bytes 20 | tf_op jit(solution)/shard_map/ppermute | solution.py:427
  36.2 0.0 collective-permute-done.7.refs_3_.refs_9_
  36.2 0.7 copy-done.12
  36.9 2.7 %matrices.2.refs_14_ = bf16[4,96,1024]{2,1,0:T(8,128)(2,1)} custom-call(f32[80,1024]{1,0:T(8,128)} %get-tuple-element.16.near.refs_0_.refs_6_, f32[80,1024]{1,0:T(8,128)} %copy-done.10, f32[80,1024]{1,0:T(8,128)} %collective-permute-done.3.refs_2_.refs_8_, f32[80,1024]{1,0:T(8,128)} %copy-done.12), custom_call_target="tpu_custom_call" | custom-call | tf_op jit(solution)/shard_map/matrices/pallas_call | solution.py:461
  39.6 0.0 collective-permute-done.refs_1_
  39.6 0.0 collective-permute-done.14.refs_17_
  39.7 0.0 copy-start.1
  39.7 1.1 %copy-done.1 = bf16[4,96,1024]{2,1,0:T(8,128)(2,1)S(1)} copy-done((bf16[4,96,1024]{2,1,0:T(8,128)(2,1)S(1)}, bf16[4,96,1024]{2,1,0:T(8,128)(2,1)}, u32[]{:S(2)}) %copy-start.1) | copy-done | bytes 786456
  40.8 1.0 %copy-done.11 = f32[80,1024]{1,0:T(8,128)S(1)} copy-done((f32[80,1024]{1,0:T(8,128)S(1)}, f32[80,1024]{1,0:T(8,128)}, u32[]{:S(2)}) %copy-start.11) | copy-done | bytes 327704
  41.8 1.0 %copy-done.13 = f32[80,1024]{1,0:T(8,128)S(1)} copy-done((f32[80,1024]{1,0:T(8,128)S(1)}, f32[80,1024]{1,0:T(8,128)}, u32[]{:S(2)}) %copy-start.13) | copy-done | bytes 327704
  42.7 19.9 %evolve.1 = (f32[64,1024]{1,0:T(8,128)S(1)}, f32[64,1024]{1,0:T(8,128)S(1)}, f32[64,1024]{1,0:T(8,128)S(1)}, f32[64,1024]{1,0:T(8,128)S(1)}, f32[2,128]{1,0:T(2,128)S(1)}) custom-call(f32[1]{0:T(128)S(6)} %copy.13.refs_0_, f32[1]{0:T(128)} %collective-permute-done.refs_1_, f32[80,1024]{1,0:T(8,128)S(1)} %copy-done.5, f32[80,1024]{1,0:T(8,128)S(1)} %copy-done.9, ...), custom_call_target="tpu_custom_call" | custom-call | tf_op jit(solution)/shard_map/evolve/pallas_call | solution.py:499
  62.7 1.0 %collective-permute-start.15 = (f32[64,1024]{1,0:T(8,128)S(1)}, f32[64,1024]{1,0:T(8,128)S(1)}, u32[]{:S(2)}, u32[]{:S(2)}) collective-permute-start(f32[64,1024]{1,0:T(8,128)S(1)} %get-tuple-element.21), channel_id=1, source_target_pairs={{0,2},{1,3},{2,0},{3,1},{4,6},{5,7},{6,4},{7,5},{8,10},{9,11},{10,... | collective-permute-start | bytes 786440 | tf_op jit(solution)/shard_map/ppermute | solution.py:427
  63.7 0.6 collective-permute-start.16
  64.3 1.9 %collective-permute-start.17 = (f32[64,1024]{1,0:T(8,128)S(1)}, f32[64,1024]{1,0:T(8,128)S(1)}, u32[]{:S(2)}, u32[]{:S(2)}) collective-permute-start(f32[64,1024]{1,0:T(8,128)S(1)} %get-tuple-element.23), channel_id=1, source_target_pairs={{0,18},{1,19},{2,16},{3,17},{4,22},{5,23},{6,20},{7,21},{8,26},{9,... | collective-permute-start | bytes 786440 | tf_op jit(solution)/shard_map/ppermute | solution.py:427
  66.3 12.7 %all_to_all.5 = f32[32,1,256]{2,1,0:T(1,128)S(1)} all-to-all(f32[32,1,256]{2,1,0:T(1,128)S(1)} %broadcast_in_dim.2), channel_id=1, replica_groups=mesh['pulse'=2,'grid'=16] {'pulse','grid'}, dimensions={0} | all-to-all | bytes 65536 | tf_op jit(solution)/shard_map/all_to_all | solution.py:527
  78.9 0.2 collective-permute-start.18
  79.1 0.4 collective-permute-start.19
  79.5 0.1 collective-permute-start.20
  79.6 0.4 collective-permute-start.21
  80.0 0.6 slice_reduce_fusion
  82.0 1.5 %unpack.1 = f32[1024,256]{1,0:T(8,128)} custom-call(f32[64,1024]{1,0:T(8,128)S(1)} %get-tuple-element.25.refs_0_, f32[64,1024]{1,0:T(8,128)S(1)} %collective-permute-done.18.refs_1_, f32[64,1024]{1,0:T(8,128)S(1)} %collective-permute-done.15.refs_2_, f32[64,1024]{1,0:T(8,128)S(1)} %collective-permute-done.19.refs_3_, ...), custom_call_target="tpu_custom_call" | custom-call | tf_op jit(solution)/shard_map/unpack/pallas_call | solution.py:532
  (37 shorter events, 0.1 us)
Async XLA Ops:
  3.9 11.4 %collective-permute-start.3 = (f32[80,1024]{1,0:T(8,128)}, f32[80,1024]{1,0:T(8,128)}, u32[]{:S(2)}, u32[]{:S(2)}) collective-permute-start(f32[80,1024]{1,0:T(8,128)} %get-tuple-element.18), channel_id=1, source_target_pairs={{0,2},{1,3},{2,0},{3,1},{4,6},{5,7},{6,4},{7,5},{8,10},{9,11},{10,... | collective-permute-start | bytes 983048 | tf_op jit(solution)/shard_map/ppermute | solution.py:427
  6.9 14.3 %collective-permute-start.8 = (f32[80,1024]{1,0:T(8,128)}, f32[80,1024]{1,0:T(8,128)S(1)}, u32[]{:S(2)}, u32[]{:S(2)}) collective-permute-start(f32[80,1024]{1,0:T(8,128)} %get-tuple-element.16.near.refs_0_.refs_6_), channel_id=1, source_target_pairs={{4,0},{5,1},{6,2},{7,3},{8,4},{9,5},{10,6},{11,7},{12,8},{13,9},{1... | collective-permute-start | bytes 983048 | tf_op jit(solution)/shard_map/ppermute | solution.py:427
  9.9 11.4 %collective-permute-start.12 = (f32[32,1024]{1,0:T(8,128)}, f32[32,1024]{1,0:T(8,128)S(1)}, u32[]{:S(2)}, u32[]{:S(2)}) collective-permute-start(f32[32,1024]{1,0:T(8,128)} %rest.1), channel_id=1, source_target_pairs={{0,2},{1,3},{14,12},{15,13},{16,18},{17,19},{30,28},{31,29}} | collective-permute-start | bytes 393224 | tf_op jit(solution)/shard_map/ppermute | solution.py:427
  11.8 11.6 %collective-permute-start.1 = (f32[80,1024]{1,0:T(8,128)}, f32[80,1024]{1,0:T(8,128)S(1)}, u32[]{:S(2)}, u32[]{:S(2)}) collective-permute-start(f32[80,1024]{1,0:T(8,128)} %get-tuple-element.16.near.refs_0_.refs_6_), channel_id=1, source_target_pairs={{0,4},{1,5},{2,6},{3,7},{4,8},{5,9},{6,10},{7,11},{8,12},{9,13},{1... | collective-permute-start | bytes 983048 | tf_op jit(solution)/shard_map/ppermute | solution.py:427
  15.3 14.7 %collective-permute-start.10 = (f32[80,1024]{1,0:T(8,128)}, f32[80,1024]{1,0:T(8,128)S(1)}, u32[]{:S(2)}, u32[]{:S(2)}) collective-permute-start(f32[80,1024]{1,0:T(8,128)} %collective-permute-done.3.refs_2_.refs_8_), channel_id=1, source_target_pairs={{4,0},{5,1},{6,2},{7,3},{8,4},{9,5},{10,6},{11,7},{12,8},{13,9},{1... | collective-permute-start | bytes 983048 | tf_op jit(solution)/shard_map/ppermute | solution.py:427
  16.6 13.6 %collective-permute-start.4 = (f32[80,1024]{1,0:T(8,128)}, f32[80,1024]{1,0:T(8,128)S(1)}, u32[]{:S(2)}, u32[]{:S(2)}) collective-permute-start(f32[80,1024]{1,0:T(8,128)} %collective-permute-done.3.refs_2_.refs_8_), channel_id=1, source_target_pairs={{0,4},{1,5},{2,6},{3,7},{4,8},{5,9},{6,10},{7,11},{8,12},{9,13},{1... | collective-permute-start | bytes 983048 | tf_op jit(solution)/shard_map/ppermute | solution.py:427
  21.2 9.6 %copy-start.2 = (f32[80,1024]{1,0:T(8,128)}, f32[80,1024]{1,0:T(8,128)S(1)}, u32[]{:S(2)}) copy-start(f32[80,1024]{1,0:T(8,128)S(1)} %collective-permute-done.8.refs_2_.refs_10_) | copy-start | bytes 983044
  21.2 9.4 %collective-permute-start.9 = (f32[80,1024]{1,0:T(8,128)S(1)}, f32[80,1024]{1,0:T(8,128)S(1)}, u32[]{:S(2)}, u32[]{:S(2)}) collective-permute-start(f32[80,1024]{1,0:T(8,128)S(1)} %collective-permute-done.8.refs_2_.refs_10_), channel_id=1, source_target_pairs={{0,1},{1,0},{2,3},{3,2},{4,5},{5,4},{6,7},{7,6},{8,9},{9,8},{10,11... | collective-permute-start | bytes 983048 | tf_op jit(solution)/shard_map/ppermute | solution.py:427
  22.2 2.9 %collective-permute-start.13 = (f32[32,1024]{1,0:T(8,128)S(1)}, f32[32,1024]{1,0:T(8,128)S(1)}, u32[]{:S(2)}, u32[]{:S(2)}) collective-permute-start(f32[32,1024]{1,0:T(8,128)S(1)} %broadcast_select_fusion), channel_id=1, source_target_pairs={{1,5},{3,7},{12,8},{14,10},{17,21},{19,23},{28,24},{30,26}} | collective-permute-start | bytes 393224 | tf_op jit(solution)/shard_map/ppermute | solution.py:427
  23.3 8.5 %copy-start.4 = (f32[80,1024]{1,0:T(8,128)}, f32[80,1024]{1,0:T(8,128)S(1)}, u32[]{:S(2)}) copy-start(f32[80,1024]{1,0:T(8,128)S(1)} %collective-permute-done.1.refs_0_.refs_2_) | copy-start | bytes 983044
  23.3 7.4 %collective-permute-start.2 = (f32[80,1024]{1,0:T(8,128)S(1)}, f32[80,1024]{1,0:T(8,128)S(1)}, u32[]{:S(2)}, u32[]{:S(2)}) collective-permute-start(f32[80,1024]{1,0:T(8,128)S(1)} %collective-permute-done.1.refs_0_.refs_2_), channel_id=1, source_target_pairs={{0,1},{1,0},{2,3},{3,2},{4,5},{5,4},{6,7},{7,6},{8,9},{9,8},{10,11... | collective-permute-start | bytes 983048 | tf_op jit(solution)/shard_map/ppermute | solution.py:427
  25.1 9.5 %collective-permute-start.6 = (f32[80,1024]{1,0:T(8,128)}, f32[80,1024]{1,0:T(8,128)S(1)}, u32[]{:S(2)}, u32[]{:S(2)}) collective-permute-start(f32[80,1024]{1,0:T(8,128)} %get-tuple-element.16.near.refs_0_.refs_6_), channel_id=1, source_target_pairs={{0,1},{1,0},{2,3},{3,2},{4,5},{5,4},{6,7},{7,6},{8,9},{9,8},{10,11... | collective-permute-start | bytes 983048 | tf_op jit(solution)/shard_map/ppermute | solution.py:427
  30.1 6.1 %collective-permute-start.7 = (f32[80,1024]{1,0:T(8,128)}, f32[80,1024]{1,0:T(8,128)S(1)}, u32[]{:S(2)}, u32[]{:S(2)}) collective-permute-start(f32[80,1024]{1,0:T(8,128)} %collective-permute-done.3.refs_2_.refs_8_), channel_id=1, source_target_pairs={{0,1},{1,0},{2,3},{3,2},{4,5},{5,4},{6,7},{7,6},{8,9},{9,8},{10,11... | collective-permute-start | bytes 983048 | tf_op jit(solution)/shard_map/ppermute | solution.py:427
  30.2 9.4 %collective-permute-start.11 = (f32[80,1024]{1,0:T(8,128)S(1)}, f32[80,1024]{1,0:T(8,128)}, u32[]{:S(2)}, u32[]{:S(2)}) collective-permute-start(f32[80,1024]{1,0:T(8,128)S(1)} %collective-permute-done.10.refs_12_), channel_id=1, source_target_pairs={{0,1},{1,0},{2,3},{3,2},{4,5},{5,4},{6,7},{7,6},{8,9},{9,8},{10,11... | collective-permute-start | bytes 983048 | tf_op jit(solution)/shard_map/ppermute | solution.py:427
  30.6 1.3 %copy-start.6 = (f32[80,1024]{1,0:T(8,128)}, f32[80,1024]{1,0:T(8,128)S(1)}, u32[]{:S(2)}) copy-start(f32[80,1024]{1,0:T(8,128)S(1)} %collective-permute-done.9.refs_3_.refs_11_) | copy-start | bytes 983044
  30.6 9.0 %collective-permute-start.5 = (f32[80,1024]{1,0:T(8,128)S(1)}, f32[80,1024]{1,0:T(8,128)}, u32[]{:S(2)}, u32[]{:S(2)}) collective-permute-start(f32[80,1024]{1,0:T(8,128)S(1)} %collective-permute-done.4.refs_4_), channel_id=1, source_target_pairs={{0,1},{1,0},{2,3},{3,2},{4,5},{5,4},{6,7},{7,6},{8,9},{9,8},{10,11... | collective-permute-start | bytes 983048 | tf_op jit(solution)/shard_map/ppermute | solution.py:427
  30.8 1.1 %copy-start.8 = (f32[80,1024]{1,0:T(8,128)}, f32[80,1024]{1,0:T(8,128)S(1)}, u32[]{:S(2)}) copy-start(f32[80,1024]{1,0:T(8,128)S(1)} %collective-permute-done.2.refs_1_.refs_3_) | copy-start | bytes 983044
  30.8 8.8 %collective-permute-start.14 = (f32[32,1024]{1,0:T(8,128)S(1)}, f32[32,1024]{1,0:T(8,128)}, u32[]{:S(2)}, u32[]{:S(2)}) collective-permute-start(f32[32,1024]{1,0:T(8,128)S(1)} %broadcast_select_fusion.1.refs_16_), channel_id=1, source_target_pairs={{0,1},{1,0},{2,3},{3,2},{4,5},{5,4},{6,7},{7,6},{8,9},{9,8},{10,11... | collective-permute-start | bytes 393224 | tf_op jit(solution)/shard_map/ppermute | solution.py:427
  34.6 5.0 %copy-start = (bf16[4,96,1024]{2,1,0:T(8,128)(2,1)S(1)}, bf16[4,96,1024]{2,1,0:T(8,128)(2,1)}, u32[]{:S(2)}) copy-start(bf16[4,96,1024]{2,1,0:T(8,128)(2,1)} %matrices.3.refs_15_) | copy-start | bytes 2359300
  34.6 5.0 %copy-start.3 = (f32[80,1024]{1,0:T(8,128)S(1)}, f32[80,1024]{1,0:T(8,128)}, u32[]{:S(2)}) copy-start(f32[80,1024]{1,0:T(8,128)} %copy-done.2) | copy-start | bytes 983044
  34.6 5.0 %copy-start.5 = (f32[80,1024]{1,0:T(8,128)S(1)}, f32[80,1024]{1,0:T(8,128)}, u32[]{:S(2)}) copy-start(f32[80,1024]{1,0:T(8,128)} %copy-done.4) | copy-start | bytes 983044
  34.6 5.1 %copy-start.7 = (f32[80,1024]{1,0:T(8,128)S(1)}, f32[80,1024]{1,0:T(8,128)}, u32[]{:S(2)}) copy-start(f32[80,1024]{1,0:T(8,128)} %copy-done.6) | copy-start | bytes 983044
  34.6 5.1 %copy-start.9 = (f32[80,1024]{1,0:T(8,128)S(1)}, f32[80,1024]{1,0:T(8,128)}, u32[]{:S(2)}) copy-start(f32[80,1024]{1,0:T(8,128)} %copy-done.8) | copy-start | bytes 983044
  34.6 1.6 %copy-start.10 = (f32[80,1024]{1,0:T(8,128)}, f32[80,1024]{1,0:T(8,128)S(1)}, u32[]{:S(2)}) copy-start(f32[80,1024]{1,0:T(8,128)S(1)} %collective-permute-done.6.refs_1_.refs_7_) | copy-start | bytes 983044
  34.6 5.0 %collective-permute-start = (f32[1]{0:T(128)}, f32[1]{0:T(128)}, u32[]{:S(2)}, u32[]{:S(2)}) collective-permute-start(f32[1]{0:T(128)} %param.9), channel_id=1, source_target_pairs={{0,16},{1,17},{2,18},{3,19},{4,20},{5,21},{6,22},{7,23},{8,24},{9,... | collective-permute-start | bytes 20 | tf_op jit(solution)/shard_map/ppermute | solution.py:427
  36.2 0.7 copy-start.12
  39.7 1.1 %copy-start.1 = (bf16[4,96,1024]{2,1,0:T(8,128)(2,1)S(1)}, bf16[4,96,1024]{2,1,0:T(8,128)(2,1)}, u32[]{:S(2)}) copy-start(bf16[4,96,1024]{2,1,0:T(8,128)(2,1)} %matrices.2.refs_14_) | copy-start | bytes 2359300
  40.8 1.0 %copy-start.11 = (f32[80,1024]{1,0:T(8,128)S(1)}, f32[80,1024]{1,0:T(8,128)}, u32[]{:S(2)}) copy-start(f32[80,1024]{1,0:T(8,128)} %copy-done.10) | copy-start | bytes 983044
  41.8 1.0 %copy-start.13 = (f32[80,1024]{1,0:T(8,128)S(1)}, f32[80,1024]{1,0:T(8,128)}, u32[]{:S(2)}) copy-start(f32[80,1024]{1,0:T(8,128)} %copy-done.12) | copy-start | bytes 983044
  62.7 16.3 %collective-permute-start.15 = (f32[64,1024]{1,0:T(8,128)S(1)}, f32[64,1024]{1,0:T(8,128)S(1)}, u32[]{:S(2)}, u32[]{:S(2)}) collective-permute-start(f32[64,1024]{1,0:T(8,128)S(1)} %get-tuple-element.21), channel_id=1, source_target_pairs={{0,2},{1,3},{2,0},{3,1},{4,6},{5,7},{6,4},{7,5},{8,10},{9,11},{10,... | collective-permute-start | bytes 786440 | tf_op jit(solution)/shard_map/ppermute | solution.py:427
  63.7 15.2 %collective-permute-start.16 = (f32[64,1024]{1,0:T(8,128)S(1)}, f32[64,1024]{1,0:T(8,128)S(1)}, u32[]{:S(2)}, u32[]{:S(2)}) collective-permute-start(f32[64,1024]{1,0:T(8,128)S(1)} %get-tuple-element.22), channel_id=1, source_target_pairs={{0,16},{1,17},{2,18},{3,19},{4,20},{5,21},{6,22},{7,23},{8,24},{9,... | collective-permute-start | bytes 786440 | tf_op jit(solution)/shard_map/ppermute | solution.py:427
  64.3 14.6 %collective-permute-start.17 = (f32[64,1024]{1,0:T(8,128)S(1)}, f32[64,1024]{1,0:T(8,128)S(1)}, u32[]{:S(2)}, u32[]{:S(2)}) collective-permute-start(f32[64,1024]{1,0:T(8,128)S(1)} %get-tuple-element.23), channel_id=1, source_target_pairs={{0,18},{1,19},{2,16},{3,17},{4,22},{5,23},{6,20},{7,21},{8,26},{9,... | collective-permute-start | bytes 786440 | tf_op jit(solution)/shard_map/ppermute | solution.py:427
  78.9 3.0 %collective-permute-start.18 = (f32[64,1024]{1,0:T(8,128)S(1)}, f32[64,1024]{1,0:T(8,128)S(1)}, u32[]{:S(2)}, u32[]{:S(2)}) collective-permute-start(f32[64,1024]{1,0:T(8,128)S(1)} %get-tuple-element.25.refs_0_), channel_id=1, source_target_pairs={{0,1},{1,0},{2,3},{3,2},{4,5},{5,4},{6,7},{7,6},{8,9},{9,8},{10,11... | collective-permute-start | bytes 786440 | tf_op jit(solution)/shard_map/ppermute | solution.py:427
  79.1 2.9 %collective-permute-start.19 = (f32[64,1024]{1,0:T(8,128)S(1)}, f32[64,1024]{1,0:T(8,128)S(1)}, u32[]{:S(2)}, u32[]{:S(2)}) collective-permute-start(f32[64,1024]{1,0:T(8,128)S(1)} %collective-permute-done.15.refs_2_), channel_id=1, source_target_pairs={{0,1},{1,0},{2,3},{3,2},{4,5},{5,4},{6,7},{7,6},{8,9},{9,8},{10,11... | collective-permute-start | bytes 786440 | tf_op jit(solution)/shard_map/ppermute | solution.py:427
  79.5 2.5 %collective-permute-start.20 = (f32[64,1024]{1,0:T(8,128)S(1)}, f32[64,1024]{1,0:T(8,128)S(1)}, u32[]{:S(2)}, u32[]{:S(2)}) collective-permute-start(f32[64,1024]{1,0:T(8,128)S(1)} %collective-permute-done.16.refs_4_), channel_id=1, source_target_pairs={{0,1},{1,0},{2,3},{3,2},{4,5},{5,4},{6,7},{7,6},{8,9},{9,8},{10,11... | collective-permute-start | bytes 786440 | tf_op jit(solution)/shard_map/ppermute | solution.py:427
  79.6 2.4 %collective-permute-start.21 = (f32[64,1024]{1,0:T(8,128)S(1)}, f32[64,1024]{1,0:T(8,128)S(1)}, u32[]{:S(2)}, u32[]{:S(2)}) collective-permute-start(f32[64,1024]{1,0:T(8,128)S(1)} %collective-permute-done.17.refs_6_), channel_id=1, source_target_pairs={{0,1},{1,0},{2,3},{3,2},{4,5},{5,4},{6,7},{7,6},{8,9},{9,8},{10,11... | collective-permute-start | bytes 786440 | tf_op jit(solution)/shard_map/ppermute | solution.py:427

commit v3 on v2

--- a/solution.py
+++ b/solution.py
@@ -90,7 +90,8 @@
                 points[source : source + 1, :].astype(F32)
             )
     used = groups * (k + 1)
-    rest[used:, :] = near[near.shape[0] - rest.shape[0] + used :, :]
+    spare = rest.shape[0] - used
+    rest[used:, :] = near[near.shape[0] - spare :, :]
 
 
 def matrix_of(proj, points, size):
@@ -107,29 +108,17 @@
     return jnp.concatenate(parts, axis=0)
 
 
-def matrices_kernel(*refs):
-    bundles, out = refs[:-1], refs[-1]
-    for number, bundle in enumerate(bundles):
-        base = bundle.shape[0] - 16
-        k, size = 8, bundle.shape[1] // LIGHT
-        high, low = split(matrix_of(bundle[base : base + k, :], bundle[base + k : base + k + 1, :], size))
-        span = LIGHT * k
-        out[number, :span] = high
-        out[number, span : 2 * span] = low
-        out[number, 2 * span :] = high
-
-
 def roll_lanes(value, shift):
     return pltpu.roll(value, shift % value.shape[1], 1)
 
 
 def evolve_kernel(slabs, shared_heavy, *refs):
     own_pulse, other_pulse = refs[:2]
-    bundles, ready = refs[2:14], refs[14:16]
-    heavies = refs[16:17] if shared_heavy else refs[16:18]
-    refs = refs[16 + len(heavies) :]
+    bundles = refs[2:14]
+    heavies = refs[14:15] if shared_heavy else refs[14:16]
+    refs = refs[14 + len(heavies) :]
     outs, moment = refs[:4], refs[4]
-    start, term1, term2, term3, start_split, split1, split2, total, light, full, pots, weights = refs[5:]
+    start, term1, term2, term3, start_split, split1, split2, total, light, full, pots, weights, coming = refs[5:]
     y, quad, x, c = place()
     quads = slabs // GROUP
     part = start.shape[1] // 2
@@ -152,18 +141,16 @@
         pots[slot] = bundle[base + k + 1 : base + k + 2, :]
         weights[slot] = bundle[base + k + 2 : base + k + 3, : 4 * span]
 
+        def build(bundle=bundle, slot=slot):
+            high, low = split(matrix_of(bundle[base : base + k, :], bundle[base + k : base + k + 1, :], size))
+            light[slot, :span] = high
+            light[slot, span : 2 * span] = low
+            light[slot, 2 * span :] = high
+
         if direction == 1:
-            light[slot] = ready[0][2 * xf + cf]
-        elif xf == 0:
-            light[slot] = ready[1][direction + cf]
+            build()
         else:
-
-            @pl.when((has_low if direction == 0 else has_high) & (slot > 0) & (slot < SLOTS - 1))
-            def _(bundle=bundle, slot=slot):
-                high, low = split(matrix_of(bundle[base : base + k, :], bundle[base + k : base + k + 1, :], size))
-                light[slot, :span] = high
-                light[slot, span : 2 * span] = low
-                light[slot, 2 * span :] = high
+            pl.when((has_low if direction == 0 else has_high) & (slot > 0) & (slot < SLOTS - 1))(build)
 
     def plane_of(slot):
         return quad * GROUP + slot - HALO
@@ -172,13 +159,15 @@
         plane = plane_of(slot)
         return (plane < edge) | (plane >= slabs - edge)
 
-    extra = 3 * span
-
-    def build_full(store, source):
+    wide = 4 * span
+
+    def build_full(store, source, slot):
+        for part_of in range(3):
+            full[store, part_of * wide : part_of * wide + span] = light[slot, part_of * span : (part_of + 1) * span]
         for group in range(3):
             high, low = split(matrix_of(source(group * k, k), source(3 * k + group, 1), size))
             for part_of, value in enumerate((high, low, high)):
-                at = part_of * extra + group * span
+                at = part_of * wide + (group + 1) * span
                 full[store, at : at + span] = value
 
     if shared_heavy:
@@ -191,7 +180,7 @@
 
             @pl.when(exists & is_heavy(slot))
             def _(slot=slot):
-                build_full(slot - 1, lambda at, n: heavies[0][slot - 1, at : at + n, :])
+                build_full(slot - 1, lambda at, n: heavies[0][slot - 1, at : at + n, :], slot)
     else:
         ends = (quad == 0) | (quad == quads - 1)
         beside = (quad == 1) | (quad == quads - 2)
@@ -204,12 +193,14 @@
         @pl.when(ends)
         def _():
             for cf in range(2):
-                build_full(c if cf == 0 else 1 - c, lambda at, n, cf=cf: heavies[cf][at : at + n, :])
+                core = c if cf == 0 else 1 - c
+                build_full(core, lambda at, n, cf=cf: heavies[cf][at : at + n, :], first_slot + core)
 
         @pl.when(beside)
         def _():
             mine = (c == 1) == low_end
-            build_full(0, lambda at, n: jnp.where(mine, heavies[0][at : at + n, :], heavies[1][at : at + n, :]))
+            lone = jnp.where(low_end, 1, SLOTS - 2)
+            build_full(0, lambda at, n: jnp.where(mine, heavies[0][at : at + n, :], heavies[1][at : at + n, :]), lone)
 
     for missing, slot in ((jnp.logical_not(has_low), HALO - 1), (jnp.logical_not(has_high), HALO + GROUP)):
 
@@ -232,24 +223,28 @@
     def columns(j):
         return slice(j * 128, (j + 1) * 128)
 
-    def neighbours(field, slot, j, v):
-        around = field[slot - 1, :, columns(j)] + field[slot + 1, :, columns(j)]
-        around += roll_lanes(v, groups_y) + roll_lanes(v, -groups_y)
-        w = field[slot, :, columns((j + 1) % 8)]
-        around += w if j < 7 else jnp.where(wrap_up, roll_lanes(w, groups_y - 1), roll_lanes(w, -1))
-        w = field[slot, :, columns((j - 1) % 8)]
-        return around + (w if j > 0 else jnp.where(wrap_down, roll_lanes(w, 1 - groups_y), roll_lanes(w, 1)))
+    def block_of(field, slot, rows):
+        values = [field[slot, rows, columns(j)] for j in range(8)]
+        beyond = [field[slot - 1, rows, columns(j)] + field[slot + 1, rows, columns(j)] for j in range(8)]
+        for j, v in enumerate(values):
+            around = beyond[j] + (roll_lanes(v, groups_y) + roll_lanes(v, -groups_y))
+            w = values[(j + 1) % 8]
+            around += w if j < 7 else jnp.where(wrap_up, roll_lanes(w, groups_y - 1), roll_lanes(w, -1))
+            w = values[(j - 1) % 8]
+            around += w if j > 0 else jnp.where(wrap_down, roll_lanes(w, 1 - groups_y), roll_lanes(w, 1))
+            yield columns(j), v, around
 
     def pulse_field(slot, p):
         strength = jnp.where(y == p, own_pulse[0], other_pulse[0])
         position = (plane_of(slot).astype(F32) + 0.5) / slabs
         return strength * 4.0 * (position - 0.5)
 
-    def put(term, halves, slot, rows, cols, value):
-        term[slot, rows, cols] = value
-        high, low = split(value)
-        halves[slot, rows, cols] = high
-        halves[slot, slice(4 * part + rows.start, 4 * part + rows.stop), cols] = low
+    def put(term, halves, slot, pieces):
+        halved = [split(value) for _, _, value in pieces]
+        for (rows, cols, value), (high, low) in zip(pieces, halved):
+            term[slot, rows, cols] = value
+            halves[slot, rows, cols] = high
+            halves[slot, slice(4 * part + rows.start, 4 * part + rows.stop), cols] = low
 
     def bounds(order):
         reach = TERMS - order
@@ -261,79 +256,105 @@
         factor = TIME_STEP / order
         low, high = bounds(order)
 
-        def ahead(slot):
-            return coefficients(
-                halves[slot], light[slot, : 2 * span, :], weights[slot][:, :span], count, span, factor
-            )
-
-        def body(slot, wide):
-            following = ahead(jnp.minimum(slot + 1, high - 1))
-            apply(slot, lax.dot_general(wide, light[slot], NN, preferred_element_type=F32))
-
-            @pl.when(is_heavy(slot))
+        begin = jnp.where(has_high, low, low - low % 2)
+        number = (high - begin + 1) // 2
+
+        def pair(i):
+            return jnp.clip(begin + 2 * i, low, high - 1), jnp.minimum(begin + 2 * i + 1, high - 1)
+
+        def ahead(i):
+            for side, slot in enumerate(pair(i)):
+                coming[i % 2, side, :count] = coefficients(
+                    halves[slot], light[slot, : 2 * span, :], weights[slot][:, :span], count, span, factor
+                )
+
+        def whole(slot, beyond):
+            store = store_of(slot)
+            weight = jnp.where(iota((1, wide), 1) < span, 0.0, weights[slot]) if beyond else weights[slot]
+            right = coefficients(halves[slot], full[store, : 2 * wide, :], weight, count, wide, factor)
+            return lax.dot_general(right, full[store], NN, preferred_element_type=F32)
+
+        def body(i, carry):
+            slots = pair(i)
+            distinct = slots[0] != slots[1]
+            both = is_heavy(slots[0]) & is_heavy(slots[1]) & distinct
+
+            @pl.when(jnp.logical_not(both))
             def _():
-                store = store_of(slot)
-                wide = coefficients(
-                    halves[slot], full[store, : 2 * extra, :], weights[slot][:, span:], count, extra, factor
-                )
-                correct(slot, lax.dot_general(wide, full[store], NN, preferred_element_type=F32))
-
-            return following
-
-        lax.fori_loop(low, high, body, ahead(low))
-
-    re, im = slice(0, 2 * part), slice(2 * part, 4 * part)
+                ahead(i + 1)
+                for side, slot in enumerate(slots):
+                    apply(
+                        slot,
+                        lax.dot_general(coming[i % 2, side, :count], light[slot], NN, preferred_element_type=F32),
+                    )
+
+            @pl.when(both)
+            def _():
+                ahead(i + 1)
+                for slot in slots:
+                    apply(slot, whole(slot, False))
+
+            for side, slot in enumerate(slots):
+
+                @pl.when(is_heavy(slot) & jnp.logical_not(both) & (distinct | (side == 0)))
+                def _(slot=slot):
+                    correct(slot, whole(slot, True))
+
+            return carry
+
+        ahead(0)
+        lax.fori_loop(0, number, body, 0)
+
+    def blocks():
+        for ri in range(2):
+            for p in range(2):
+                here, there = (2 * ri + p) * part, (2 * (1 - ri) + p) * part
+                yield ri, p, slice(here, here + part), slice(there, there + part)
 
     def apply_first(slot, projected):
-        fields = [pulse_field(slot, p) for p in range(2)]
-        pot = pots[slot] + 3.0
-        for j in range(8):
-            cols = columns(j)
-            v = start[slot, :, cols]
-            around = neighbours(start, slot, j, v)
-            sign = jnp.where(iota(v.shape, 0) < part, -TIME_STEP, TIME_STEP)
-            image = sign * (pot[:, cols] * v - 0.5 * around) + projected[:, cols]
-            turned = sign * v
+        for ri in range(2):
+            sign = TIME_STEP if ri else -TIME_STEP
+            rows = slice(ri * part, (ri + 1) * part)
+            pot = (pots[slot] + 3.0) * sign
+            images = [
+                (cols, pot[:, cols] * v - (0.5 * sign) * around + projected[rows, cols], v)
+                for cols, v, around in block_of(start, slot, rows)
+            ]
             for p in range(2):
-                value = image + fields[p] * turned
-                put(term1, split1, slot, slice(p * part, (p + 1) * part), cols, value[part:])
-                put(term1, split1, slot, slice((2 + p) * part, (3 + p) * part), cols, value[:part])
+                there = (2 * (1 - ri) + p) * part
+                field = pulse_field(slot, p) * sign
+                there = slice(there, there + part)
+                put(term1, split1, slot, [(there, cols, image + field * v) for cols, image, v in images])
+
+    def correct_with(term, halves, slot, rows, there, projected):
+        put(
+            term, halves, slot,
+            [(there, columns(j), term[slot, there, columns(j)] + projected[rows, columns(j)]) for j in range(8)],
+        )
 
     def correct_first(slot, projected):
-        for j in range(8):
-            cols = columns(j)
-            for p in range(2):
-                for ri in range(2):
-                    rows = slice((2 * ri + p) * part, (2 * ri + p + 1) * part)
-                    more = projected[(1 - ri) * part : (2 - ri) * part, cols]
-                    put(term1, split1, slot, rows, cols, term1[slot, rows, cols] + more)
+        for ri, p, _, there in blocks():
+            correct_with(term1, split1, slot, slice(ri * part, (ri + 1) * part), there, projected)
 
     sweep(1, start_split, 2 * part, apply_first, correct_first)
 
-    def image_of(order, source, slot, projected):
-        factor = TIME_STEP / order
-        fields = [pulse_field(slot, p) for p in range(2)]
-        row = iota((4 * part, 128), 0)
-        sign = jnp.where(row < 2 * part, -factor, factor)
-        shift = sign * jnp.where(row // part % 2 == 0, 3.0 + fields[0], 3.0 + fields[1])
-        half = -0.5 * sign
-        for j in range(8):
-            cols = columns(j)
-            v = source[slot, :, cols]
-            around = neighbours(source, slot, j, v)
-            yield cols, (pots[slot][:, cols] * sign + shift) * v + half * around + projected[:, cols]
+    def images(order, source, slot, projected):
+        for ri, p, here, there in blocks():
+            sign = TIME_STEP / order if ri else -TIME_STEP / order
+            pot = (pots[slot] + (3.0 + pulse_field(slot, p))) * sign
+            yield [
+                (there, cols, pot[:, cols] * v - (0.5 * sign) * around + projected[here, cols])
+                for cols, v, around in block_of(source, slot, here)
+            ]
 
     def later(order, source, halves, target, target_split):
         def apply(slot, projected):
-            for cols, image in image_of(order, source, slot, projected):
-                put(target, target_split, slot, re, cols, image[im])
-                put(target, target_split, slot, im, cols, image[re])
+            for pieces in images(order, source, slot, projected):
+                put(target, target_split, slot, pieces)
 
         def correct(slot, projected):
-            for j in range(8):
-                cols = columns(j)
-                put(target, target_split, slot, re, cols, target[slot, re, cols] + projected[im, cols])
-                put(target, target_split, slot, im, cols, target[slot, im, cols] + projected[re, cols])
+            for _, _, here, there in blocks():
+                correct_with(target, target_split, slot, here, there, projected)
 
         sweep(order, halves, 4 * part, apply, correct)
 
@@ -342,19 +363,19 @@
 
     def apply_last(slot, projected):
         at = slot - HALO
-        for cols, image in image_of(TERMS, term3, slot, projected):
-            terms = term1[slot, :, cols] + term2[slot, :, cols] + term3[slot, :, cols]
-            for ri in range(2):
-                begun = start[slot, ri * part : (ri + 1) * part, cols]
-                for p in range(2):
-                    rows = slice((2 * ri + p) * part, (2 * ri + p + 1) * part)
-                    turned = slice((2 - 2 * ri + p) * part, (3 - 2 * ri + p) * part)
-                    total[at, rows, cols] = begun + terms[rows] + image[turned]
+        for pieces in images(TERMS, term3, slot, projected):
+            sums = []
+            for there, cols, image in pieces:
+                begun = (there.start // (2 * part)) * part
+                terms = term1[slot, there, cols] + term2[slot, there, cols] + term3[slot, there, cols]
+                sums.append(start[slot, begun : begun + part, cols] + terms + image)
+            for (there, cols, _), value in zip(pieces, sums):
+                total[at, there, cols] = value
 
     def correct_last(slot, projected):
         at = slot - HALO
-        total[at, re] += projected[im]
-        total[at, im] += projected[re]
+        for _, _, here, there in blocks():
+            total[at, there] += projected[here]
 
     sweep(TERMS, split1, 4 * part, apply_last, correct_last)
 
@@ -439,6 +460,7 @@
         in_specs=[VMEM] * 5 + [SMEM],
         out_specs=[VMEM] * 2,
         scratch_shapes=[pltpu.VMEM((cells, channels // 2), F32), pltpu.VMEM((channels // 2, cells), F32)],
+        compiler_params=pltpu.CompilerParams(vmem_limit_bytes=8 * 2**20),
         name="pack",
     )(orbitals.reshape(cells, channels), potential.reshape(nx, ny), projectors, couplings.T, sphere_points, atom_count)
     beside = permute(far, lambda p, s: (p, s ^ 2))
@@ -448,25 +470,16 @@
         out_shape=jax.ShapeDtypeStruct((32, cells), F32),
         in_specs=[VMEM] * 3,
         out_specs=VMEM,
+        compiler_params=pltpu.CompilerParams(vmem_limit_bytes=4 * 2**20),
         name="rest",
     )(projectors, sphere_points, near)
-    pulse_sent, heavy = lax.optimization_barrier((pulse, heavy))
     below2, above2 = shift(beside, GROUP), shift(beside, -GROUP)
+    near_mate, pulse_sent = lax.optimization_barrier((swap_core(near), pulse))
     other_pulse = permute(pulse_sent, lambda p, s: (1 - p, s))
+    above1, below1, other_pulse = lax.optimization_barrier((above1, below1, other_pulse))
     order = []
     for piece in (below1, below2, near, beside, above1, above2):
-        order += [piece, swap_core(piece)]
-
-    def matrices(bundles):
-        return pl.pallas_call(
-            matrices_kernel,
-            out_shape=jax.ShapeDtypeStruct((len(bundles), 3 * LIGHT * k, cells), BF16),
-            in_specs=[VMEM] * len(bundles),
-            out_specs=VMEM,
-            name="matrices",
-        )(*bundles)
-
-    ready = [matrices(order[4:8]), matrices(order[:2] + order[8:10])]
+        order += [piece, near_mate if piece is near else swap_core(piece)]
 
     edge = max(slabs // 8, 1)
     shared_heavy = not (edge == 2 and quads >= 4)
@@ -478,28 +491,20 @@
         stores = SLOTS - 2
     else:
         crowded = (0, 1, slabs - 2, slabs - 1)
-        across = permute(heavy, lambda p, s: (p, s ^ 2) if s in crowded else None)
         x = (g // 2) % 2
         own = ((quad == 0) & (x == 0)) | ((quad == quads - 1) & (x == 1))
-        held = jnp.where(own, heavy, across)
-
-        def outward(p, s):
-            if s // GROUP == 0 and s % 2 == 1:
-                return p, s + GROUP
-            if s // GROUP == quads - 1 and s % 2 == 0:
-                return p, s - GROUP
-            return None
-
-        moved = permute(held, outward)
-        held = jnp.where((quad == 0) | (quad == quads - 1), held, moved)
+        inner = {1: GROUP, slabs - 2: -GROUP}
+        across = permute(heavy, lambda p, s: (p, s ^ 2) if s in crowded else None)
+        along = permute(heavy, lambda p, s: (p, s + inner[s]) if s in inner else None)
+        over = permute(heavy, lambda p, s: (p, (s + inner[s]) ^ 2) if s in inner else None)
+        held = jnp.where(own, heavy, across + along + over)
         heavies = [held, swap_core(held)]
         stores = 2
 
-    wide = 3 * (atoms - LIGHT) * k
     outs = pl.pallas_call(
         functools.partial(evolve_kernel, slabs, shared_heavy),
         out_shape=[jax.ShapeDtypeStruct((4 * part, cells), F32)] * 4 + [jax.ShapeDtypeStruct((2, 128), F32)],
-        in_specs=[SMEM] * 2 + [VMEM] * (14 + len(heavies)),
+        in_specs=[SMEM] * 2 + [VMEM] * (12 + len(heavies)),
         out_specs=[VMEM] * 5,
         scratch_shapes=[pltpu.VMEM((SLOTS, 2 * part, cells), F32)]
         + [pltpu.VMEM((SLOTS, 4 * part, cells), F32)] * 3
@@ -508,13 +513,14 @@
         + [
             pltpu.VMEM((GROUP, 4 * part, cells), F32),
             pltpu.VMEM((SLOTS, 3 * LIGHT * k, cells), BF16),
-            pltpu.VMEM((stores, wide, cells), BF16),
+            pltpu.VMEM((stores, 3 * atoms * k, cells), BF16),
             pltpu.VMEM((SLOTS, 1, cells), F32),
             pltpu.VMEM((SLOTS, 1, 128), F32),
+            pltpu.VMEM((2, 2, 4 * part, 3 * LIGHT * k), BF16),
         ],
-        compiler_params=pltpu.CompilerParams(vmem_limit_bytes=(36 if not shared_heavy else 50) * 2**20),
+        compiler_params=pltpu.CompilerParams(vmem_limit_bytes=(28 if not shared_heavy else 40) * 2**20),
         name="evolve",
-    )(pulse, other_pulse, *order, *ready, *heavies)
+    )(pulse, other_pulse, *order, *heavies)
     moment = outs[4]
     finals = [
         outs[0],

time: 85.2 us -> 75.3 us (0.88)
  Pallas kernels: 31.1 us -> 18.6 us
  waiting for transfers between devices: 0.78 us -> 5.74 us
  starting transfers between devices: 29.9 us -> 28.6 us
  other arithmetic: 1.61 us -> 0.68 us
    pallas_call x2 -> x0, Pallas kernels: 5.36 us -> none  [matrices(): pl.pallas_call(matrices_kernel, out_shape=jax.ShapeDtypeStruct((len(bundl...]
    ppermute x22 -> x23, waiting for transfers between devices: 0.78 us -> 5.74 us  [permute(): return lax.ppermute(value, BOTH, pairs)]
    pallas_call x1, Pallas kernels: 19.9 us -> 16.5 us  [local(): pl.pallas_call(functools.partial(evolve_kernel, slabs, shared_heavy), out...]
    pallas_call x1, Pallas kernels: 2.67 us -> 0.56 us  [local(): pl.pallas_call(pack_kernel, out_shape=(bundle, bundle), in_specs=[VMEM] *...]
    pallas_call x1, Pallas kernels: 1.69 us -> 0.02 us  [local(): pl.pallas_call(rest_kernel, out_shape=jax.ShapeDtypeStruct((32, cells), F...]
    ppermute x22 -> x23, starting transfers between devices: 29.9 us -> 28.6 us  [permute(): return lax.ppermute(value, BOTH, pairs)]
    select_n x2 -> x1, other arithmetic: 0.97 us -> 0.03 us  [local(): held = jnp.where(own, heavy, across + along + over)]
    unnamed x28 -> x10, local copies, waits for them, and re-layouts: 3.83 us -> 3.52 us
  transfers between devices with their start and end apart: 22 -> 23, of which waited for: 3 -> 7; matrix products, arithmetic and copies ran while one was open for 2% -> 1% of each run, Pallas kernels for 8% -> 0%
where the time goes in v3:
time: 75.3 us; the launch traced here: 74.8 us
  starting transfers between devices  28.6 us (38%)
  Pallas kernels  18.6 us (25%)
  blocking collectives  13.1 us (17%)
  waiting for transfers between devices  5.74 us (8%)
  between operations  4.57 us (6%)
  local copies, waits for them, and re-layouts  3.54 us (5%)
    ppermute x23, starting transfers between devices, permute(): return lax.ppermute(value, BOTH, pairs)  28.6 us
    pallas_call x1, Pallas kernels, local(): pl.pallas_call(functools.partial(evolve_kernel, slabs, shared_heavy), out...  16.5 us
    all_to_all x1, blocking collectives, local(): shares = lax.all_to_all(shares, BOTH, 0, 0)  13.1 us
    ppermute x23, waiting for transfers between devices, permute(): return lax.ppermute(value, BOTH, pairs)  5.74 us
    unnamed x10, local copies, waits for them, and re-layouts  3.52 us
    pallas_call x1, Pallas kernels, local(): pl.pallas_call(unpack_kernel, out_shape=jax.ShapeDtypeStruct((cells, chan...  1.51 us
  transfers between devices with their start and end apart: 23, of which 7 were waited for; matrix products, arithmetic and copies ran while one was open for 1% of the time, Pallas kernels for 0%

profile of v3, /device:TPU:0, one launch (start us, length us, event | category | flops | bytes accessed | tf_op | source)
XLA Modules:
  0.0 74.8 jit_solution(1124121589006910622)
XLA Ops:
  1.3 0.0 copy-done.4
  1.3 1.2 %copy-done = f32[1,32,32,256]{3,2,1,0:T(8,128)S(1)} copy-done((f32[1,32,32,256]{3,2,1,0:T(8,128)S(1)}, f32[1,32,32,256]{3,2,1,0:T(8,128)}, u32[]{:S(2)}) %copy-start) | copy-done | bytes 1048600
  2.5 0.8 %copy-done.1 = bf16[16,8,256]{2,1,0:T(8,128)(2,1)S(1)} copy-done((bf16[16,8,256]{2,1,0:T(8,128)(2,1)S(1)}, bf16[16,8,256]{2,1,0:T(8,128)(2,1)}, u32[]{:S(2)}) %copy-start.1) | copy-done | bytes 65560
  3.4 0.7 copy-done.2
  4.1 0.7 copy-done.3
  4.8 0.6 pack.1
  5.4 3.0 %collective-permute-start.5 = (f32[80,1024]{1,0:T(8,128)S(1)}, f32[80,1024]{1,0:T(8,128)S(1)}, u32[]{:S(2)}, u32[]{:S(2)}) collective-permute-start(f32[80,1024]{1,0:T(8,128)S(1)} %get-tuple-element.23), channel_id=1, source_target_pairs={{0,2},{1,3},{2,0},{3,1},{4,6},{5,7},{6,4},{7,5},{8,10},{9,11},{10,... | collective-permute-start | bytes 983048 | tf_op jit(solution)/shard_map/ppermute | solution.py:448
  8.4 0.7 collective-permute-start.14
  9.1 0.7 collective-permute-start.13
  9.8 1.9 %collective-permute-start.12 = (f32[32,1024]{1,0:T(8,128)S(1)}, f32[32,1024]{1,0:T(8,128)S(1)}, u32[]{:S(2)}, u32[]{:S(2)}) collective-permute-start(f32[32,1024]{1,0:T(8,128)S(1)} %rest.1), channel_id=1, source_target_pairs={{0,2},{1,3},{14,12},{15,13},{16,18},{17,19},{30,28},{31,29}} | collective-permute-start | bytes 393224 | tf_op jit(solution)/shard_map/ppermute | solution.py:448
  11.7 2.1 %collective-permute-start.2 = (f32[80,1024]{1,0:T(8,128)S(1)}, f32[80,1024]{1,0:T(8,128)S(1)}, u32[]{:S(2)}, u32[]{:S(2)}) collective-permute-start(f32[80,1024]{1,0:T(8,128)S(1)} %get-tuple-element.19.near.refs_6_), channel_id=1, source_target_pairs={{0,1},{1,0},{2,3},{3,2},{4,5},{5,4},{6,7},{7,6},{8,9},{9,8},{10,11... | collective-permute-start | bytes 983048 | tf_op jit(solution)/shard_map/ppermute | solution.py:448
  13.8 0.0 collective-permute-done.14
  13.8 1.3 %collective-permute-start.1 = (f32[80,1024]{1,0:T(8,128)S(1)}, f32[80,1024]{1,0:T(8,128)S(1)}, u32[]{:S(2)}, u32[]{:S(2)}) collective-permute-start(f32[80,1024]{1,0:T(8,128)S(1)} %get-tuple-element.19.near.refs_6_), channel_id=1, source_target_pairs={{0,4},{1,5},{2,6},{3,7},{4,8},{5,9},{6,10},{7,11},{8,12},{9,13},{1... | collective-permute-start | bytes 983048 | tf_op jit(solution)/shard_map/ppermute | solution.py:448
  15.1 0.0 collective-permute-done.13
  15.2 1.3 %collective-permute-start = (f32[80,1024]{1,0:T(8,128)S(1)}, f32[80,1024]{1,0:T(8,128)S(1)}, u32[]{:S(2)}, u32[]{:S(2)}) collective-permute-start(f32[80,1024]{1,0:T(8,128)S(1)} %get-tuple-element.19.near.refs_6_), channel_id=1, source_target_pairs={{4,0},{5,1},{6,2},{7,3},{8,4},{9,5},{10,6},{11,7},{12,8},{13,9},{1... | collective-permute-start | bytes 983048 | tf_op jit(solution)/shard_map/ppermute | solution.py:448
  16.4 0.1 collective-permute-done.5.refs_8_
  16.5 1.3 %collective-permute-start.10 = (f32[80,1024]{1,0:T(8,128)S(1)}, f32[80,1024]{1,0:T(8,128)S(1)}, u32[]{:S(2)}, u32[]{:S(2)}) collective-permute-start(f32[80,1024]{1,0:T(8,128)S(1)} %collective-permute-done.5.refs_8_), channel_id=1, source_target_pairs={{4,0},{5,1},{6,2},{7,3},{8,4},{9,5},{10,6},{11,7},{12,8},{13,9},{1... | collective-permute-start | bytes 983048 | tf_op jit(solution)/shard_map/ppermute | solution.py:448
  17.8 0.4 collective-permute-done.12
  18.2 9.0 %collective-permute-start.6 = (f32[80,1024]{1,0:T(8,128)S(1)}, f32[80,1024]{1,0:T(8,128)S(1)}, u32[]{:S(2)}, u32[]{:S(2)}) collective-permute-start(f32[80,1024]{1,0:T(8,128)S(1)} %collective-permute-done.5.refs_8_), channel_id=1, source_target_pairs={{0,4},{1,5},{2,6},{3,7},{4,8},{5,9},{6,10},{7,11},{8,12},{9,13},{1... | collective-permute-start | bytes 983048 | tf_op jit(solution)/shard_map/ppermute | solution.py:448
  27.2 0.1 collective-permute-start.15
  27.3 0.0 collective-permute-done.1.refs_2_
  27.3 1.6 %collective-permute-start.3 = (f32[1]{0:T(128)}, f32[1]{0:T(128)}, u32[]{:S(2)}, u32[]{:S(2)}) collective-permute-start(f32[1]{0:T(128)} %param.9), channel_id=1, source_target_pairs={{0,16},{1,17},{2,18},{3,19},{4,20},{5,21},{6,22},{7,23},{8,24},{9,... | collective-permute-start | bytes 20 | tf_op jit(solution)/shard_map/ppermute | solution.py:448
  28.9 1.4 %collective-permute-done.refs_10_ = f32[80,1024]{1,0:T(8,128)S(1)} collective-permute-done((f32[80,1024]{1,0:T(8,128)S(1)}, f32[80,1024]{1,0:T(8,128)S(1)}, u32[]{:S(2)}, u32[]{:S(2)}) %collective-permute-start) | collective-permute-done | bytes 327712 | tf_op jit(solution)/shard_map/ppermute | solution.py:448
  30.2 0.0 collective-permute-start.8
  30.3 0.9 %collective-permute-done.3.refs_1_ = f32[1]{0:T(128)} collective-permute-done((f32[1]{0:T(128)}, f32[1]{0:T(128)}, u32[]{:S(2)}, u32[]{:S(2)}) %collective-permute-start.3) | collective-permute-done | bytes 36 | tf_op jit(solution)/shard_map/ppermute | solution.py:448
  31.1 0.0 collective-permute-start.4
  31.1 0.0 collective-permute-done.15.refs_15_
  31.1 0.5 collective-permute-start.9
  31.7 2.1 %collective-permute-done.10.refs_12_ = f32[80,1024]{1,0:T(8,128)S(1)} collective-permute-done((f32[80,1024]{1,0:T(8,128)S(1)}, f32[80,1024]{1,0:T(8,128)S(1)}, u32[]{:S(2)}, u32[]{:S(2)}) %collective-permute-start.10) | collective-permute-done | bytes 327712 | tf_op jit(solution)/shard_map/ppermute | solution.py:448
  33.8 0.0 collective-permute-start.11
  33.8 0.5 collective-permute-start.7
  34.9 0.0 collective-permute-done.8.refs_9_
  34.9 0.0 collective-permute-done.9.refs_11_
  35.0 0.4 collective-permute-done.11.refs_13_
  35.4 0.5 collective-permute-done.7.refs_5_
  35.9 16.5 %evolve.1 = (f32[64,1024]{1,0:T(8,128)S(1)}, f32[64,1024]{1,0:T(8,128)S(1)}, f32[64,1024]{1,0:T(8,128)S(1)}, f32[64,1024]{1,0:T(8,128)S(1)}, f32[2,128]{1,0:T(2,128)S(1)}) custom-call(f32[1]{0:T(128)S(6)} %copy.13.refs_0_, f32[1]{0:T(128)} %collective-permute-done.3.refs_1_, f32[80,1024]{1,0:T(8,128)S(1)} %collective-permute-done.1.refs_2_, ...), custom_call_target="tpu_custom_call" | custom-call | tf_op jit(solution)/shard_map/evolve/pallas_call | solution.py:504
  52.4 0.1 collective-permute-start.16
  52.5 1.6 %collective-permute-start.17 = (f32[64,1024]{1,0:T(8,128)S(1)}, f32[64,1024]{1,0:T(8,128)S(1)}, u32[]{:S(2)}, u32[]{:S(2)}) collective-permute-start(f32[64,1024]{1,0:T(8,128)S(1)} %get-tuple-element.28), channel_id=1, source_target_pairs={{0,16},{1,17},{2,18},{3,19},{4,20},{5,21},{6,22},{7,23},{8,24},{9,... | collective-permute-start | bytes 786440 | tf_op jit(solution)/shard_map/ppermute | solution.py:448
  54.1 1.9 %collective-permute-start.18 = (f32[64,1024]{1,0:T(8,128)S(1)}, f32[64,1024]{1,0:T(8,128)S(1)}, u32[]{:S(2)}, u32[]{:S(2)}) collective-permute-start(f32[64,1024]{1,0:T(8,128)S(1)} %get-tuple-element.29), channel_id=1, source_target_pairs={{0,18},{1,19},{2,16},{3,17},{4,22},{5,23},{6,20},{7,21},{8,26},{9,... | collective-permute-start | bytes 786440 | tf_op jit(solution)/shard_map/ppermute | solution.py:448
  56.0 13.1 %all_to_all.5 = f32[32,1,256]{2,1,0:T(1,128)S(1)} all-to-all(f32[32,1,256]{2,1,0:T(1,128)S(1)} %broadcast_in_dim.2), channel_id=1, replica_groups=mesh['pulse'=2,'grid'=16] {'pulse','grid'}, dimensions={0} | all-to-all | bytes 65536 | tf_op jit(solution)/shard_map/all_to_all | solution.py:533
  69.1 0.0 collective-permute-done.16.refs_2_
  69.1 0.0 collective-permute-done.17.refs_4_
  69.1 0.2 collective-permute-start.19
  69.3 0.4 collective-permute-start.20
  69.7 0.1 collective-permute-start.21
  69.8 0.4 collective-permute-start.22
  70.2 0.6 slice_reduce_fusion
  72.2 1.5 %unpack.1 = f32[1024,256]{1,0:T(8,128)} custom-call(f32[64,1024]{1,0:T(8,128)S(1)} %get-tuple-element.31.refs_0_, f32[64,1024]{1,0:T(8,128)S(1)} %collective-permute-done.19.refs_1_, f32[64,1024]{1,0:T(8,128)S(1)} %collective-permute-done.16.refs_2_, f32[64,1024]{1,0:T(8,128)S(1)} %collective-permute-done.20.refs_3_, ...), custom_call_target="tpu_custom_call" | custom-call | tf_op jit(solution)/shard_map/unpack/pallas_call | solution.py:538
  (18 shorter events, 0.1 us)
Async XLA Ops:
  0.6 0.7 copy-start.4
  1.3 1.2 %copy-start = (f32[1,32,32,256]{3,2,1,0:T(8,128)S(1)}, f32[1,32,32,256]{3,2,1,0:T(8,128)}, u32[]{:S(2)}) copy-start(f32[1,32,32,256]{3,2,1,0:T(8,128)} %param.7) | copy-start | bytes 3145732
  2.5 0.8 %copy-start.1 = (bf16[16,8,256]{2,1,0:T(8,128)(2,1)S(1)}, bf16[16,8,256]{2,1,0:T(8,128)(2,1)}, u32[]{:S(2)}) copy-start(bf16[16,8,256]{2,1,0:T(8,128)(2,1)} %proj.3) | copy-start | bytes 196612
  3.4 0.7 copy-start.2
  4.1 0.7 copy-start.3
  5.4 11.1 %collective-permute-start.5 = (f32[80,1024]{1,0:T(8,128)S(1)}, f32[80,1024]{1,0:T(8,128)S(1)}, u32[]{:S(2)}, u32[]{:S(2)}) collective-permute-start(f32[80,1024]{1,0:T(8,128)S(1)} %get-tuple-element.23), channel_id=1, source_target_pairs={{0,2},{1,3},{2,0},{3,1},{4,6},{5,7},{6,4},{7,5},{8,10},{9,11},{10,... | collective-permute-start | bytes 983048 | tf_op jit(solution)/shard_map/ppermute | solution.py:448
  8.4 5.4 %collective-permute-start.14 = (f32[32,1024]{1,0:T(8,128)S(1)}, f32[32,1024]{1,0:T(8,128)S(1)}, u32[]{:S(2)}, u32[]{:S(2)}) collective-permute-start(f32[32,1024]{1,0:T(8,128)S(1)} %rest.1), channel_id=1, source_target_pairs={{1,7},{14,8},{17,23},{30,24}} | collective-permute-start | bytes 393224 | tf_op jit(solution)/shard_map/ppermute | solution.py:448
  9.1 6.1 %collective-permute-start.13 = (f32[32,1024]{1,0:T(8,128)S(1)}, f32[32,1024]{1,0:T(8,128)S(1)}, u32[]{:S(2)}, u32[]{:S(2)}) collective-permute-start(f32[32,1024]{1,0:T(8,128)S(1)} %rest.1), channel_id=1, source_target_pairs={{1,5},{14,10},{17,21},{30,26}} | collective-permute-start | bytes 393224 | tf_op jit(solution)/shard_map/ppermute | solution.py:448
  9.8 8.4 %collective-permute-start.12 = (f32[32,1024]{1,0:T(8,128)S(1)}, f32[32,1024]{1,0:T(8,128)S(1)}, u32[]{:S(2)}, u32[]{:S(2)}) collective-permute-start(f32[32,1024]{1,0:T(8,128)S(1)} %rest.1), channel_id=1, source_target_pairs={{0,2},{1,3},{14,12},{15,13},{16,18},{17,19},{30,28},{31,29}} | collective-permute-start | bytes 393224 | tf_op jit(solution)/shard_map/ppermute | solution.py:448
  11.7 15.5 %collective-permute-start.2 = (f32[80,1024]{1,0:T(8,128)S(1)}, f32[80,1024]{1,0:T(8,128)S(1)}, u32[]{:S(2)}, u32[]{:S(2)}) collective-permute-start(f32[80,1024]{1,0:T(8,128)S(1)} %get-tuple-element.19.near.refs_6_), channel_id=1, source_target_pairs={{0,1},{1,0},{2,3},{3,2},{4,5},{5,4},{6,7},{7,6},{8,9},{9,8},{10,11... | collective-permute-start | bytes 983048 | tf_op jit(solution)/shard_map/ppermute | solution.py:448
  13.8 13.5 %collective-permute-start.1 = (f32[80,1024]{1,0:T(8,128)S(1)}, f32[80,1024]{1,0:T(8,128)S(1)}, u32[]{:S(2)}, u32[]{:S(2)}) collective-permute-start(f32[80,1024]{1,0:T(8,128)S(1)} %get-tuple-element.19.near.refs_6_), channel_id=1, source_target_pairs={{0,4},{1,5},{2,6},{3,7},{4,8},{5,9},{6,10},{7,11},{8,12},{9,13},{1... | collective-permute-start | bytes 983048 | tf_op jit(solution)/shard_map/ppermute | solution.py:448
  15.2 15.1 %collective-permute-start = (f32[80,1024]{1,0:T(8,128)S(1)}, f32[80,1024]{1,0:T(8,128)S(1)}, u32[]{:S(2)}, u32[]{:S(2)}) collective-permute-start(f32[80,1024]{1,0:T(8,128)S(1)} %get-tuple-element.19.near.refs_6_), channel_id=1, source_target_pairs={{4,0},{5,1},{6,2},{7,3},{8,4},{9,5},{10,6},{11,7},{12,8},{13,9},{1... | collective-permute-start | bytes 983048 | tf_op jit(solution)/shard_map/ppermute | solution.py:448
  16.5 17.2 %collective-permute-start.10 = (f32[80,1024]{1,0:T(8,128)S(1)}, f32[80,1024]{1,0:T(8,128)S(1)}, u32[]{:S(2)}, u32[]{:S(2)}) collective-permute-start(f32[80,1024]{1,0:T(8,128)S(1)} %collective-permute-done.5.refs_8_), channel_id=1, source_target_pairs={{4,0},{5,1},{6,2},{7,3},{8,4},{9,5},{10,6},{11,7},{12,8},{13,9},{1... | collective-permute-start | bytes 983048 | tf_op jit(solution)/shard_map/ppermute | solution.py:448
  18.2 15.6 %collective-permute-start.6 = (f32[80,1024]{1,0:T(8,128)S(1)}, f32[80,1024]{1,0:T(8,128)S(1)}, u32[]{:S(2)}, u32[]{:S(2)}) collective-permute-start(f32[80,1024]{1,0:T(8,128)S(1)} %collective-permute-done.5.refs_8_), channel_id=1, source_target_pairs={{0,4},{1,5},{2,6},{3,7},{4,8},{5,9},{6,10},{7,11},{8,12},{9,13},{1... | collective-permute-start | bytes 983048 | tf_op jit(solution)/shard_map/ppermute | solution.py:448
  27.2 3.9 %collective-permute-start.15 = (f32[32,1024]{1,0:T(8,128)S(1)}, f32[32,1024]{1,0:T(8,128)S(1)}, u32[]{:S(2)}, u32[]{:S(2)}) collective-permute-start(f32[32,1024]{1,0:T(8,128)S(1)} %add_select_fusion.refs_14_), channel_id=1, source_target_pairs={{0,1},{1,0},{2,3},{3,2},{4,5},{5,4},{6,7},{7,6},{8,9},{9,8},{10,11... | collective-permute-start | bytes 393224 | tf_op jit(solution)/shard_map/ppermute | solution.py:448
  27.3 3.8 %collective-permute-start.3 = (f32[1]{0:T(128)}, f32[1]{0:T(128)}, u32[]{:S(2)}, u32[]{:S(2)}) collective-permute-start(f32[1]{0:T(128)} %param.9), channel_id=1, source_target_pairs={{0,16},{1,17},{2,18},{3,19},{4,20},{5,21},{6,22},{7,23},{8,24},{9,... | collective-permute-start | bytes 20 | tf_op jit(solution)/shard_map/ppermute | solution.py:448
  30.2 4.7 %collective-permute-start.8 = (f32[80,1024]{1,0:T(8,128)S(1)}, f32[80,1024]{1,0:T(8,128)S(1)}, u32[]{:S(2)}, u32[]{:S(2)}) collective-permute-start(f32[80,1024]{1,0:T(8,128)S(1)} %collective-permute-done.5.refs_8_), channel_id=1, source_target_pairs={{0,1},{1,0},{2,3},{3,2},{4,5},{5,4},{6,7},{7,6},{8,9},{9,8},{10,11... | collective-permute-start | bytes 983048 | tf_op jit(solution)/shard_map/ppermute | solution.py:448
  31.1 3.8 %collective-permute-start.4 = (f32[80,1024]{1,0:T(8,128)S(1)}, f32[80,1024]{1,0:T(8,128)S(1)}, u32[]{:S(2)}, u32[]{:S(2)}) collective-permute-start(f32[80,1024]{1,0:T(8,128)S(1)} %collective-permute-done.1.refs_2_), channel_id=1, source_target_pairs={{0,1},{1,0},{2,3},{3,2},{4,5},{5,4},{6,7},{7,6},{8,9},{9,8},{10,11... | collective-permute-start | bytes 983048 | tf_op jit(solution)/shard_map/ppermute | solution.py:448
  31.1 3.8 %collective-permute-start.9 = (f32[80,1024]{1,0:T(8,128)S(1)}, f32[80,1024]{1,0:T(8,128)S(1)}, u32[]{:S(2)}, u32[]{:S(2)}) collective-permute-start(f32[80,1024]{1,0:T(8,128)S(1)} %collective-permute-done.refs_10_), channel_id=1, source_target_pairs={{0,1},{1,0},{2,3},{3,2},{4,5},{5,4},{6,7},{7,6},{8,9},{9,8},{10,11... | collective-permute-start | bytes 983048 | tf_op jit(solution)/shard_map/ppermute | solution.py:448
  33.8 1.6 %collective-permute-start.11 = (f32[80,1024]{1,0:T(8,128)S(1)}, f32[80,1024]{1,0:T(8,128)S(1)}, u32[]{:S(2)}, u32[]{:S(2)}) collective-permute-start(f32[80,1024]{1,0:T(8,128)S(1)} %collective-permute-done.10.refs_12_), channel_id=1, source_target_pairs={{0,1},{1,0},{2,3},{3,2},{4,5},{5,4},{6,7},{7,6},{8,9},{9,8},{10,11... | collective-permute-start | bytes 983048 | tf_op jit(solution)/shard_map/ppermute | solution.py:448
  33.8 2.1 %collective-permute-start.7 = (f32[80,1024]{1,0:T(8,128)S(1)}, f32[80,1024]{1,0:T(8,128)S(1)}, u32[]{:S(2)}, u32[]{:S(2)}) collective-permute-start(f32[80,1024]{1,0:T(8,128)S(1)} %collective-permute-done.6.refs_4_), channel_id=1, source_target_pairs={{0,1},{1,0},{2,3},{3,2},{4,5},{5,4},{6,7},{7,6},{8,9},{9,8},{10,11... | collective-permute-start | bytes 983048 | tf_op jit(solution)/shard_map/ppermute | solution.py:448
  52.4 16.7 %collective-permute-start.16 = (f32[64,1024]{1,0:T(8,128)S(1)}, f32[64,1024]{1,0:T(8,128)S(1)}, u32[]{:S(2)}, u32[]{:S(2)}) collective-permute-start(f32[64,1024]{1,0:T(8,128)S(1)} %get-tuple-element.27), channel_id=1, source_target_pairs={{0,2},{1,3},{2,0},{3,1},{4,6},{5,7},{6,4},{7,5},{8,10},{9,11},{10,... | collective-permute-start | bytes 786440 | tf_op jit(solution)/shard_map/ppermute | solution.py:448
  52.5 16.6 %collective-permute-start.17 = (f32[64,1024]{1,0:T(8,128)S(1)}, f32[64,1024]{1,0:T(8,128)S(1)}, u32[]{:S(2)}, u32[]{:S(2)}) collective-permute-start(f32[64,1024]{1,0:T(8,128)S(1)} %get-tuple-element.28), channel_id=1, source_target_pairs={{0,16},{1,17},{2,18},{3,19},{4,20},{5,21},{6,22},{7,23},{8,24},{9,... | collective-permute-start | bytes 786440 | tf_op jit(solution)/shard_map/ppermute | solution.py:448
  54.1 15.0 %collective-permute-start.18 = (f32[64,1024]{1,0:T(8,128)S(1)}, f32[64,1024]{1,0:T(8,128)S(1)}, u32[]{:S(2)}, u32[]{:S(2)}) collective-permute-start(f32[64,1024]{1,0:T(8,128)S(1)} %get-tuple-element.29), channel_id=1, source_target_pairs={{0,18},{1,19},{2,16},{3,17},{4,22},{5,23},{6,20},{7,21},{8,26},{9,... | collective-permute-start | bytes 786440 | tf_op jit(solution)/shard_map/ppermute | solution.py:448
  69.1 3.0 %collective-permute-start.19 = (f32[64,1024]{1,0:T(8,128)S(1)}, f32[64,1024]{1,0:T(8,128)S(1)}, u32[]{:S(2)}, u32[]{:S(2)}) collective-permute-start(f32[64,1024]{1,0:T(8,128)S(1)} %get-tuple-element.31.refs_0_), channel_id=1, source_target_pairs={{0,1},{1,0},{2,3},{3,2},{4,5},{5,4},{6,7},{7,6},{8,9},{9,8},{10,11... | collective-permute-start | bytes 786440 | tf_op jit(solution)/shard_map/ppermute | solution.py:448
  69.3 2.9 %collective-permute-start.20 = (f32[64,1024]{1,0:T(8,128)S(1)}, f32[64,1024]{1,0:T(8,128)S(1)}, u32[]{:S(2)}, u32[]{:S(2)}) collective-permute-start(f32[64,1024]{1,0:T(8,128)S(1)} %collective-permute-done.16.refs_2_), channel_id=1, source_target_pairs={{0,1},{1,0},{2,3},{3,2},{4,5},{5,4},{6,7},{7,6},{8,9},{9,8},{10,11... | collective-permute-start | bytes 786440 | tf_op jit(solution)/shard_map/ppermute | solution.py:448
  69.7 2.5 %collective-permute-start.21 = (f32[64,1024]{1,0:T(8,128)S(1)}, f32[64,1024]{1,0:T(8,128)S(1)}, u32[]{:S(2)}, u32[]{:S(2)}) collective-permute-start(f32[64,1024]{1,0:T(8,128)S(1)} %collective-permute-done.17.refs_4_), channel_id=1, source_target_pairs={{0,1},{1,0},{2,3},{3,2},{4,5},{5,4},{6,7},{7,6},{8,9},{9,8},{10,11... | collective-permute-start | bytes 786440 | tf_op jit(solution)/shard_map/ppermute | solution.py:448
  69.8 2.4 %collective-permute-start.22 = (f32[64,1024]{1,0:T(8,128)S(1)}, f32[64,1024]{1,0:T(8,128)S(1)}, u32[]{:S(2)}, u32[]{:S(2)}) collective-permute-start(f32[64,1024]{1,0:T(8,128)S(1)} %collective-permute-done.18.refs_6_), channel_id=1, source_target_pairs={{0,1},{1,0},{2,3},{3,2},{4,5},{5,4},{6,7},{7,6},{8,9},{9,8},{10,11... | collective-permute-start | bytes 786440 | tf_op jit(solution)/shard_map/ppermute | solution.py:448

commit v4 on v3

--- a/solution.py
+++ b/solution.py
@@ -130,6 +130,14 @@
     edge = max(slabs // 8, 1)
     has_low, has_high = quad > 0, quad < quads - 1
 
+    def plane_of(slot):
+        return quad * GROUP + slot - HALO
+
+    def pulse_field(slot, p):
+        strength = jnp.where(y == p, own_pulse[0], other_pulse[0])
+        position = (plane_of(slot).astype(F32) + 0.5) / slabs
+        return strength * 4.0 * (position - 0.5)
+
     for number, bundle in enumerate(bundles):
         direction, xf, cf = number // 4, number // 2 % 2, number % 2
         slot = direction * GROUP + 2 * (x if xf == 0 else 1 - x) + (c if cf == 0 else 1 - c)
@@ -138,7 +146,9 @@
         high, low = split(rows)
         start_split[slot, : 2 * part] = high
         start_split[slot, 2 * part :] = low
-        pots[slot] = bundle[base + k + 1 : base + k + 2, :]
+        pot_row = bundle[base + k + 1 : base + k + 2, :] + 3.0
+        for p in range(2):
+            pots[slot, p] = pot_row + pulse_field(slot, p)
         weights[slot] = bundle[base + k + 2 : base + k + 3, : 4 * span]
 
         def build(bundle=bundle, slot=slot):
@@ -151,9 +161,6 @@
             build()
         else:
             pl.when((has_low if direction == 0 else has_high) & (slot > 0) & (slot < SLOTS - 1))(build)
-
-    def plane_of(slot):
-        return quad * GROUP + slot - HALO
 
     def is_heavy(slot):
         plane = plane_of(slot)
@@ -234,11 +241,6 @@
             around += w if j > 0 else jnp.where(wrap_down, roll_lanes(w, 1 - groups_y), roll_lanes(w, 1))
             yield columns(j), v, around
 
-    def pulse_field(slot, p):
-        strength = jnp.where(y == p, own_pulse[0], other_pulse[0])
-        position = (plane_of(slot).astype(F32) + 0.5) / slabs
-        return strength * 4.0 * (position - 0.5)
-
     def put(term, halves, slot, pieces):
         halved = [split(value) for _, _, value in pieces]
         for (rows, cols, value), (high, low) in zip(pieces, halved):
@@ -294,11 +296,13 @@
                 for slot in slots:
                     apply(slot, whole(slot, False))
 
-            for side, slot in enumerate(slots):
-
-                @pl.when(is_heavy(slot) & jnp.logical_not(both) & (distinct | (side == 0)))
-                def _(slot=slot):
-                    correct(slot, whole(slot, True))
+            @pl.when((is_heavy(slots[0]) | is_heavy(slots[1])) & jnp.logical_not(both))
+            def _():
+                for side, slot in enumerate(slots):
+
+                    @pl.when(is_heavy(slot) & (distinct | (side == 0)))
+                    def _(slot=slot):
+                        correct(slot, whole(slot, True))
 
             return carry
 
@@ -315,16 +319,15 @@
         for ri in range(2):
             sign = TIME_STEP if ri else -TIME_STEP
             rows = slice(ri * part, (ri + 1) * part)
-            pot = (pots[slot] + 3.0) * sign
             images = [
-                (cols, pot[:, cols] * v - (0.5 * sign) * around + projected[rows, cols], v)
+                (cols, projected[rows, cols] - (0.5 * sign) * around, v)
                 for cols, v, around in block_of(start, slot, rows)
             ]
             for p in range(2):
                 there = (2 * (1 - ri) + p) * part
-                field = pulse_field(slot, p) * sign
                 there = slice(there, there + part)
-                put(term1, split1, slot, [(there, cols, image + field * v) for cols, image, v in images])
+                pot = pots[slot, p] * sign
+                put(term1, split1, slot, [(there, cols, image + pot[:, cols] * v) for cols, image, v in images])
 
     def correct_with(term, halves, slot, rows, there, projected):
         put(
@@ -341,7 +344,7 @@
     def images(order, source, slot, projected):
         for ri, p, here, there in blocks():
             sign = TIME_STEP / order if ri else -TIME_STEP / order
-            pot = (pots[slot] + (3.0 + pulse_field(slot, p))) * sign
+            pot = pots[slot, p] * sign
             yield [
                 (there, cols, pot[:, cols] * v - (0.5 * sign) * around + projected[here, cols])
                 for cols, v, around in block_of(source, slot, here)
@@ -514,7 +517,7 @@
             pltpu.VMEM((GROUP, 4 * part, cells), F32),
             pltpu.VMEM((SLOTS, 3 * LIGHT * k, cells), BF16),
             pltpu.VMEM((stores, 3 * atoms * k, cells), BF16),
-            pltpu.VMEM((SLOTS, 1, cells), F32),
+            pltpu.VMEM((SLOTS, 2, 1, cells), F32),
             pltpu.VMEM((SLOTS, 1, 128), F32),
             pltpu.VMEM((2, 2, 4 * part, 3 * LIGHT * k), BF16),
         ],

time: 75.3 us -> 75.2 us (level)
  no operation moved by 1% of the time
where the time goes in v4:
time: 75.2 us; the launch traced here: 74.7 us
  starting transfers between devices  28.6 us (38%)
  Pallas kernels  18.5 us (25%)
  blocking collectives  13 us (17%)
  waiting for transfers between devices  5.74 us (8%)
  between operations  4.58 us (6%)
  local copies, waits for them, and re-layouts  3.54 us (5%)
    ppermute x23, starting transfers between devices, permute(): return lax.ppermute(value, BOTH, pairs)  28.6 us
    pallas_call x1, Pallas kernels, local(): pl.pallas_call(functools.partial(evolve_kernel, slabs, shared_heavy), out...  16.5 us
    all_to_all x1, blocking collectives, local(): shares = lax.all_to_all(shares, BOTH, 0, 0)  13 us
    ppermute x23, waiting for transfers between devices, permute(): return lax.ppermute(value, BOTH, pairs)  5.74 us
    unnamed x10, local copies, waits for them, and re-layouts  3.52 us
    pallas_call x1, Pallas kernels, local(): pl.pallas_call(unpack_kernel, out_shape=jax.ShapeDtypeStruct((cells, chan...  1.51 us
  transfers between devices with their start and end apart: 23, of which 7 were waited for; matrix products, arithmetic and copies ran while one was open for 1% of the time, Pallas kernels for 0%

profile of v4, /device:TPU:0, one launch (start us, length us, event | category | flops | bytes accessed | tf_op | source)
XLA Modules:
  0.0 74.7 jit_solution(16716824833935558099)
XLA Ops:
  1.3 0.0 copy-done.4
  1.3 1.2 %copy-done = f32[1,32,32,256]{3,2,1,0:T(8,128)S(1)} copy-done((f32[1,32,32,256]{3,2,1,0:T(8,128)S(1)}, f32[1,32,32,256]{3,2,1,0:T(8,128)}, u32[]{:S(2)}) %copy-start) | copy-done | bytes 1048600
  2.5 0.8 %copy-done.1 = bf16[16,8,256]{2,1,0:T(8,128)(2,1)S(1)} copy-done((bf16[16,8,256]{2,1,0:T(8,128)(2,1)S(1)}, bf16[16,8,256]{2,1,0:T(8,128)(2,1)}, u32[]{:S(2)}) %copy-start.1) | copy-done | bytes 65560
  3.4 0.7 copy-done.2
  4.1 0.7 copy-done.3
  4.8 0.6 pack.1
  5.4 3.0 %collective-permute-start.5 = (f32[80,1024]{1,0:T(8,128)S(1)}, f32[80,1024]{1,0:T(8,128)S(1)}, u32[]{:S(2)}, u32[]{:S(2)}) collective-permute-start(f32[80,1024]{1,0:T(8,128)S(1)} %get-tuple-element.23), channel_id=1, source_target_pairs={{0,2},{1,3},{2,0},{3,1},{4,6},{5,7},{6,4},{7,5},{8,10},{9,11},{10,... | collective-permute-start | bytes 983048 | tf_op jit(solution)/shard_map/ppermute | solution.py:451
  8.4 0.7 collective-permute-start.14
  9.1 0.7 collective-permute-start.13
  9.8 1.9 %collective-permute-start.12 = (f32[32,1024]{1,0:T(8,128)S(1)}, f32[32,1024]{1,0:T(8,128)S(1)}, u32[]{:S(2)}, u32[]{:S(2)}) collective-permute-start(f32[32,1024]{1,0:T(8,128)S(1)} %rest.1), channel_id=1, source_target_pairs={{0,2},{1,3},{14,12},{15,13},{16,18},{17,19},{30,28},{31,29}} | collective-permute-start | bytes 393224 | tf_op jit(solution)/shard_map/ppermute | solution.py:451
  11.7 2.1 %collective-permute-start.2 = (f32[80,1024]{1,0:T(8,128)S(1)}, f32[80,1024]{1,0:T(8,128)S(1)}, u32[]{:S(2)}, u32[]{:S(2)}) collective-permute-start(f32[80,1024]{1,0:T(8,128)S(1)} %get-tuple-element.19.near.refs_6_), channel_id=1, source_target_pairs={{0,1},{1,0},{2,3},{3,2},{4,5},{5,4},{6,7},{7,6},{8,9},{9,8},{10,11... | collective-permute-start | bytes 983048 | tf_op jit(solution)/shard_map/ppermute | solution.py:451
  13.8 0.0 collective-permute-done.14
  13.8 1.3 %collective-permute-start.1 = (f32[80,1024]{1,0:T(8,128)S(1)}, f32[80,1024]{1,0:T(8,128)S(1)}, u32[]{:S(2)}, u32[]{:S(2)}) collective-permute-start(f32[80,1024]{1,0:T(8,128)S(1)} %get-tuple-element.19.near.refs_6_), channel_id=1, source_target_pairs={{0,4},{1,5},{2,6},{3,7},{4,8},{5,9},{6,10},{7,11},{8,12},{9,13},{1... | collective-permute-start | bytes 983048 | tf_op jit(solution)/shard_map/ppermute | solution.py:451
  15.1 0.0 collective-permute-done.13
  15.2 1.3 %collective-permute-start = (f32[80,1024]{1,0:T(8,128)S(1)}, f32[80,1024]{1,0:T(8,128)S(1)}, u32[]{:S(2)}, u32[]{:S(2)}) collective-permute-start(f32[80,1024]{1,0:T(8,128)S(1)} %get-tuple-element.19.near.refs_6_), channel_id=1, source_target_pairs={{4,0},{5,1},{6,2},{7,3},{8,4},{9,5},{10,6},{11,7},{12,8},{13,9},{1... | collective-permute-start | bytes 983048 | tf_op jit(solution)/shard_map/ppermute | solution.py:451
  16.4 0.1 collective-permute-done.5.refs_8_
  16.5 1.3 %collective-permute-start.10 = (f32[80,1024]{1,0:T(8,128)S(1)}, f32[80,1024]{1,0:T(8,128)S(1)}, u32[]{:S(2)}, u32[]{:S(2)}) collective-permute-start(f32[80,1024]{1,0:T(8,128)S(1)} %collective-permute-done.5.refs_8_), channel_id=1, source_target_pairs={{4,0},{5,1},{6,2},{7,3},{8,4},{9,5},{10,6},{11,7},{12,8},{13,9},{1... | collective-permute-start | bytes 983048 | tf_op jit(solution)/shard_map/ppermute | solution.py:451
  17.8 0.4 collective-permute-done.12
  18.2 9.0 %collective-permute-start.6 = (f32[80,1024]{1,0:T(8,128)S(1)}, f32[80,1024]{1,0:T(8,128)S(1)}, u32[]{:S(2)}, u32[]{:S(2)}) collective-permute-start(f32[80,1024]{1,0:T(8,128)S(1)} %collective-permute-done.5.refs_8_), channel_id=1, source_target_pairs={{0,4},{1,5},{2,6},{3,7},{4,8},{5,9},{6,10},{7,11},{8,12},{9,13},{1... | collective-permute-start | bytes 983048 | tf_op jit(solution)/shard_map/ppermute | solution.py:451
  27.2 0.0 collective-permute-done.2.refs_7_
  27.2 0.1 collective-permute-start.15
  27.3 0.0 collective-permute-done.1.refs_2_
  27.3 1.6 %collective-permute-start.3 = (f32[1]{0:T(128)}, f32[1]{0:T(128)}, u32[]{:S(2)}, u32[]{:S(2)}) collective-permute-start(f32[1]{0:T(128)} %param.9), channel_id=1, source_target_pairs={{0,16},{1,17},{2,18},{3,19},{4,20},{5,21},{6,22},{7,23},{8,24},{9,... | collective-permute-start | bytes 20 | tf_op jit(solution)/shard_map/ppermute | solution.py:451
  28.9 1.4 %collective-permute-done.refs_10_ = f32[80,1024]{1,0:T(8,128)S(1)} collective-permute-done((f32[80,1024]{1,0:T(8,128)S(1)}, f32[80,1024]{1,0:T(8,128)S(1)}, u32[]{:S(2)}, u32[]{:S(2)}) %collective-permute-start) | collective-permute-done | bytes 327712 | tf_op jit(solution)/shard_map/ppermute | solution.py:451
  30.2 0.0 collective-permute-start.8
  30.3 0.9 %collective-permute-done.3.refs_1_ = f32[1]{0:T(128)} collective-permute-done((f32[1]{0:T(128)}, f32[1]{0:T(128)}, u32[]{:S(2)}, u32[]{:S(2)}) %collective-permute-start.3) | collective-permute-done | bytes 36 | tf_op jit(solution)/shard_map/ppermute | solution.py:451
  31.1 0.0 collective-permute-start.4
  31.1 0.0 collective-permute-done.15.refs_15_
  31.1 0.5 collective-permute-start.9
  31.7 2.1 %collective-permute-done.10.refs_12_ = f32[80,1024]{1,0:T(8,128)S(1)} collective-permute-done((f32[80,1024]{1,0:T(8,128)S(1)}, f32[80,1024]{1,0:T(8,128)S(1)}, u32[]{:S(2)}, u32[]{:S(2)}) %collective-permute-start.10) | collective-permute-done | bytes 327712 | tf_op jit(solution)/shard_map/ppermute | solution.py:451
  33.8 0.0 collective-permute-done.6.refs_4_
  33.8 0.5 collective-permute-start.7
  34.9 0.0 collective-permute-done.8.refs_9_
  34.9 0.0 collective-permute-done.4.refs_3_
  35.0 0.4 collective-permute-done.11.refs_13_
  35.4 0.5 collective-permute-done.7.refs_5_
  35.9 16.5 %evolve.1 = (f32[64,1024]{1,0:T(8,128)S(1)}, f32[64,1024]{1,0:T(8,128)S(1)}, f32[64,1024]{1,0:T(8,128)S(1)}, f32[64,1024]{1,0:T(8,128)S(1)}, f32[2,128]{1,0:T(2,128)S(1)}) custom-call(f32[1]{0:T(128)S(6)} %copy.13.refs_0_, f32[1]{0:T(128)} %collective-permute-done.3.refs_1_, f32[80,1024]{1,0:T(8,128)S(1)} %collective-permute-done.1.refs_2_, ...), custom_call_target="tpu_custom_call" | custom-call | tf_op jit(solution)/shard_map/evolve/pallas_call | solution.py:507
  52.3 0.1 collective-permute-start.16
  52.4 1.6 %collective-permute-start.17 = (f32[64,1024]{1,0:T(8,128)S(1)}, f32[64,1024]{1,0:T(8,128)S(1)}, u32[]{:S(2)}, u32[]{:S(2)}) collective-permute-start(f32[64,1024]{1,0:T(8,128)S(1)} %get-tuple-element.28), channel_id=1, source_target_pairs={{0,16},{1,17},{2,18},{3,19},{4,20},{5,21},{6,22},{7,23},{8,24},{9,... | collective-permute-start | bytes 786440 | tf_op jit(solution)/shard_map/ppermute | solution.py:451
  54.0 1.9 %collective-permute-start.18 = (f32[64,1024]{1,0:T(8,128)S(1)}, f32[64,1024]{1,0:T(8,128)S(1)}, u32[]{:S(2)}, u32[]{:S(2)}) collective-permute-start(f32[64,1024]{1,0:T(8,128)S(1)} %get-tuple-element.29), channel_id=1, source_target_pairs={{0,18},{1,19},{2,16},{3,17},{4,22},{5,23},{6,20},{7,21},{8,26},{9,... | collective-permute-start | bytes 786440 | tf_op jit(solution)/shard_map/ppermute | solution.py:451
  55.9 13.0 %all_to_all.5 = f32[32,1,256]{2,1,0:T(1,128)S(1)} all-to-all(f32[32,1,256]{2,1,0:T(1,128)S(1)} %broadcast_in_dim.2), channel_id=1, replica_groups=mesh['pulse'=2,'grid'=16] {'pulse','grid'}, dimensions={0} | all-to-all | bytes 65536 | tf_op jit(solution)/shard_map/all_to_all | solution.py:536
  69.0 0.2 collective-permute-start.19
  69.1 0.4 collective-permute-start.20
  69.5 0.1 collective-permute-start.21
  69.6 0.4 collective-permute-start.22
  70.0 0.6 slice_reduce_fusion
  72.0 0.0 collective-permute-done.20.refs_3_
  72.0 1.5 %unpack.1 = f32[1024,256]{1,0:T(8,128)} custom-call(f32[64,1024]{1,0:T(8,128)S(1)} %get-tuple-element.31.refs_0_, f32[64,1024]{1,0:T(8,128)S(1)} %collective-permute-done.19.refs_1_, f32[64,1024]{1,0:T(8,128)S(1)} %collective-permute-done.16.refs_2_, f32[64,1024]{1,0:T(8,128)S(1)} %collective-permute-done.20.refs_3_, ...), custom_call_target="tpu_custom_call" | custom-call | tf_op jit(solution)/shard_map/unpack/pallas_call | solution.py:541
  (18 shorter events, 0.1 us)
Async XLA Ops:
  0.6 0.7 copy-start.4
  1.3 1.2 %copy-start = (f32[1,32,32,256]{3,2,1,0:T(8,128)S(1)}, f32[1,32,32,256]{3,2,1,0:T(8,128)}, u32[]{:S(2)}) copy-start(f32[1,32,32,256]{3,2,1,0:T(8,128)} %param.7) | copy-start | bytes 3145732
  2.5 0.8 %copy-start.1 = (bf16[16,8,256]{2,1,0:T(8,128)(2,1)S(1)}, bf16[16,8,256]{2,1,0:T(8,128)(2,1)}, u32[]{:S(2)}) copy-start(bf16[16,8,256]{2,1,0:T(8,128)(2,1)} %proj.3) | copy-start | bytes 196612
  3.4 0.7 copy-start.2
  4.1 0.7 copy-start.3
  5.4 11.1 %collective-permute-start.5 = (f32[80,1024]{1,0:T(8,128)S(1)}, f32[80,1024]{1,0:T(8,128)S(1)}, u32[]{:S(2)}, u32[]{:S(2)}) collective-permute-start(f32[80,1024]{1,0:T(8,128)S(1)} %get-tuple-element.23), channel_id=1, source_target_pairs={{0,2},{1,3},{2,0},{3,1},{4,6},{5,7},{6,4},{7,5},{8,10},{9,11},{10,... | collective-permute-start | bytes 983048 | tf_op jit(solution)/shard_map/ppermute | solution.py:451
  8.4 5.4 %collective-permute-start.14 = (f32[32,1024]{1,0:T(8,128)S(1)}, f32[32,1024]{1,0:T(8,128)S(1)}, u32[]{:S(2)}, u32[]{:S(2)}) collective-permute-start(f32[32,1024]{1,0:T(8,128)S(1)} %rest.1), channel_id=1, source_target_pairs={{1,7},{14,8},{17,23},{30,24}} | collective-permute-start | bytes 393224 | tf_op jit(solution)/shard_map/ppermute | solution.py:451
  9.1 6.1 %collective-permute-start.13 = (f32[32,1024]{1,0:T(8,128)S(1)}, f32[32,1024]{1,0:T(8,128)S(1)}, u32[]{:S(2)}, u32[]{:S(2)}) collective-permute-start(f32[32,1024]{1,0:T(8,128)S(1)} %rest.1), channel_id=1, source_target_pairs={{1,5},{14,10},{17,21},{30,26}} | collective-permute-start | bytes 393224 | tf_op jit(solution)/shard_map/ppermute | solution.py:451
  9.8 8.4 %collective-permute-start.12 = (f32[32,1024]{1,0:T(8,128)S(1)}, f32[32,1024]{1,0:T(8,128)S(1)}, u32[]{:S(2)}, u32[]{:S(2)}) collective-permute-start(f32[32,1024]{1,0:T(8,128)S(1)} %rest.1), channel_id=1, source_target_pairs={{0,2},{1,3},{14,12},{15,13},{16,18},{17,19},{30,28},{31,29}} | collective-permute-start | bytes 393224 | tf_op jit(solution)/shard_map/ppermute | solution.py:451
  11.7 15.5 %collective-permute-start.2 = (f32[80,1024]{1,0:T(8,128)S(1)}, f32[80,1024]{1,0:T(8,128)S(1)}, u32[]{:S(2)}, u32[]{:S(2)}) collective-permute-start(f32[80,1024]{1,0:T(8,128)S(1)} %get-tuple-element.19.near.refs_6_), channel_id=1, source_target_pairs={{0,1},{1,0},{2,3},{3,2},{4,5},{5,4},{6,7},{7,6},{8,9},{9,8},{10,11... | collective-permute-start | bytes 983048 | tf_op jit(solution)/shard_map/ppermute | solution.py:451
  13.8 13.5 %collective-permute-start.1 = (f32[80,1024]{1,0:T(8,128)S(1)}, f32[80,1024]{1,0:T(8,128)S(1)}, u32[]{:S(2)}, u32[]{:S(2)}) collective-permute-start(f32[80,1024]{1,0:T(8,128)S(1)} %get-tuple-element.19.near.refs_6_), channel_id=1, source_target_pairs={{0,4},{1,5},{2,6},{3,7},{4,8},{5,9},{6,10},{7,11},{8,12},{9,13},{1... | collective-permute-start | bytes 983048 | tf_op jit(solution)/shard_map/ppermute | solution.py:451
  15.2 15.1 %collective-permute-start = (f32[80,1024]{1,0:T(8,128)S(1)}, f32[80,1024]{1,0:T(8,128)S(1)}, u32[]{:S(2)}, u32[]{:S(2)}) collective-permute-start(f32[80,1024]{1,0:T(8,128)S(1)} %get-tuple-element.19.near.refs_6_), channel_id=1, source_target_pairs={{4,0},{5,1},{6,2},{7,3},{8,4},{9,5},{10,6},{11,7},{12,8},{13,9},{1... | collective-permute-start | bytes 983048 | tf_op jit(solution)/shard_map/ppermute | solution.py:451
  16.5 17.2 %collective-permute-start.10 = (f32[80,1024]{1,0:T(8,128)S(1)}, f32[80,1024]{1,0:T(8,128)S(1)}, u32[]{:S(2)}, u32[]{:S(2)}) collective-permute-start(f32[80,1024]{1,0:T(8,128)S(1)} %collective-permute-done.5.refs_8_), channel_id=1, source_target_pairs={{4,0},{5,1},{6,2},{7,3},{8,4},{9,5},{10,6},{11,7},{12,8},{13,9},{1... | collective-permute-start | bytes 983048 | tf_op jit(solution)/shard_map/ppermute | solution.py:451
  18.2 15.6 %collective-permute-start.6 = (f32[80,1024]{1,0:T(8,128)S(1)}, f32[80,1024]{1,0:T(8,128)S(1)}, u32[]{:S(2)}, u32[]{:S(2)}) collective-permute-start(f32[80,1024]{1,0:T(8,128)S(1)} %collective-permute-done.5.refs_8_), channel_id=1, source_target_pairs={{0,4},{1,5},{2,6},{3,7},{4,8},{5,9},{6,10},{7,11},{8,12},{9,13},{1... | collective-permute-start | bytes 983048 | tf_op jit(solution)/shard_map/ppermute | solution.py:451
  27.2 3.9 %collective-permute-start.15 = (f32[32,1024]{1,0:T(8,128)S(1)}, f32[32,1024]{1,0:T(8,128)S(1)}, u32[]{:S(2)}, u32[]{:S(2)}) collective-permute-start(f32[32,1024]{1,0:T(8,128)S(1)} %add_select_fusion.refs_14_), channel_id=1, source_target_pairs={{0,1},{1,0},{2,3},{3,2},{4,5},{5,4},{6,7},{7,6},{8,9},{9,8},{10,11... | collective-permute-start | bytes 393224 | tf_op jit(solution)/shard_map/ppermute | solution.py:451
  27.3 3.8 %collective-permute-start.3 = (f32[1]{0:T(128)}, f32[1]{0:T(128)}, u32[]{:S(2)}, u32[]{:S(2)}) collective-permute-start(f32[1]{0:T(128)} %param.9), channel_id=1, source_target_pairs={{0,16},{1,17},{2,18},{3,19},{4,20},{5,21},{6,22},{7,23},{8,24},{9,... | collective-permute-start | bytes 20 | tf_op jit(solution)/shard_map/ppermute | solution.py:451
  30.2 4.7 %collective-permute-start.8 = (f32[80,1024]{1,0:T(8,128)S(1)}, f32[80,1024]{1,0:T(8,128)S(1)}, u32[]{:S(2)}, u32[]{:S(2)}) collective-permute-start(f32[80,1024]{1,0:T(8,128)S(1)} %collective-permute-done.5.refs_8_), channel_id=1, source_target_pairs={{0,1},{1,0},{2,3},{3,2},{4,5},{5,4},{6,7},{7,6},{8,9},{9,8},{10,11... | collective-permute-start | bytes 983048 | tf_op jit(solution)/shard_map/ppermute | solution.py:451
  31.1 3.8 %collective-permute-start.4 = (f32[80,1024]{1,0:T(8,128)S(1)}, f32[80,1024]{1,0:T(8,128)S(1)}, u32[]{:S(2)}, u32[]{:S(2)}) collective-permute-start(f32[80,1024]{1,0:T(8,128)S(1)} %collective-permute-done.1.refs_2_), channel_id=1, source_target_pairs={{0,1},{1,0},{2,3},{3,2},{4,5},{5,4},{6,7},{7,6},{8,9},{9,8},{10,11... | collective-permute-start | bytes 983048 | tf_op jit(solution)/shard_map/ppermute | solution.py:451
  31.1 3.8 %collective-permute-start.9 = (f32[80,1024]{1,0:T(8,128)S(1)}, f32[80,1024]{1,0:T(8,128)S(1)}, u32[]{:S(2)}, u32[]{:S(2)}) collective-permute-start(f32[80,1024]{1,0:T(8,128)S(1)} %collective-permute-done.refs_10_), channel_id=1, source_target_pairs={{0,1},{1,0},{2,3},{3,2},{4,5},{5,4},{6,7},{7,6},{8,9},{9,8},{10,11... | collective-permute-start | bytes 983048 | tf_op jit(solution)/shard_map/ppermute | solution.py:451
  33.8 1.6 %collective-permute-start.11 = (f32[80,1024]{1,0:T(8,128)S(1)}, f32[80,1024]{1,0:T(8,128)S(1)}, u32[]{:S(2)}, u32[]{:S(2)}) collective-permute-start(f32[80,1024]{1,0:T(8,128)S(1)} %collective-permute-done.10.refs_12_), channel_id=1, source_target_pairs={{0,1},{1,0},{2,3},{3,2},{4,5},{5,4},{6,7},{7,6},{8,9},{9,8},{10,11... | collective-permute-start | bytes 983048 | tf_op jit(solution)/shard_map/ppermute | solution.py:451
  33.8 2.1 %collective-permute-start.7 = (f32[80,1024]{1,0:T(8,128)S(1)}, f32[80,1024]{1,0:T(8,128)S(1)}, u32[]{:S(2)}, u32[]{:S(2)}) collective-permute-start(f32[80,1024]{1,0:T(8,128)S(1)} %collective-permute-done.6.refs_4_), channel_id=1, source_target_pairs={{0,1},{1,0},{2,3},{3,2},{4,5},{5,4},{6,7},{7,6},{8,9},{9,8},{10,11... | collective-permute-start | bytes 983048 | tf_op jit(solution)/shard_map/ppermute | solution.py:451
  52.3 16.6 %collective-permute-start.16 = (f32[64,1024]{1,0:T(8,128)S(1)}, f32[64,1024]{1,0:T(8,128)S(1)}, u32[]{:S(2)}, u32[]{:S(2)}) collective-permute-start(f32[64,1024]{1,0:T(8,128)S(1)} %get-tuple-element.27), channel_id=1, source_target_pairs={{0,2},{1,3},{2,0},{3,1},{4,6},{5,7},{6,4},{7,5},{8,10},{9,11},{10,... | collective-permute-start | bytes 786440 | tf_op jit(solution)/shard_map/ppermute | solution.py:451
  52.4 16.6 %collective-permute-start.17 = (f32[64,1024]{1,0:T(8,128)S(1)}, f32[64,1024]{1,0:T(8,128)S(1)}, u32[]{:S(2)}, u32[]{:S(2)}) collective-permute-start(f32[64,1024]{1,0:T(8,128)S(1)} %get-tuple-element.28), channel_id=1, source_target_pairs={{0,16},{1,17},{2,18},{3,19},{4,20},{5,21},{6,22},{7,23},{8,24},{9,... | collective-permute-start | bytes 786440 | tf_op jit(solution)/shard_map/ppermute | solution.py:451
  54.0 15.0 %collective-permute-start.18 = (f32[64,1024]{1,0:T(8,128)S(1)}, f32[64,1024]{1,0:T(8,128)S(1)}, u32[]{:S(2)}, u32[]{:S(2)}) collective-permute-start(f32[64,1024]{1,0:T(8,128)S(1)} %get-tuple-element.29), channel_id=1, source_target_pairs={{0,18},{1,19},{2,16},{3,17},{4,22},{5,23},{6,20},{7,21},{8,26},{9,... | collective-permute-start | bytes 786440 | tf_op jit(solution)/shard_map/ppermute | solution.py:451
  69.0 3.0 %collective-permute-start.19 = (f32[64,1024]{1,0:T(8,128)S(1)}, f32[64,1024]{1,0:T(8,128)S(1)}, u32[]{:S(2)}, u32[]{:S(2)}) collective-permute-start(f32[64,1024]{1,0:T(8,128)S(1)} %get-tuple-element.31.refs_0_), channel_id=1, source_target_pairs={{0,1},{1,0},{2,3},{3,2},{4,5},{5,4},{6,7},{7,6},{8,9},{9,8},{10,11... | collective-permute-start | bytes 786440 | tf_op jit(solution)/shard_map/ppermute | solution.py:451
  69.1 2.9 %collective-permute-start.20 = (f32[64,1024]{1,0:T(8,128)S(1)}, f32[64,1024]{1,0:T(8,128)S(1)}, u32[]{:S(2)}, u32[]{:S(2)}) collective-permute-start(f32[64,1024]{1,0:T(8,128)S(1)} %collective-permute-done.16.refs_2_), channel_id=1, source_target_pairs={{0,1},{1,0},{2,3},{3,2},{4,5},{5,4},{6,7},{7,6},{8,9},{9,8},{10,11... | collective-permute-start | bytes 786440 | tf_op jit(solution)/shard_map/ppermute | solution.py:451
  69.5 2.5 %collective-permute-start.21 = (f32[64,1024]{1,0:T(8,128)S(1)}, f32[64,1024]{1,0:T(8,128)S(1)}, u32[]{:S(2)}, u32[]{:S(2)}) collective-permute-start(f32[64,1024]{1,0:T(8,128)S(1)} %collective-permute-done.17.refs_4_), channel_id=1, source_target_pairs={{0,1},{1,0},{2,3},{3,2},{4,5},{5,4},{6,7},{7,6},{8,9},{9,8},{10,11... | collective-permute-start | bytes 786440 | tf_op jit(solution)/shard_map/ppermute | solution.py:451
  69.6 2.4 %collective-permute-start.22 = (f32[64,1024]{1,0:T(8,128)S(1)}, f32[64,1024]{1,0:T(8,128)S(1)}, u32[]{:S(2)}, u32[]{:S(2)}) collective-permute-start(f32[64,1024]{1,0:T(8,128)S(1)} %collective-permute-done.18.refs_6_), channel_id=1, source_target_pairs={{0,1},{1,0},{2,3},{3,2},{4,5},{5,4},{6,7},{7,6},{8,9},{9,8},{10,11... | collective-permute-start | bytes 786440 | tf_op jit(solution)/shard_map/ppermute | solution.py:451

commit v5 on v3

--- a/solution.py
+++ b/solution.py
@@ -387,10 +387,10 @@
             v = total[slot, :, columns(j)]
             squares += v * v
         shares += position * squares
-    for p in range(2):
-        rows = slice(p * part, (p + 1) * part)
-        value = jnp.sum(shares[rows] + shares[slice((2 + p) * part, (3 + p) * part)])
-        moment[p : p + 1, :] = jnp.full((1, 128), value, F32)
+    values = [
+        jnp.sum(shares[p * part : (p + 1) * part] + shares[(2 + p) * part : (3 + p) * part]) for p in range(2)
+    ]
+    moment[...] = jnp.where(iota(moment.shape, 2) < 64, values[0], values[1])
     for number, out in enumerate(outs):
         yy = y if number // 2 == 0 else 1 - y
         xx = x if number % 2 == 0 else 1 - x
@@ -503,7 +503,7 @@
 
     outs = pl.pallas_call(
         functools.partial(evolve_kernel, slabs, shared_heavy),
-        out_shape=[jax.ShapeDtypeStruct((4 * part, cells), F32)] * 4 + [jax.ShapeDtypeStruct((2, 128), F32)],
+        out_shape=[jax.ShapeDtypeStruct((4 * part, cells), F32)] * 4 + [jax.ShapeDtypeStruct((2 * slabs, 1, 128), F32)],
         in_specs=[SMEM] * 2 + [VMEM] * (12 + len(heavies)),
         out_specs=[VMEM] * 5,
         scratch_shapes=[pltpu.VMEM((SLOTS, 2 * part, cells), F32)]
@@ -528,9 +528,7 @@
         permute(outs[2], lambda p, s: (1 - p, s)),
         permute(outs[3], lambda p, s: (1 - p, s ^ 2)),
     ]
-    devices = 2 * slabs
-    shares = jnp.broadcast_to(jnp.concatenate([moment[0], moment[1]])[None, None, :], (devices, 1, 256))
-    shares = lax.all_to_all(shares, BOTH, 0, 0)
+    shares = lax.all_to_all(moment, BOTH, 0, 0)
     *finals, shares = lax.optimization_barrier((*finals, shares))
     pieces = []
     for piece in finals:
@@ -545,7 +543,7 @@
         name="unpack",
     )(*pieces)
 
-    total = jnp.where(y == 0, jnp.sum(shares[:, 0, 0]), jnp.sum(shares[:, 0, 128]))
+    total = jnp.where(y == 0, jnp.sum(shares[:, 0, 0]), jnp.sum(shares[:, 0, 64]))
     dipole = total / (slabs * cells * (channels // 2))
     return plane.reshape(orbitals.shape), dipole.reshape(1)
 

time: 75.3 us -> 75.4 us (level)
  no operation moved by 1% of the time
where the time goes in v5:
time: 75.4 us; the launch traced here: 74.8 us
  starting transfers between devices  28.5 us (38%)
  Pallas kernels  18.8 us (25%)
  blocking collectives  13 us (17%)
  waiting for transfers between devices  5.74 us (8%)
  between operations  4.58 us (6%)
  local copies, waits for them, and re-layouts  3.52 us (5%)
    ppermute x23, starting transfers between devices, permute(): return lax.ppermute(value, BOTH, pairs)  28.5 us
    pallas_call x1, Pallas kernels, local(): pl.pallas_call(functools.partial(evolve_kernel, slabs, shared_heavy), out...  16.7 us
    all_to_all x1, blocking collectives, local(): shares = lax.all_to_all(moment, BOTH, 0, 0)  13 us
    ppermute x23, waiting for transfers between devices, permute(): return lax.ppermute(value, BOTH, pairs)  5.74 us
    unnamed x10, local copies, waits for them, and re-layouts  3.52 us
  transfers between devices with their start and end apart: 23, of which 7 were waited for; matrix products, arithmetic and copies ran while one was open for 1% of the time, Pallas kernels for 0%

profile of v5, /device:TPU:0, one launch (start us, length us, event | category | flops | bytes accessed | tf_op | source)
XLA Modules:
  0.0 74.8 jit_solution(13742147612444039925)
XLA Ops:
  1.3 0.0 copy-done.4
  1.3 1.2 %copy-done = f32[1,32,32,256]{3,2,1,0:T(8,128)S(1)} copy-done((f32[1,32,32,256]{3,2,1,0:T(8,128)S(1)}, f32[1,32,32,256]{3,2,1,0:T(8,128)}, u32[]{:S(2)}) %copy-start) | copy-done | bytes 1048600
  2.5 0.8 %copy-done.1 = bf16[16,8,256]{2,1,0:T(8,128)(2,1)S(1)} copy-done((bf16[16,8,256]{2,1,0:T(8,128)(2,1)S(1)}, bf16[16,8,256]{2,1,0:T(8,128)(2,1)}, u32[]{:S(2)}) %copy-start.1) | copy-done | bytes 65560
  3.4 0.7 copy-done.2
  4.1 0.7 copy-done.3
  4.8 0.6 pack.1
  5.4 3.0 %collective-permute-start.5 = (f32[80,1024]{1,0:T(8,128)S(1)}, f32[80,1024]{1,0:T(8,128)S(1)}, u32[]{:S(2)}, u32[]{:S(2)}) collective-permute-start(f32[80,1024]{1,0:T(8,128)S(1)} %get-tuple-element.23), channel_id=1, source_target_pairs={{0,2},{1,3},{2,0},{3,1},{4,6},{5,7},{6,4},{7,5},{8,10},{9,11},{10,... | collective-permute-start | bytes 983048 | tf_op jit(solution)/shard_map/ppermute | solution.py:448
  8.4 0.7 collective-permute-start.14
  9.1 0.7 collective-permute-start.13
  9.8 1.9 %collective-permute-start.12 = (f32[32,1024]{1,0:T(8,128)S(1)}, f32[32,1024]{1,0:T(8,128)S(1)}, u32[]{:S(2)}, u32[]{:S(2)}) collective-permute-start(f32[32,1024]{1,0:T(8,128)S(1)} %rest.1), channel_id=1, source_target_pairs={{0,2},{1,3},{14,12},{15,13},{16,18},{17,19},{30,28},{31,29}} | collective-permute-start | bytes 393224 | tf_op jit(solution)/shard_map/ppermute | solution.py:448
  11.7 2.1 %collective-permute-start.2 = (f32[80,1024]{1,0:T(8,128)S(1)}, f32[80,1024]{1,0:T(8,128)S(1)}, u32[]{:S(2)}, u32[]{:S(2)}) collective-permute-start(f32[80,1024]{1,0:T(8,128)S(1)} %get-tuple-element.19.near.refs_6_), channel_id=1, source_target_pairs={{0,1},{1,0},{2,3},{3,2},{4,5},{5,4},{6,7},{7,6},{8,9},{9,8},{10,11... | collective-permute-start | bytes 983048 | tf_op jit(solution)/shard_map/ppermute | solution.py:448
  13.8 0.0 collective-permute-done.14
  13.8 1.3 %collective-permute-start.1 = (f32[80,1024]{1,0:T(8,128)S(1)}, f32[80,1024]{1,0:T(8,128)S(1)}, u32[]{:S(2)}, u32[]{:S(2)}) collective-permute-start(f32[80,1024]{1,0:T(8,128)S(1)} %get-tuple-element.19.near.refs_6_), channel_id=1, source_target_pairs={{0,4},{1,5},{2,6},{3,7},{4,8},{5,9},{6,10},{7,11},{8,12},{9,13},{1... | collective-permute-start | bytes 983048 | tf_op jit(solution)/shard_map/ppermute | solution.py:448
  15.1 0.0 collective-permute-done.13
  15.2 1.3 %collective-permute-start = (f32[80,1024]{1,0:T(8,128)S(1)}, f32[80,1024]{1,0:T(8,128)S(1)}, u32[]{:S(2)}, u32[]{:S(2)}) collective-permute-start(f32[80,1024]{1,0:T(8,128)S(1)} %get-tuple-element.19.near.refs_6_), channel_id=1, source_target_pairs={{4,0},{5,1},{6,2},{7,3},{8,4},{9,5},{10,6},{11,7},{12,8},{13,9},{1... | collective-permute-start | bytes 983048 | tf_op jit(solution)/shard_map/ppermute | solution.py:448
  16.4 0.1 collective-permute-done.5.refs_8_
  16.5 1.3 %collective-permute-start.10 = (f32[80,1024]{1,0:T(8,128)S(1)}, f32[80,1024]{1,0:T(8,128)S(1)}, u32[]{:S(2)}, u32[]{:S(2)}) collective-permute-start(f32[80,1024]{1,0:T(8,128)S(1)} %collective-permute-done.5.refs_8_), channel_id=1, source_target_pairs={{4,0},{5,1},{6,2},{7,3},{8,4},{9,5},{10,6},{11,7},{12,8},{13,9},{1... | collective-permute-start | bytes 983048 | tf_op jit(solution)/shard_map/ppermute | solution.py:448
  17.8 0.4 collective-permute-done.12
  18.2 9.0 %collective-permute-start.6 = (f32[80,1024]{1,0:T(8,128)S(1)}, f32[80,1024]{1,0:T(8,128)S(1)}, u32[]{:S(2)}, u32[]{:S(2)}) collective-permute-start(f32[80,1024]{1,0:T(8,128)S(1)} %collective-permute-done.5.refs_8_), channel_id=1, source_target_pairs={{0,4},{1,5},{2,6},{3,7},{4,8},{5,9},{6,10},{7,11},{8,12},{9,13},{1... | collective-permute-start | bytes 983048 | tf_op jit(solution)/shard_map/ppermute | solution.py:448
  27.2 0.0 collective-permute-done.2.refs_7_
  27.2 0.1 collective-permute-start.15
  27.3 0.0 collective-permute-done.1.refs_2_
  27.3 1.6 %collective-permute-start.3 = (f32[1]{0:T(128)}, f32[1]{0:T(128)}, u32[]{:S(2)}, u32[]{:S(2)}) collective-permute-start(f32[1]{0:T(128)} %param.9), channel_id=1, source_target_pairs={{0,16},{1,17},{2,18},{3,19},{4,20},{5,21},{6,22},{7,23},{8,24},{9,... | collective-permute-start | bytes 20 | tf_op jit(solution)/shard_map/ppermute | solution.py:448
  28.9 1.4 %collective-permute-done.refs_10_ = f32[80,1024]{1,0:T(8,128)S(1)} collective-permute-done((f32[80,1024]{1,0:T(8,128)S(1)}, f32[80,1024]{1,0:T(8,128)S(1)}, u32[]{:S(2)}, u32[]{:S(2)}) %collective-permute-start) | collective-permute-done | bytes 327712 | tf_op jit(solution)/shard_map/ppermute | solution.py:448
  30.2 0.0 collective-permute-start.8
  30.3 0.7 collective-permute-done.3.refs_1_
  31.0 0.0 collective-permute-start.4
  31.0 0.0 collective-permute-done.15.refs_15_
  31.0 0.5 collective-permute-start.9
  31.5 2.3 %collective-permute-done.10.refs_12_ = f32[80,1024]{1,0:T(8,128)S(1)} collective-permute-done((f32[80,1024]{1,0:T(8,128)S(1)}, f32[80,1024]{1,0:T(8,128)S(1)}, u32[]{:S(2)}, u32[]{:S(2)}) %collective-permute-start.10) | collective-permute-done | bytes 327712 | tf_op jit(solution)/shard_map/ppermute | solution.py:448
  33.8 0.5 collective-permute-start.7
  34.9 0.0 collective-permute-done.8.refs_9_
  35.0 0.4 collective-permute-done.11.refs_13_
  35.4 0.5 collective-permute-done.7.refs_5_
  35.9 16.7 %evolve.1 = (f32[64,1024]{1,0:T(8,128)S(1)}, f32[64,1024]{1,0:T(8,128)S(1)}, f32[64,1024]{1,0:T(8,128)S(1)}, f32[64,1024]{1,0:T(8,128)S(1)}, f32[32,1,128]{2,1,0:T(1,128)S(1)}) custom-call(f32[1]{0:T(128)S(6)} %copy.9.refs_0_, f32[1]{0:T(128)} %collective-permute-done.3.refs_1_, f32[80,1024]{1,0:T(8,128)S(1)} %collective-permute-done.1.refs_2_, ...), custom_call_target="tpu_custom_call" | custom-call | tf_op jit(solution)/shard_map/evolve/pallas_call | solution.py:504
  52.5 0.1 collective-permute-start.16
  52.6 1.6 %collective-permute-start.17 = (f32[64,1024]{1,0:T(8,128)S(1)}, f32[64,1024]{1,0:T(8,128)S(1)}, u32[]{:S(2)}, u32[]{:S(2)}) collective-permute-start(f32[64,1024]{1,0:T(8,128)S(1)} %get-tuple-element.28), channel_id=1, source_target_pairs={{0,16},{1,17},{2,18},{3,19},{4,20},{5,21},{6,22},{7,23},{8,24},{9,... | collective-permute-start | bytes 786440 | tf_op jit(solution)/shard_map/ppermute | solution.py:448
  54.2 1.9 %collective-permute-start.18 = (f32[64,1024]{1,0:T(8,128)S(1)}, f32[64,1024]{1,0:T(8,128)S(1)}, u32[]{:S(2)}, u32[]{:S(2)}) collective-permute-start(f32[64,1024]{1,0:T(8,128)S(1)} %get-tuple-element.29), channel_id=1, source_target_pairs={{0,18},{1,19},{2,16},{3,17},{4,22},{5,23},{6,20},{7,21},{8,26},{9,... | collective-permute-start | bytes 786440 | tf_op jit(solution)/shard_map/ppermute | solution.py:448
  56.1 13.0 %all_to_all.5 = f32[32,1,128]{2,1,0:T(1,128)S(1)} all-to-all(f32[32,1,128]{2,1,0:T(1,128)S(1)} %get-tuple-element.30), channel_id=1, replica_groups=mesh['pulse'=2,'grid'=16] {'pulse','grid'}, dimensions={0} | all-to-all | bytes 32768 | tf_op jit(solution)/shard_map/all_to_all | solution.py:531
  69.1 0.1 collective-permute-start.19
  69.2 0.5 collective-permute-start.20
  69.7 0.1 collective-permute-start.21
  69.7 0.4 collective-permute-start.22
  70.2 0.7 slice_reduce_fusion
  72.2 0.0 collective-permute-done.19.refs_1_
  72.2 0.0 collective-permute-done.20.refs_3_
  72.2 0.0 collective-permute-done.22.refs_7_
  72.2 1.5 %unpack.1 = f32[1024,256]{1,0:T(8,128)} custom-call(f32[64,1024]{1,0:T(8,128)S(1)} %get-tuple-element.31.refs_0_, f32[64,1024]{1,0:T(8,128)S(1)} %collective-permute-done.19.refs_1_, f32[64,1024]{1,0:T(8,128)S(1)} %collective-permute-done.16.refs_2_, f32[64,1024]{1,0:T(8,128)S(1)} %collective-permute-done.20.refs_3_, ...), custom_call_target="tpu_custom_call" | custom-call | tf_op jit(solution)/shard_map/unpack/pallas_call | solution.py:536
  (15 shorter events, 0.1 us)
Async XLA Ops:
  0.6 0.7 copy-start.4
  1.3 1.2 %copy-start = (f32[1,32,32,256]{3,2,1,0:T(8,128)S(1)}, f32[1,32,32,256]{3,2,1,0:T(8,128)}, u32[]{:S(2)}) copy-start(f32[1,32,32,256]{3,2,1,0:T(8,128)} %param.7) | copy-start | bytes 3145732
  2.5 0.8 %copy-start.1 = (bf16[16,8,256]{2,1,0:T(8,128)(2,1)S(1)}, bf16[16,8,256]{2,1,0:T(8,128)(2,1)}, u32[]{:S(2)}) copy-start(bf16[16,8,256]{2,1,0:T(8,128)(2,1)} %proj.3) | copy-start | bytes 196612
  3.4 0.7 copy-start.2
  4.1 0.7 copy-start.3
  5.4 11.1 %collective-permute-start.5 = (f32[80,1024]{1,0:T(8,128)S(1)}, f32[80,1024]{1,0:T(8,128)S(1)}, u32[]{:S(2)}, u32[]{:S(2)}) collective-permute-start(f32[80,1024]{1,0:T(8,128)S(1)} %get-tuple-element.23), channel_id=1, source_target_pairs={{0,2},{1,3},{2,0},{3,1},{4,6},{5,7},{6,4},{7,5},{8,10},{9,11},{10,... | collective-permute-start | bytes 983048 | tf_op jit(solution)/shard_map/ppermute | solution.py:448
  8.4 5.4 %collective-permute-start.14 = (f32[32,1024]{1,0:T(8,128)S(1)}, f32[32,1024]{1,0:T(8,128)S(1)}, u32[]{:S(2)}, u32[]{:S(2)}) collective-permute-start(f32[32,1024]{1,0:T(8,128)S(1)} %rest.1), channel_id=1, source_target_pairs={{1,7},{14,8},{17,23},{30,24}} | collective-permute-start | bytes 393224 | tf_op jit(solution)/shard_map/ppermute | solution.py:448
  9.1 6.1 %collective-permute-start.13 = (f32[32,1024]{1,0:T(8,128)S(1)}, f32[32,1024]{1,0:T(8,128)S(1)}, u32[]{:S(2)}, u32[]{:S(2)}) collective-permute-start(f32[32,1024]{1,0:T(8,128)S(1)} %rest.1), channel_id=1, source_target_pairs={{1,5},{14,10},{17,21},{30,26}} | collective-permute-start | bytes 393224 | tf_op jit(solution)/shard_map/ppermute | solution.py:448
  9.8 8.4 %collective-permute-start.12 = (f32[32,1024]{1,0:T(8,128)S(1)}, f32[32,1024]{1,0:T(8,128)S(1)}, u32[]{:S(2)}, u32[]{:S(2)}) collective-permute-start(f32[32,1024]{1,0:T(8,128)S(1)} %rest.1), channel_id=1, source_target_pairs={{0,2},{1,3},{14,12},{15,13},{16,18},{17,19},{30,28},{31,29}} | collective-permute-start | bytes 393224 | tf_op jit(solution)/shard_map/ppermute | solution.py:448
  11.7 15.5 %collective-permute-start.2 = (f32[80,1024]{1,0:T(8,128)S(1)}, f32[80,1024]{1,0:T(8,128)S(1)}, u32[]{:S(2)}, u32[]{:S(2)}) collective-permute-start(f32[80,1024]{1,0:T(8,128)S(1)} %get-tuple-element.19.near.refs_6_), channel_id=1, source_target_pairs={{0,1},{1,0},{2,3},{3,2},{4,5},{5,4},{6,7},{7,6},{8,9},{9,8},{10,11... | collective-permute-start | bytes 983048 | tf_op jit(solution)/shard_map/ppermute | solution.py:448
  13.8 13.5 %collective-permute-start.1 = (f32[80,1024]{1,0:T(8,128)S(1)}, f32[80,1024]{1,0:T(8,128)S(1)}, u32[]{:S(2)}, u32[]{:S(2)}) collective-permute-start(f32[80,1024]{1,0:T(8,128)S(1)} %get-tuple-element.19.near.refs_6_), channel_id=1, source_target_pairs={{0,4},{1,5},{2,6},{3,7},{4,8},{5,9},{6,10},{7,11},{8,12},{9,13},{1... | collective-permute-start | bytes 983048 | tf_op jit(solution)/shard_map/ppermute | solution.py:448
  15.2 15.1 %collective-permute-start = (f32[80,1024]{1,0:T(8,128)S(1)}, f32[80,1024]{1,0:T(8,128)S(1)}, u32[]{:S(2)}, u32[]{:S(2)}) collective-permute-start(f32[80,1024]{1,0:T(8,128)S(1)} %get-tuple-element.19.near.refs_6_), channel_id=1, source_target_pairs={{4,0},{5,1},{6,2},{7,3},{8,4},{9,5},{10,6},{11,7},{12,8},{13,9},{1... | collective-permute-start | bytes 983048 | tf_op jit(solution)/shard_map/ppermute | solution.py:448
  16.5 17.2 %collective-permute-start.10 = (f32[80,1024]{1,0:T(8,128)S(1)}, f32[80,1024]{1,0:T(8,128)S(1)}, u32[]{:S(2)}, u32[]{:S(2)}) collective-permute-start(f32[80,1024]{1,0:T(8,128)S(1)} %collective-permute-done.5.refs_8_), channel_id=1, source_target_pairs={{4,0},{5,1},{6,2},{7,3},{8,4},{9,5},{10,6},{11,7},{12,8},{13,9},{1... | collective-permute-start | bytes 983048 | tf_op jit(solution)/shard_map/ppermute | solution.py:448
  18.2 15.6 %collective-permute-start.6 = (f32[80,1024]{1,0:T(8,128)S(1)}, f32[80,1024]{1,0:T(8,128)S(1)}, u32[]{:S(2)}, u32[]{:S(2)}) collective-permute-start(f32[80,1024]{1,0:T(8,128)S(1)} %collective-permute-done.5.refs_8_), channel_id=1, source_target_pairs={{0,4},{1,5},{2,6},{3,7},{4,8},{5,9},{6,10},{7,11},{8,12},{9,13},{1... | collective-permute-start | bytes 983048 | tf_op jit(solution)/shard_map/ppermute | solution.py:448
  27.2 3.8 %collective-permute-start.15 = (f32[32,1024]{1,0:T(8,128)S(1)}, f32[32,1024]{1,0:T(8,128)S(1)}, u32[]{:S(2)}, u32[]{:S(2)}) collective-permute-start(f32[32,1024]{1,0:T(8,128)S(1)} %add_select_fusion.refs_14_), channel_id=1, source_target_pairs={{0,1},{1,0},{2,3},{3,2},{4,5},{5,4},{6,7},{7,6},{8,9},{9,8},{10,11... | collective-permute-start | bytes 393224 | tf_op jit(solution)/shard_map/ppermute | solution.py:448
  27.3 3.7 %collective-permute-start.3 = (f32[1]{0:T(128)}, f32[1]{0:T(128)}, u32[]{:S(2)}, u32[]{:S(2)}) collective-permute-start(f32[1]{0:T(128)} %param.9), channel_id=1, source_target_pairs={{0,16},{1,17},{2,18},{3,19},{4,20},{5,21},{6,22},{7,23},{8,24},{9,... | collective-permute-start | bytes 20 | tf_op jit(solution)/shard_map/ppermute | solution.py:448
  30.2 4.7 %collective-permute-start.8 = (f32[80,1024]{1,0:T(8,128)S(1)}, f32[80,1024]{1,0:T(8,128)S(1)}, u32[]{:S(2)}, u32[]{:S(2)}) collective-permute-start(f32[80,1024]{1,0:T(8,128)S(1)} %collective-permute-done.5.refs_8_), channel_id=1, source_target_pairs={{0,1},{1,0},{2,3},{3,2},{4,5},{5,4},{6,7},{7,6},{8,9},{9,8},{10,11... | collective-permute-start | bytes 983048 | tf_op jit(solution)/shard_map/ppermute | solution.py:448
  31.0 4.0 %collective-permute-start.4 = (f32[80,1024]{1,0:T(8,128)S(1)}, f32[80,1024]{1,0:T(8,128)S(1)}, u32[]{:S(2)}, u32[]{:S(2)}) collective-permute-start(f32[80,1024]{1,0:T(8,128)S(1)} %collective-permute-done.1.refs_2_), channel_id=1, source_target_pairs={{0,1},{1,0},{2,3},{3,2},{4,5},{5,4},{6,7},{7,6},{8,9},{9,8},{10,11... | collective-permute-start | bytes 983048 | tf_op jit(solution)/shard_map/ppermute | solution.py:448
  31.0 4.0 %collective-permute-start.9 = (f32[80,1024]{1,0:T(8,128)S(1)}, f32[80,1024]{1,0:T(8,128)S(1)}, u32[]{:S(2)}, u32[]{:S(2)}) collective-permute-start(f32[80,1024]{1,0:T(8,128)S(1)} %collective-permute-done.refs_10_), channel_id=1, source_target_pairs={{0,1},{1,0},{2,3},{3,2},{4,5},{5,4},{6,7},{7,6},{8,9},{9,8},{10,11... | collective-permute-start | bytes 983048 | tf_op jit(solution)/shard_map/ppermute | solution.py:448
  33.8 1.6 %collective-permute-start.11 = (f32[80,1024]{1,0:T(8,128)S(1)}, f32[80,1024]{1,0:T(8,128)S(1)}, u32[]{:S(2)}, u32[]{:S(2)}) collective-permute-start(f32[80,1024]{1,0:T(8,128)S(1)} %collective-permute-done.10.refs_12_), channel_id=1, source_target_pairs={{0,1},{1,0},{2,3},{3,2},{4,5},{5,4},{6,7},{7,6},{8,9},{9,8},{10,11... | collective-permute-start | bytes 983048 | tf_op jit(solution)/shard_map/ppermute | solution.py:448
  33.8 2.1 %collective-permute-start.7 = (f32[80,1024]{1,0:T(8,128)S(1)}, f32[80,1024]{1,0:T(8,128)S(1)}, u32[]{:S(2)}, u32[]{:S(2)}) collective-permute-start(f32[80,1024]{1,0:T(8,128)S(1)} %collective-permute-done.6.refs_4_), channel_id=1, source_target_pairs={{0,1},{1,0},{2,3},{3,2},{4,5},{5,4},{6,7},{7,6},{8,9},{9,8},{10,11... | collective-permute-start | bytes 983048 | tf_op jit(solution)/shard_map/ppermute | solution.py:448
  52.5 16.5 %collective-permute-start.16 = (f32[64,1024]{1,0:T(8,128)S(1)}, f32[64,1024]{1,0:T(8,128)S(1)}, u32[]{:S(2)}, u32[]{:S(2)}) collective-permute-start(f32[64,1024]{1,0:T(8,128)S(1)} %get-tuple-element.27), channel_id=1, source_target_pairs={{0,2},{1,3},{2,0},{3,1},{4,6},{5,7},{6,4},{7,5},{8,10},{9,11},{10,... | collective-permute-start | bytes 786440 | tf_op jit(solution)/shard_map/ppermute | solution.py:448
  52.6 16.5 %collective-permute-start.17 = (f32[64,1024]{1,0:T(8,128)S(1)}, f32[64,1024]{1,0:T(8,128)S(1)}, u32[]{:S(2)}, u32[]{:S(2)}) collective-permute-start(f32[64,1024]{1,0:T(8,128)S(1)} %get-tuple-element.28), channel_id=1, source_target_pairs={{0,16},{1,17},{2,18},{3,19},{4,20},{5,21},{6,22},{7,23},{8,24},{9,... | collective-permute-start | bytes 786440 | tf_op jit(solution)/shard_map/ppermute | solution.py:448
  54.2 14.9 %collective-permute-start.18 = (f32[64,1024]{1,0:T(8,128)S(1)}, f32[64,1024]{1,0:T(8,128)S(1)}, u32[]{:S(2)}, u32[]{:S(2)}) collective-permute-start(f32[64,1024]{1,0:T(8,128)S(1)} %get-tuple-element.29), channel_id=1, source_target_pairs={{0,18},{1,19},{2,16},{3,17},{4,22},{5,23},{6,20},{7,21},{8,26},{9,... | collective-permute-start | bytes 786440 | tf_op jit(solution)/shard_map/ppermute | solution.py:448
  69.1 3.1 %collective-permute-start.19 = (f32[64,1024]{1,0:T(8,128)S(1)}, f32[64,1024]{1,0:T(8,128)S(1)}, u32[]{:S(2)}, u32[]{:S(2)}) collective-permute-start(f32[64,1024]{1,0:T(8,128)S(1)} %get-tuple-element.31.refs_0_), channel_id=1, source_target_pairs={{0,1},{1,0},{2,3},{3,2},{4,5},{5,4},{6,7},{7,6},{8,9},{9,8},{10,11... | collective-permute-start | bytes 786440 | tf_op jit(solution)/shard_map/ppermute | solution.py:448
  69.2 3.0 %collective-permute-start.20 = (f32[64,1024]{1,0:T(8,128)S(1)}, f32[64,1024]{1,0:T(8,128)S(1)}, u32[]{:S(2)}, u32[]{:S(2)}) collective-permute-start(f32[64,1024]{1,0:T(8,128)S(1)} %collective-permute-done.16.refs_2_), channel_id=1, source_target_pairs={{0,1},{1,0},{2,3},{3,2},{4,5},{5,4},{6,7},{7,6},{8,9},{9,8},{10,11... | collective-permute-start | bytes 786440 | tf_op jit(solution)/shard_map/ppermute | solution.py:448
  69.7 2.5 %collective-permute-start.21 = (f32[64,1024]{1,0:T(8,128)S(1)}, f32[64,1024]{1,0:T(8,128)S(1)}, u32[]{:S(2)}, u32[]{:S(2)}) collective-permute-start(f32[64,1024]{1,0:T(8,128)S(1)} %collective-permute-done.17.refs_4_), channel_id=1, source_target_pairs={{0,1},{1,0},{2,3},{3,2},{4,5},{5,4},{6,7},{7,6},{8,9},{9,8},{10,11... | collective-permute-start | bytes 786440 | tf_op jit(solution)/shard_map/ppermute | solution.py:448
  69.7 2.5 %collective-permute-start.22 = (f32[64,1024]{1,0:T(8,128)S(1)}, f32[64,1024]{1,0:T(8,128)S(1)}, u32[]{:S(2)}, u32[]{:S(2)}) collective-permute-start(f32[64,1024]{1,0:T(8,128)S(1)} %collective-permute-done.18.refs_6_), channel_id=1, source_target_pairs={{0,1},{1,0},{2,3},{3,2},{4,5},{5,4},{6,7},{7,6},{8,9},{9,8},{10,11... | collective-permute-start | bytes 786440 | tf_op jit(solution)/shard_map/ppermute | solution.py:448
